TPU v7x, 128 devices: a whole 4x4x4 slice. The times are simulated.
128 devices in a mesh: fsdp: 4 (over x), table: 32 (over y, z, core).
Axes of the slice: x: 4, y: 4, z: 4, core: 2. Of those that a mesh axis runs over, the one named last changes fastest.
Arguments:
- embedded: bfloat16 [262144, 512], P(('fsdp', 'table')), may hold values from -6 to 6
- grad_out: bfloat16 [262144, 512], P(('fsdp', 'table')), may hold values from -6 to 6
- w_in: bfloat16 [512, 2048], P('fsdp'), may hold values from -0.25 to 0.25
- w_out: bfloat16 [512, 512], P('fsdp'), may hold values from -0.25 to 0.25
- lengths: int32 [512], P(('fsdp', 'table')), may hold values from 1 to 512, as said below
- slot_of: int32 [262144], P(('fsdp', 'table')), may hold values from 0 to 1613, as said below
- local_rows: int32 [206592], P(('fsdp', 'table')), may hold values from 0 to 4095, as said below
- send_counts: int32 [128, 32], P(('fsdp', 'table')), may hold values from 30 to 64, as said below
- send_offsets: int32 [128, 32], P(('fsdp', 'table')), may hold values from 0 to 1564, as said below
Outputs:
- grad_w_in: float32 [512, 2048], P('fsdp')
- grad_w_out: float32 [512, 512], P('fsdp')
- grad_table: float32 [131072, 512], P('table', 'fsdp')
Inputs may be any that keep to these rules, and one draw needn't show every extreme that they name: `lengths`: at least one sequence has 512 real actions in every draw. `send_counts`: row d counts, for each owner o, the slots of device d whose items lie in rows o * 4096 to (o + 1) * 4096 - 1; in every draw one owner other than the last gets exactly 64 from every device, and some device sends exactly 50 to every other owner; a row sums to at most 1614. `send_offsets`: row d is the exclusive prefix sum of row d of send_counts, so each owner's slots are consecutive and in owner order. Action t of device d reads slot slot_of[t] of device d's list; the slots used are exactly those below the sum of row d of send_counts. `local_rows`: two used slots of one device and one owner hold different rows; slots past the used ones are ignored.
All inputs are finite; a program needn't handle non-finite values.
Results may differ from a plain program's by a relative error of at most 0.011.
Values may be sent and summed in bfloat16 or wider, within the bound.
No kernel may reach another device: no remote copies, remote signals or barrier semaphores. Data moves between devices by JAX's collectives and lax.ppermute only.
A program may use at most 256 MiB of HBM per device.

v0:
```python
import math

import jax
import jax.numpy as jnp
from jax import lax
from jax.sharding import PartitionSpec as P

HEAD_DIM = 128
ROWS_DEV = 4096
CAP = 64


def layer_norm(field):
    center = field - jnp.mean(field, axis=-1, keepdims=True)
    spread = jnp.mean(center * center, axis=-1, keepdims=True)
    return center * lax.rsqrt(spread + 1e-05)


def attend(hidden, seq_lens):
    seq_count = seq_lens.shape[0]
    model_width = hidden.shape[1] // 4
    seq_len = hidden.shape[0] // seq_count
    head_count = model_width // HEAD_DIM
    gating, values, queries, keys_in = jnp.split(hidden, 4, axis=1)

    def heads_of(block):
        return block.reshape(seq_count, seq_len, head_count, HEAD_DIM)

    positions = jnp.arange(seq_len, dtype=jnp.int32)
    causal = positions[None, :] <= positions[:, None]
    score_factor = 1.0 / math.sqrt(HEAD_DIM)

    def one_seq(items):
        query_seq, key_seq, value_seq, seq_length = items
        scores = (
            jnp.einsum("qhd,khd->hqk", query_seq, key_seq, preferred_element_type=jnp.float32)
            * score_factor
        )
        keep_mask = causal & (positions[:, None] < seq_length)
        weights_b = jnp.where(keep_mask[None], jax.nn.silu(scores) / seq_len, 0.0).astype(
            jnp.bfloat16
        )
        return jnp.einsum("hqk,khd->qhd", weights_b, value_seq, preferred_element_type=jnp.float32)

    mixed = lax.map(one_seq, (heads_of(queries), heads_of(keys_in), heads_of(values), seq_lens))
    mixed = mixed.reshape(-1, model_width)
    return (layer_norm(mixed) * gating.astype(jnp.float32)).astype(jnp.bfloat16)


def layer_grads(embedded, grad_out, seq_lens, w_in, w_out):
    normed = layer_norm(embedded.astype(jnp.float32))
    normed_b = normed.astype(jnp.bfloat16)
    projected = jnp.dot(normed_b, w_in, preferred_element_type=jnp.float32)
    hidden = jax.nn.silu(projected).astype(jnp.bfloat16)
    mixed_b, attend_back = jax.vjp(lambda block: attend(block, seq_lens), hidden)
    grad_mixed = jnp.dot(grad_out, w_out.T, preferred_element_type=jnp.float32).astype(jnp.bfloat16)
    grad_wout = jnp.dot(mixed_b.T, grad_out, preferred_element_type=jnp.float32)
    (grad_hidden,) = attend_back(grad_mixed)
    sigma = jax.nn.sigmoid(projected)
    grad_proj = (
        grad_hidden.astype(jnp.float32) * sigma * (1.0 + projected * (1.0 - sigma))
    ).astype(jnp.bfloat16)
    grad_win = jnp.dot(normed_b.T, grad_proj, preferred_element_type=jnp.float32)
    grad_normed = jnp.dot(grad_proj, w_in.T, preferred_element_type=jnp.float32)
    _, norm_back = jax.vjp(layer_norm, embedded.astype(jnp.float32))
    (grad_embed,) = norm_back(grad_normed)
    token_grad = (grad_embed + grad_out.astype(jnp.float32)).astype(jnp.bfloat16)
    return (token_grad, grad_win, grad_wout)


def per_device(
    embedded, grad_out, w_in, w_out, lengths, slot_of, local_rows, send_counts, send_offsets
):
    fsdp_count = lax.axis_size("fsdp")
    table_count = lax.axis_size("table")
    w_in_full, w_out_full = (
        lax.all_gather(w_in, "fsdp", axis=0, tiled=True),
        lax.all_gather(w_out, "fsdp", axis=0, tiled=True),
    )
    token_grad, grad_win, grad_wout = layer_grads(
        embedded, grad_out, lengths, w_in_full, w_out_full
    )
    factor = 1.0 / math.sqrt(embedded.shape[0] * fsdp_count * table_count)
    total_in, total_out = lax.psum((grad_win, grad_wout), ("fsdp", "table"))
    share_rows = total_in.shape[0] // fsdp_count
    first_row = lax.axis_index("fsdp") * share_rows
    share_in = lax.dynamic_slice_in_dim(total_in, first_row, share_rows, 0)
    share_out = lax.dynamic_slice_in_dim(total_out, first_row, share_rows, 0)
    slot_total = local_rows.shape[0]
    onehot = (slot_of[None, :] == jnp.arange(slot_total, dtype=jnp.int32)[:, None]).astype(
        jnp.bfloat16
    )
    uniq_grad = jnp.dot(onehot, token_grad, preferred_element_type=jnp.float32)
    counts = send_counts[0]
    offsets = send_offsets[0]
    position = jnp.arange(CAP, dtype=jnp.int32)
    in_use = position[None, :] < counts[:, None]
    slot_index = jnp.minimum(offsets[:, None] + position[None, :], slot_total - 1)
    bucket = jnp.where(in_use[:, :, None], uniq_grad[slot_index], 0.0)
    target = jnp.where(in_use, local_rows[slot_index], ROWS_DEV).astype(jnp.float32)
    model_width = bucket.shape[2]
    col_width = model_width // fsdp_count
    values = bucket.reshape(table_count, CAP, fsdp_count, col_width).transpose(2, 0, 1, 3)
    values = values.reshape(fsdp_count * table_count, CAP, col_width)
    labels = jnp.broadcast_to(target[None, :, :, None], (fsdp_count, table_count, CAP, 1))
    labels = labels.reshape(fsdp_count * table_count, CAP, 1)
    got_values, got_labels = (
        lax.all_to_all(values, ("fsdp", "table"), split_axis=0, concat_axis=1, tiled=True),
        lax.all_to_all(labels, ("fsdp", "table"), split_axis=0, concat_axis=1, tiled=True),
    )
    flat_values = got_values.reshape(-1, col_width)
    flat_labels = got_labels.reshape(-1).astype(jnp.int32)
    grad_table = jax.ops.segment_sum(flat_values, flat_labels, num_segments=ROWS_DEV + 1)[:ROWS_DEV]
    return (share_in * factor, share_out * factor, grad_table)


def solution(mesh):
    placed = (
        P(("fsdp", "table"), None),
        P(("fsdp", "table"), None),
        P("fsdp", None),
        P("fsdp", None),
        P(("fsdp", "table")),
        P(("fsdp", "table")),
        P(("fsdp", "table")),
        P(("fsdp", "table"), None),
        P(("fsdp", "table"), None),
    )
    return jax.shard_map(
        per_device,
        mesh=mesh,
        in_specs=placed,
        out_specs=(P("fsdp", None), P("fsdp", None), P("table", "fsdp")),
        check_vma=False,
    )
```

profile of v0, /device:TPU:1, one launch (start us, length us, event | category | flops | bytes accessed | tf_op | source)
XLA Modules:
  0.0 585.4 jit_solution(11186841068851206278)
XLA Ops:
  8.7 11.8 %gather_fusion = s32[2048]{0:T(1024)S(1)} fusion(s32[1614]{0:T(1024)S(1)} %copy-done, s32[2048]{0:T(1024)S(1)} %broadcast_clamp_fusion), kind=kCustom, calls=%fused_computation | custom fusion | bytes 24576 | tf_op jit(solution)/shard_map/gather | solution.py:100
  21.3 12.0 %all-to-all-start = ((f32[128,64,1]{1,2,0:T(1,128)}), f32[128,64,1]{1,2,0:T(1,128)}, u32[]{:S(2)}, u32[]{:S(2)}) async-start(f32[128,64,1]{1,2,0:T(1,128)} %bitcast.19), calls=%async_computation | async-start | bytes 131072 | tf_op jit(solution)/shard_map/all_to_all | solution.py:109
  40.9 11.3 %all_gather.7 = bf16[512,512]{1,0:T(8,128)(2,1)S(1)} all-gather(bf16[128,512]{1,0:T(8,128)(2,1)S(1)} %copy-done.16), channel_id=1, replica_groups=mesh['fsdp'=4,'table'=32] {'fsdp'}, dimensions={0}, use_global_device_ids=true | all-gather | bytes 655360 | tf_op jit(solution)/shard_map/all_gather | solution.py:78
  54.5 12.3 %multiply_convert_fusion.1 = (bf16[2048,2048]{0,1:T(8,128)(2,1)S(1)}, f32[2048,2048]{0,1:T(8,128)}) fusion(bf16[512,2048]{1,0:T(8,128)(2,1)} %all-gather.2.cloned.1.call-done, bf16[2048,512]{0,1:T(8,128)(2,1)S(1)} %copy.47, f32[2048]{0:T(1024)S(1)} %fusion.72, f32[2048]{0:T(1024)S(1)} %broadcast_multiply_fusion.1), kind=kOutput, calls=%fused_computation.59 | convolution fusion | flops 4320133120 | bytes 29376512 | tf_op jit(solution)/shard_map/dot_general | solution.py:53
  92.5 65.2 %while.41 = (s32[]{:T(128)}, f32[4,512,4,128]{1,3,2,0:T(8,128)}, f32[4,4,512,512]{3,2,1,0:T(8,128)}, f32[4,4,512,512]{3,2,1,0:T(8,128)}, f32[4,4,512,512]{3,2,1,...) while((s32[]{:T(128)}, f32[4,512,4,128]{1,3,2,0:T(8,128)}, ...), condition=%wide.region_3.4_spmd.clone, body=%wide.region_2.3_spmd.clone.sunk | while | flops 560464384 | bytes 31986308 | solution.py:45
  92.5 7.4 %bitcast_dynamic-update-slice_fusion.5 = (f32[4,4,512,512]{3,2,1,0:T(8,128)}, f32[4,4,512,512]{3,2,1,0:T(8,128)}, f32[4,4,512,512]{3,2,1,0:T(8,128)}, f32[4,512,512]{2,1,0:T(8,128)S(1)}) fusion(f32[4,4,512,512]{3,2,1,0:T(8,128)} %get-tuple-element.721, s32[]{:T(128)} %get-tuple-element.717, f32[4,4,512,512]{3,2,1,0:T(8,128)} %get-tuple-element.720, ...), kind=kOutput, calls=%fused_computation.38.clone.1 | convolution fusion | flops 274726912 | bytes 17827328 | tf_op jit(solution)/shard_map/jvp()/while/body/eval_jaxpr/qhd,khd->hqk/dot_general | solution.py:36
  108.9 7.2 %bitcast_dynamic-update-slice_fusion.5 = (f32[4,4,512,512]{3,2,1,0:T(8,128)}, f32[4,4,512,512]{3,2,1,0:T(8,128)}, f32[4,4,512,512]{3,2,1,0:T(8,128)}, f32[4,512,512]{2,1,0:T(8,128)S(1)}) fusion(f32[4,4,512,512]{3,2,1,0:T(8,128)} %get-tuple-element.721, s32[]{:T(128)} %get-tuple-element.717, f32[4,4,512,512]{3,2,1,0:T(8,128)} %get-tuple-element.720, ...), kind=kOutput, calls=%fused_computation.38.clone.1 | convolution fusion | flops 274726912 | bytes 17827328 | tf_op jit(solution)/shard_map/jvp()/while/body/eval_jaxpr/qhd,khd->hqk/dot_general | solution.py:36
  125.2 7.2 %bitcast_dynamic-update-slice_fusion.5 = (f32[4,4,512,512]{3,2,1,0:T(8,128)}, f32[4,4,512,512]{3,2,1,0:T(8,128)}, f32[4,4,512,512]{3,2,1,0:T(8,128)}, f32[4,512,512]{2,1,0:T(8,128)S(1)}) fusion(f32[4,4,512,512]{3,2,1,0:T(8,128)} %get-tuple-element.721, s32[]{:T(128)} %get-tuple-element.717, f32[4,4,512,512]{3,2,1,0:T(8,128)} %get-tuple-element.720, ...), kind=kOutput, calls=%fused_computation.38.clone.1 | convolution fusion | flops 274726912 | bytes 17827328 | tf_op jit(solution)/shard_map/jvp()/while/body/eval_jaxpr/qhd,khd->hqk/dot_general | solution.py:36
  141.4 7.2 %bitcast_dynamic-update-slice_fusion.5 = (f32[4,4,512,512]{3,2,1,0:T(8,128)}, f32[4,4,512,512]{3,2,1,0:T(8,128)}, f32[4,4,512,512]{3,2,1,0:T(8,128)}, f32[4,512,512]{2,1,0:T(8,128)S(1)}) fusion(f32[4,4,512,512]{3,2,1,0:T(8,128)} %get-tuple-element.721, s32[]{:T(128)} %get-tuple-element.717, f32[4,4,512,512]{3,2,1,0:T(8,128)} %get-tuple-element.720, ...), kind=kOutput, calls=%fused_computation.38.clone.1 | convolution fusion | flops 274726912 | bytes 17827328 | tf_op jit(solution)/shard_map/jvp()/while/body/eval_jaxpr/qhd,khd->hqk/dot_general | solution.py:36
  157.7 6.9 %copy.51 = f32[4,512,4,128]{1,0,3,2:T(4,128)} copy(f32[4,512,4,128]{1,3,2,0:T(8,128)} %get-tuple-element.376) | data formatting | bytes 8388608 | tf_op jit(solution)/shard_map/jvp()/while | solution.py:45
  190.8 73.0 %while.40 = (s32[]{:T(128)}, bf16[4,512,4,128]{3,1,2,0:T(8,128)(2,1)}, bf16[4,512,4,128]{3,1,2,0:T(8,128)(2,1)}, bf16[4,512,4,128]{1,3,2,0:T(8,128)(2,1)}, pred[...) while((s32[]{:T(128)}, ...), condition=%wide.region_9.10_spmd, body=%wide.region_8.9_spmd.sunk | while | flops 1083179008 | bytes 28315804 | solution.py:45
  194.2 6.5 %fusion.108 = bf16[4,512,512]{2,1,0:T(8,128)(2,1)S(1)} fusion(f32[4,4,512,512]{3,2,1,0:T(8,128)} %get-tuple-element.780, s32[]{:T(128)S(6)} %sub.117, f32[4,4,512,512]{3,2,1,0:T(8,128)} %get-tuple-element.779, f32[4,4,512,512]{3,2,1,0:T(8,128)} %get-tuple-element.778, pred[4,4,512,512]{3,2,1,0:T(32,128)(4,1)} %get-tuple-element.775, ...), kind=kOutput, calls=%fused_computation.7.clone.1 | convolution fusion | flops 277872640 | bytes 16778240 | tf_op jit(solution)/shard_map/transpose(jvp())/while/body/eval_jaxpr/hqk,khd->qhd/dot_general | solution.py:43
  212.4 6.6 %fusion.108 = bf16[4,512,512]{2,1,0:T(8,128)(2,1)S(1)} fusion(f32[4,4,512,512]{3,2,1,0:T(8,128)} %get-tuple-element.780, s32[]{:T(128)S(6)} %sub.117, f32[4,4,512,512]{3,2,1,0:T(8,128)} %get-tuple-element.779, f32[4,4,512,512]{3,2,1,0:T(8,128)} %get-tuple-element.778, pred[4,4,512,512]{3,2,1,0:T(32,128)(4,1)} %get-tuple-element.775, ...), kind=kOutput, calls=%fused_computation.7.clone.1 | convolution fusion | flops 277872640 | bytes 16778240 | tf_op jit(solution)/shard_map/transpose(jvp())/while/body/eval_jaxpr/hqk,khd->qhd/dot_general | solution.py:43
  230.6 6.6 %fusion.108 = bf16[4,512,512]{2,1,0:T(8,128)(2,1)S(1)} fusion(f32[4,4,512,512]{3,2,1,0:T(8,128)} %get-tuple-element.780, s32[]{:T(128)S(6)} %sub.117, f32[4,4,512,512]{3,2,1,0:T(8,128)} %get-tuple-element.779, f32[4,4,512,512]{3,2,1,0:T(8,128)} %get-tuple-element.778, pred[4,4,512,512]{3,2,1,0:T(32,128)(4,1)} %get-tuple-element.775, ...), kind=kOutput, calls=%fused_computation.7.clone.1 | convolution fusion | flops 277872640 | bytes 16778240 | tf_op jit(solution)/shard_map/transpose(jvp())/while/body/eval_jaxpr/hqk,khd->qhd/dot_general | solution.py:43
  248.9 6.7 %fusion.108 = bf16[4,512,512]{2,1,0:T(8,128)(2,1)S(1)} fusion(f32[4,4,512,512]{3,2,1,0:T(8,128)} %get-tuple-element.780, s32[]{:T(128)S(6)} %sub.117, f32[4,4,512,512]{3,2,1,0:T(8,128)} %get-tuple-element.779, f32[4,4,512,512]{3,2,1,0:T(8,128)} %get-tuple-element.778, pred[4,4,512,512]{3,2,1,0:T(32,128)(4,1)} %get-tuple-element.775, ...), kind=kOutput, calls=%fused_computation.7.clone.1 | convolution fusion | flops 277872640 | bytes 16778240 | tf_op jit(solution)/shard_map/transpose(jvp())/while/body/eval_jaxpr/hqk,khd->qhd/dot_general | solution.py:43
  275.6 4.6 copy.59
  283.1 9.7 %multiply_convert_fusion = bf16[2048,2048]{0,1:T(8,128)(2,1)S(1)} fusion(f32[2048,2048]{0,1:T(8,128)} %get-tuple-element.546, bf16[2048,512]{0,1:T(8,128)(2,1)S(1)} %bitcast.195, bf16[2048,512]{0,1:T(8,128)(2,1)S(1)} %bitcast.194, bf16[2048,512]{0,1:T(8,128)(2,1)S(1)} %bitcast.193, bf16[2048,512]{0,1:T(8,128)(2,1)S(1)} %copy-done.7), kind=kLoop, calls=%fused_computation.58 | loop fusion | flops 71303168 | bytes 33554432 | tf_op jit(solution)/shard_map/convert_element_type | solution.py:62
  292.9 4.6 fusion.55
  303.2 8.9 %gather_fusion.1 = f32[2048,512]{1,0:T(8,128)} fusion(f32[1614,512]{1,0:T(8,128)S(1)} %fusion.47, s32[2048]{0:T(1024)S(1)} %copy-done.15), kind=kCustom, calls=%fused_computation.1 | custom fusion | bytes 8396800 | tf_op jit(solution)/shard_map/gather | solution.py:99
  312.1 5.3 gather.10
  321.5 12.1 %all-to-all-start.1 = ((f32[128,64,128]{2,1,0:T(8,128)}), f32[128,64,128]{2,1,0:T(8,128)}, u32[]{:S(2)}, u32[]{:S(2)}) async-start(f32[128,64,128]{2,1,0:T(8,128)} %bitcast.190), calls=%async_computation.1 | async-start | bytes 8388608 | tf_op jit(solution)/shard_map/all_to_all | solution.py:108
  333.7 9.7 %fusion.65 = f32[512,2048]{1,0:T(8,128)} fusion(bf16[2048,2048]{0,1:T(8,128)(2,1)} %copy-done.11, bf16[2048,512]{0,1:T(8,128)(2,1)S(1)} %copy-done.4, f32[2048]{0:T(1024)S(1)} %copy-done.22, f32[2048]{0:T(1024)S(1)} %copy-done.18), kind=kOutput, calls=%fused_computation.92 | convolution fusion | flops 4299161600 | bytes 14696448 | tf_op jit(solution)/shard_map/dot_general | solution.py:63
  344.5 181.5 %all-reduce.3.cloned.1.call-done = (f32[512,2048]{1,0:T(8,128)}, f32[512,512]{1,0:T(8,128)}) async-done(((f32[512,2048]{1,0:T(8,128)}, f32[512,512]{1,0:T(8,128)}), (f32[512,2048]{1,0:T(8,128)}, f32[512,512]{1,0:T(8,128)})) %all-reduce.3.cloned.1.call-update) | async-done | bytes 5242896 | tf_op jit(solution)/shard_map/psum | solution.py:84
  530.0 46.9 %scatter_custom_fusion = f32[4097,128]{1,0:T(8,128)S(1)} fusion(s32[8192]{0:T(1024)S(1)} %reshape.282, f32[8192,128]{1,0:T(8,128)} %bitcast.22, f32[]{:T(128)} %constant.149.clone.1), kind=kCustom, calls=%fused_computation.94 | custom fusion | flops 1048576 | bytes 2098176 | tf_op jit(solution)/shard_map/scatter-add | solution.py:113
  (171 shorter events, 177.5 us)
Async XLA Ops:
  7.2 47.3 %all-gather.2.cloned.1.call-start = ((), (), s32[]{:S(2)}) async-start(), calls=%async_computation.2 | async-start | bytes 2621440 | tf_op jit(solution)/shard_map/all_gather | solution.py:77
  8.7 11.8 %copy-start.14 = (s32[2048]{0:T(1024)}, s32[2048]{0:T(1024)S(1)}, u32[]{:S(2)}) copy-start(s32[2048]{0:T(1024)S(1)} %broadcast_clamp_fusion) | copy-start | bytes 24580
  8.7 11.9 %copy-start.24 = (s32[1,32]{1,0:T(1,128)S(1)}, s32[1,32]{1,0:T(1,128)}, u32[]{:S(2)}) copy-start(s32[1,32]{1,0:T(1,128)} %param.20) | copy-start | bytes 388
  21.3 300.2 %all-to-all-start = ((f32[128,64,1]{1,2,0:T(1,128)}), f32[128,64,1]{1,2,0:T(1,128)}, u32[]{:S(2)}, u32[]{:S(2)}) async-start(f32[128,64,1]{1,2,0:T(1,128)} %bitcast.19), calls=%async_computation | async-start | bytes 131072 | tf_op jit(solution)/shard_map/all_to_all | solution.py:109
  33.4 7.5 %copy-start.16 = (bf16[128,512]{1,0:T(8,128)(2,1)S(1)}, bf16[128,512]{1,0:T(8,128)(2,1)}, u32[]{:S(2)}) copy-start(bf16[128,512]{1,0:T(8,128)(2,1)} %param.16) | copy-start | bytes 393220
  36.3 18.1 %copy-start.2 = (bf16[2048,512]{0,1:T(8,128)(2,1)}, bf16[2048,512]{0,1:T(8,128)(2,1)S(1)}, u32[]{:S(2)}) copy-start(bf16[2048,512]{0,1:T(8,128)(2,1)S(1)} %copy.47) | copy-start | bytes 6291460
  53.2 13.5 %copy-start.17 = (f32[2048]{0:T(1024)}, f32[2048]{0:T(1024)S(1)}, u32[]{:S(2)}) copy-start(f32[2048]{0:T(1024)S(1)} %broadcast_multiply_fusion.1) | copy-start | bytes 24580
  54.4 12.3 %copy-start.21 = (f32[2048]{0:T(1024)}, f32[2048]{0:T(1024)S(1)}, u32[]{:S(2)}) copy-start(f32[2048]{0:T(1024)S(1)} %fusion.72) | copy-start | bytes 24580
  66.7 5.1 copy-start.6
  86.2 6.3 %copy-start.27 = (s32[4]{0:T(128)S(1)}, s32[4]{0:T(128)}, u32[]{:S(2)}) copy-start(s32[4]{0:T(128)} %param.17) | copy-start | bytes 52
  170.6 5.3 slice-start
  263.8 5.4 copy-start.10
  275.6 7.0 %copy-start.7 = (bf16[2048,512]{0,1:T(8,128)(2,1)S(1)}, bf16[2048,512]{0,1:T(8,128)(2,1)}, u32[]{:S(2)}) copy-start(bf16[2048,512]{0,1:T(8,128)(2,1)} %get-tuple-element.539) | copy-start | bytes 6291460
  283.1 9.7 %copy-start.3 = (bf16[2048,512]{0,1:T(8,128)(2,1)S(1)}, bf16[2048,512]{0,1:T(8,128)(2,1)}, u32[]{:S(2)}) copy-start(bf16[2048,512]{0,1:T(8,128)(2,1)} %copy-done.2) | copy-start | bytes 6291460
  283.1 9.7 %copy-start.18 = (f32[2048]{0:T(1024)S(1)}, f32[2048]{0:T(1024)}, u32[]{:S(2)}) copy-start(f32[2048]{0:T(1024)} %copy-done.17) | copy-start | bytes 24580
  283.1 9.7 %copy-start.25 = (bf16[512,2048]{1,0:T(8,128)(2,1)S(1)}, bf16[512,2048]{1,0:T(8,128)(2,1)}, u32[]{:S(2)}) copy-start(bf16[512,2048]{1,0:T(8,128)(2,1)} %all-gather.2.cloned.1.call-done) | copy-start | bytes 6291460
  292.8 4.7 copy-start.11
  292.9 4.7 copy-start.20
  292.9 4.7 copy-start.22
  312.1 5.3 copy-start.23
  321.5 12.2 %copy-start.4 = (bf16[2048,512]{0,1:T(8,128)(2,1)S(1)}, bf16[2048,512]{0,1:T(8,128)(2,1)}, u32[]{:S(2)}) copy-start(bf16[2048,512]{0,1:T(8,128)(2,1)} %copy-done.2) | copy-start | bytes 6291460
  321.5 208.5 %all-to-all-start.1 = ((f32[128,64,128]{2,1,0:T(8,128)}), f32[128,64,128]{2,1,0:T(8,128)}, u32[]{:S(2)}, u32[]{:S(2)}) async-start(f32[128,64,128]{2,1,0:T(8,128)} %bitcast.190), calls=%async_computation.1 | async-start | bytes 8388608 | tf_op jit(solution)/shard_map/all_to_all | solution.py:108
  333.6 192.4 %all-reduce.3.cloned.1.call-start = ((), (), s32[]{:S(2)}) async-start(), calls=%async_computation.3 | async-start | bytes 10485760 | tf_op jit(solution)/shard_map/psum | solution.py:84
  527.7 50.6 %copy-start.1 = (s32[1614]{0:T(1024)S(1)}, s32[1614]{0:T(1024)}, u32[]{:S(2)}) copy-start(s32[1614]{0:T(1024)} %param.19) | copy-start | bytes 19372
  (10 other events, 23.4 us)
Sparse Core Ops, SparseCore 0:
  9.7 34.7 all-gather.1
  343.5 182.4 all-reduce.2
where the time goes:
time: 590 us; the launch traced here: 585 us
  waiting for transfers between devices  182 us (31%)
  matrix products  139 us (24%)
  local copies, waits for them, and re-layouts  121 us (21%)
  other arithmetic  93.2 us (16%)
  starting transfers between devices  24.2 us (4%)
  between operations  14.8 us (3%)
  blocking collectives  11.3 us (2%)
    psum x1, waiting for transfers between devices, per_device(): total_in, total_out = lax.psum((grad_win, grad_wout), ('fsdp', 'table'))  181 us
    dot_general x12, matrix products, one_seq(): jnp.einsum('hqk,khd->qhd', weights_b, value_seq, preferred_element_type=j...  52.4 us
    dot_general x12, matrix products, one_seq(): jnp.einsum('qhd,khd->hqk', query_seq, key_seq, preferred_element_type=jnp...  50.2 us
    scatter-add x1, other arithmetic, per_device(): jax.ops.segment_sum(flat_values, flat_labels, num_segments=ROWS_DEV + 1)  46.9 us
    unnamed x71, local copies, waits for them, and re-layouts  29.6 us
    while x5, local copies, waits for them, and re-layouts, attend(): lax.map(one_seq, (heads_of(queries), heads_of(keys_in), heads_of(values),...  20.7 us
    dynamic_slice x12, local copies, waits for them, and re-layouts, attend(): lax.map(one_seq, (heads_of(queries), heads_of(keys_in), heads_of(values),...  16 us
    gather x2, local copies, waits for them, and re-layouts, per_device(): bucket = jnp.where(in_use[:, :, None], uniq_grad[slot_index], 0.0)  14.2 us
  transfers between devices with their start and end apart: 4, of which 1 were waited for; matrix products, arithmetic and copies ran while one was open for 51% of the time, Pallas kernels for 0%

commit v1 on v0

v1 whole, which is shorter than its diff:
```python
import functools
import math

import jax
import jax.numpy as jnp
from jax import lax
from jax.experimental import pallas as pl
from jax.experimental.pallas import tpu as pltpu
from jax.sharding import PartitionSpec as P

HEAD_DIM = 128
ROWS_DEV = 4096
CAP = 64
PACKET = 72
SEQ = 512
WIDTH = 512
HEADS = WIDTH // HEAD_DIM
HALF = SEQ // 2
EPS = 1e-05
BF = jnp.bfloat16
F32 = jnp.float32
BOTH = ("fsdp", "table")


def dot_nn(a, b):
    return lax.dot_general(a, b, (((1,), (0,)), ((), ())), preferred_element_type=F32)


def dot_nt(a, b):
    return lax.dot_general(a, b, (((1,), (1,)), ((), ())), preferred_element_type=F32)


def dot_tn(a, b):
    return lax.dot_general(a, b, (((0,), (0,)), ((), ())), preferred_element_type=F32)


def normalise(x):
    center = x - jnp.mean(x, axis=-1, keepdims=True)
    rstd = lax.rsqrt(jnp.mean(center * center, axis=-1, keepdims=True) + EPS)
    return center * rstd, rstd


def norm_back(xhat, rstd, cot):
    return rstd * (
        cot
        - jnp.mean(cot, axis=-1, keepdims=True)
        - xhat * jnp.mean(cot * xhat, axis=-1, keepdims=True)
    )


def norm_kernel(emb, after, normed, turned):
    chunk = 64

    @pl.loop(0, SEQ // chunk)
    def _(i):
        rows = pl.ds(pl.multiple_of(i * chunk, chunk), chunk)
        xhat, _ = normalise(emb[rows, :].astype(F32))
        normed[rows, :] = xhat.astype(BF)

    turned[...] = normed[...].T


def run_norm(embedded, after):
    tokens = embedded.shape[0]
    return pl.pallas_call(
        norm_kernel,
        grid=(tokens // SEQ,),
        in_specs=[
            pl.BlockSpec((SEQ, WIDTH), lambda i: (i, 0)),
            pl.BlockSpec(memory_space=pl.ANY),
        ],
        out_specs=[
            pl.BlockSpec((SEQ, WIDTH), lambda i: (i, 0)),
            pl.BlockSpec((WIDTH, SEQ), lambda i: (0, i)),
        ],
        out_shape=[
            jax.ShapeDtypeStruct((tokens, WIDTH), BF),
            jax.ShapeDtypeStruct((WIDTH, tokens), BF),
        ],
        compiler_params=pltpu.CompilerParams(vmem_limit_bytes=56 * 1024 * 1024),
        cost_estimate=pl.CostEstimate(
            flops=20_000_000, bytes_accessed=6_000_000, transcendentals=2048
        ),
        name="norm",
    )(embedded, after)


def layer_kernel(
    coords, lens, normed, go, turned, own_in, own_out,
    low, high, low_o, high_o, far_a, far_b, far_ao, far_bo,
    gp, mine, other, w_turned,
    w, proj, slope, hidden, probs, rates, mixed, cot, seq_sum, gp_all, gwout,
):
    step = pl.program_id(0)

    @pl.when(step == 0)
    def _():
        me, core = coords[0], coords[1]

        def put(shard, which, offset, piece):
            row = lax.rem(shard, 4) * 128 + which * 64 + offset
            w[pl.ds(pl.multiple_of(row, 32), piece.shape[0]), :] = piece[...]

        home = pl.ds(pl.multiple_of(me * 128, 128), 128)
        w[home, 0 : 4 * WIDTH] = own_in[...]
        w[home, 4 * WIDTH :] = own_out[...]
        put(me + 3, core, 0, low)
        put(me + 3, 1 - core, 0, low_o)
        put(me + 1, core, 0, high)
        put(me + 1, 1 - core, 0, high_o)
        put(me + 2, core, 0, far_a)
        put(me + 2, core, 32, far_b)
        put(me + 2, 1 - core, 0, far_ao)
        put(me + 2, 1 - core, 32, far_bo)
        gwout[...] = jnp.zeros_like(gwout)

        @pl.loop(0, 4)
        def _(i):
            cols = pl.ds(pl.multiple_of(i * WIDTH, WIDTH), WIDTH)
            w_turned[cols, :] = w[:, cols].T

    chunk = 64

    def rows_of(i, size=chunk):
        return pl.ds(pl.multiple_of(i * size, size), size)

    for block in range(4):
        cols = slice(block * WIDTH, (block + 1) * WIDTH)
        proj[...] = dot_nn(normed[...], w[:, cols])

        @pl.loop(0, SEQ // chunk)
        def _(i):
            half = 0.5 * proj[rows_of(i), :]
            t = jnp.tanh(half)
            ht = half * t
            hidden[rows_of(i), cols] = (half + ht).astype(BF)
            slope[rows_of(i), cols] = 0.5 * ((1.0 + half) + t * (1.0 - ht))

    factor = 0.5 / math.sqrt(HEAD_DIM)

    def head_cols(block, head):
        return slice(block * WIDTH + head * HEAD_DIM, block * WIDTH + (head + 1) * HEAD_DIM)

    causal = lax.broadcasted_iota(jnp.int32, (HALF, HALF), 1) <= lax.broadcasted_iota(
        jnp.int32, (HALF, HALF), 0
    )
    for head in range(HEADS):
        v_cols, q_cols, k_cols = (head_cols(b, head) for b in (1, 2, 3))
        for qi in range(2):
            q_rows = slice(qi * HALF, (qi + 1) * HALF)
            for ki in range(qi + 1):
                k_rows = slice(ki * HALF, (ki + 1) * HALF)
                z = factor * dot_nt(hidden[q_rows, q_cols], hidden[k_rows, k_cols])
                t = jnp.tanh(z)
                zt = z * t
                prob = z + zt
                rate = (1.0 + z) + t * (1.0 - zt)
                if qi == ki:
                    prob = jnp.where(causal, prob, 0.0)
                    rate = jnp.where(causal, rate, 0.0)
                probs[head, q_rows, k_rows] = prob.astype(BF)
                rates[head, q_rows, k_rows] = rate.astype(BF)
            seen = slice(0, (qi + 1) * HALF)
            mixed[q_rows, head_cols(0, head)] = dot_nn(
                probs[head, q_rows, seen], hidden[seen, v_cols]
            )

    proj[...] = dot_nt(go[...], w[:, 4 * WIDTH :])
    seq_len = lens[step]

    @pl.loop(0, SEQ // chunk)
    def _(i):
        rows = rows_of(i)
        place = lax.broadcasted_iota(jnp.int32, (chunk, 1), 0) + i * chunk
        keep = place < seq_len
        raw = jnp.where(keep, mixed[rows, :] * (1.0 / SEQ), 0.0)
        xhat, rstd = normalise(raw)
        gate = hidden[rows, 0:WIDTH].astype(F32)
        down = proj[rows, :].astype(BF).astype(F32)
        seq_sum[rows, :] = (xhat * gate).astype(BF)
        grad_gate = ((down * xhat).astype(BF).astype(F32) * slope[rows, 0:WIDTH]).astype(BF)
        gp[rows, 0:WIDTH] = grad_gate
        gp_all[pl.ds(pl.multiple_of(step * SEQ + i * chunk, chunk), chunk), 0:WIDTH] = grad_gate
        back = norm_back(xhat, rstd, down * gate)
        cot[rows, :] = jnp.where(keep, back * (1.0 / SEQ), 0.0).astype(BF)

    gwout[...] += dot_tn(seq_sum[...], go[...])

    def finish(value, rows, cols):
        grad = (value.astype(BF).astype(F32) * slope[rows, cols]).astype(BF)
        gp[rows, cols] = grad
        here = pl.ds(pl.multiple_of(step * SEQ + rows.start, HALF), rows.stop - rows.start)
        gp_all[here, cols] = grad

    top, low_half, whole = slice(0, HALF), slice(HALF, SEQ), slice(0, SEQ)
    for head in range(HEADS):
        v_cols, q_cols, k_cols = (head_cols(b, head) for b in (1, 2, 3))
        c_cols = head_cols(0, head)
        for q_rows, seen in ((top, top), (low_half, whole)):
            down = dot_nt(cot[q_rows, c_cols], hidden[seen, v_cols]).astype(BF)
            score = down * rates[head, q_rows, seen]
            rates[head, q_rows, seen] = score
            finish(factor * dot_nn(score, hidden[seen, k_cols]), q_rows, q_cols)
        for k_rows, seen in ((top, whole), (low_half, low_half)):
            finish(dot_tn(probs[head, seen, k_rows], cot[seen, c_cols]), k_rows, v_cols)
            finish(
                factor * dot_tn(rates[head, seen, k_rows], hidden[seen, q_cols]),
                k_rows,
                k_cols,
            )

    @pl.when(step == pl.num_programs(0) - 1)
    def _():
        tile, per_half = 256, 5
        core = coords[1]

        def place(half, col, value):
            cols = pl.ds(pl.multiple_of(col, tile), value.shape[1])

            @pl.when(half == core)
            def _():
                mine[:, cols] = value

            @pl.when(half != core)
            def _():
                other[:, cols] = value

        @pl.loop(0, 4 * WIDTH // tile)
        def _(j):
            cols = pl.ds(pl.multiple_of(j * tile, tile), tile)
            value = dot_nn(turned[...], gp_all[:, cols]).astype(BF)
            place(j // per_half, lax.rem(j, per_half) * tile, value)

        place(1, 4 * WIDTH - per_half * tile, gwout[...].astype(BF))


def run_layer(coords, lengths, normed, turned, grad_out, pieces):
    tokens = normed.shape[0]
    smem = pl.BlockSpec(memory_space=pltpu.SMEM)

    def whole(shape):
        return pl.BlockSpec(shape, lambda i: (0, 0))

    def by_seq(cols):
        return pl.BlockSpec((SEQ, cols), lambda i: (i, 0))

    return pl.pallas_call(
        layer_kernel,
        grid=(tokens // SEQ,),
        in_specs=[smem, smem, by_seq(WIDTH), by_seq(WIDTH)]
        + [whole(p.shape) for p in (turned, *pieces)],
        out_specs=[
            by_seq(4 * WIDTH),
            whole((WIDTH, 5 * WIDTH // 2)),
            whole((WIDTH, 5 * WIDTH // 2)),
            whole((4 * WIDTH, WIDTH)),
        ],
        out_shape=[
            jax.ShapeDtypeStruct((tokens, 4 * WIDTH), BF),
            jax.ShapeDtypeStruct((WIDTH, 5 * WIDTH // 2), BF),
            jax.ShapeDtypeStruct((WIDTH, 5 * WIDTH // 2), BF),
            jax.ShapeDtypeStruct((4 * WIDTH, WIDTH), BF),
        ],
        scratch_shapes=[
            pltpu.VMEM((WIDTH, 5 * WIDTH), BF),
            pltpu.VMEM((SEQ, WIDTH), F32),
            pltpu.VMEM((SEQ, 4 * WIDTH), F32),
            pltpu.VMEM((SEQ, 4 * WIDTH), BF),
            pltpu.VMEM((HEADS, SEQ, SEQ), BF),
            pltpu.VMEM((HEADS, SEQ, SEQ), BF),
            pltpu.VMEM((SEQ, WIDTH), F32),
            pltpu.VMEM((SEQ, WIDTH), BF),
            pltpu.VMEM((SEQ, WIDTH), BF),
            pltpu.VMEM((tokens, 4 * WIDTH), BF),
            pltpu.VMEM((WIDTH, WIDTH), F32),
        ],
        compiler_params=pltpu.CompilerParams(vmem_limit_bytes=56 * 1024 * 1024),
        cost_estimate=pl.CostEstimate(
            flops=20_000_000_000, bytes_accessed=20_000_000, transcendentals=8_000_000
        ),
        name="layer",
    )(coords, lengths, normed, grad_out, turned, *pieces)


def token_kernel(emb, go, gp, w, after, tokens, grads):
    chunk = 64
    grads[...] = dot_nn(gp[...], w[...])

    @pl.loop(0, SEQ // chunk)
    def _(i):
        rows = pl.ds(pl.multiple_of(i * chunk, chunk), chunk)
        xhat, rstd = normalise(emb[rows, :].astype(F32))
        back = norm_back(xhat, rstd, grads[rows, :])
        tokens[rows, :] = (back + go[rows, :].astype(F32)).astype(BF)


def run_tokens(embedded, grad_out, grad_proj, w, after):
    count = embedded.shape[0]

    def by_seq(cols):
        return pl.BlockSpec((SEQ, cols), lambda i: (i, 0))

    return pl.pallas_call(
        token_kernel,
        grid=(count // SEQ,),
        in_specs=[
            by_seq(WIDTH),
            by_seq(WIDTH),
            by_seq(4 * WIDTH),
            pl.BlockSpec((4 * WIDTH, WIDTH), lambda i: (0, 0)),
            pl.BlockSpec(memory_space=pl.ANY),
        ],
        out_specs=by_seq(WIDTH),
        out_shape=jax.ShapeDtypeStruct((count, WIDTH), BF),
        scratch_shapes=[pltpu.VMEM((SEQ, WIDTH), F32)],
        compiler_params=pltpu.CompilerParams(vmem_limit_bytes=56 * 1024 * 1024),
        cost_estimate=pl.CostEstimate(
            flops=4_300_000_000, bytes_accessed=16_000_000, transcendentals=2048
        ),
        name="token_grads",
    )(embedded, grad_out, grad_proj, w, after)


def bucket_kernel(bucket, labels, tokens, after, out):
    owners, total = out.shape[1], tokens.shape[0]
    tile = owners * CAP
    slot = lax.broadcasted_iota(jnp.int32, (tile, total), 0) + pl.program_id(0) * tile
    pick = jnp.where(slot == bucket[...], 1.0, 0.0).astype(BF)
    sums = dot_nn(pick, tokens[...]).astype(BF)
    marks = labels[...].astype(F32).astype(BF)
    for part in range(out.shape[0]):
        for owner in range(owners):
            cols = slice(part * 128, (part + 1) * 128)
            out[part, owner, 0:CAP, :] = sums[owner * CAP : (owner + 1) * CAP, cols]
            out[part, owner, CAP:PACKET, :] = jnp.broadcast_to(
                marks[owner : owner + 1, :], (PACKET - CAP, 128)
            )


def run_buckets(bucket, labels, tokens, parts, after):
    count, width = tokens.shape
    owners = labels.shape[0]
    per_step = 8
    return pl.pallas_call(
        bucket_kernel,
        grid=(owners // per_step,),
        in_specs=[
            pl.BlockSpec((1, count), lambda i: (0, 0)),
            pl.BlockSpec((per_step, 128), lambda i: (i, 0)),
            pl.BlockSpec((count, width), lambda i: (0, 0)),
            pl.BlockSpec(memory_space=pl.ANY),
        ],
        out_specs=pl.BlockSpec((parts, per_step, PACKET, 128), lambda i: (0, i, 0, 0)),
        out_shape=jax.ShapeDtypeStruct((parts, owners, PACKET, 128), BF),
        compiler_params=pltpu.CompilerParams(vmem_limit_bytes=56 * 1024 * 1024),
        cost_estimate=pl.CostEstimate(
            flops=4_300_000_000, bytes_accessed=6_000_000, transcendentals=0
        ),
        name="bucket_rows",
    )(bucket, labels, tokens, after)


def label_kernel(counts, offsets, rows, out):
    last = rows.shape[0] - 1

    @pl.loop(0, counts.shape[0])
    def _(owner):
        count, first = counts[owner], offsets[owner]
        for place in range(CAP):
            row = rows[jnp.minimum(first + place, last)]
            row = jnp.where(place < count, row, ROWS_DEV)
            out[owner, place] = lax.shift_right_logical(row, 6)
            out[owner, CAP + place] = jnp.bitwise_and(row, 63)


def run_labels(counts, offsets, rows):
    smem = pl.BlockSpec(memory_space=pltpu.SMEM)
    return pl.pallas_call(
        label_kernel,
        in_specs=[smem] * 3,
        out_specs=smem,
        out_shape=jax.ShapeDtypeStruct((counts.shape[0], 2 * CAP), jnp.int32),
        cost_estimate=pl.CostEstimate(flops=10_000, bytes_accessed=10_000, transcendentals=0),
        name="labels",
    )(counts, offsets, rows)


def scatter_kernel(rows, out, table, block, words, labels, sem):
    batch = 16
    marks = rows[:, CAP, :].astype(F32)
    marks = marks * 64.0 + pltpu.roll(marks, CAP, 1)
    words[...] = marks.astype(jnp.int32)
    copy = pltpu.make_async_copy(words, labels, sem)
    copy.start()

    @pl.loop(0, ROWS_DEV // 128)
    def _(i):
        table[pl.ds(pl.multiple_of(i * 128, 128), 128), :] = jnp.zeros((128, 128), F32)

    table[ROWS_DEV : ROWS_DEV + 8, :] = jnp.zeros((8, 128), F32)
    copy.wait()

    @pl.loop(0, rows.shape[0])
    def _(source):
        block[...] = rows[source, 0:CAP, :].astype(F32)

        def add_batch(start):
            places = range(start, start + batch)
            wheres = [labels[source, p] for p in places]
            sums = [
                table[pl.ds(w, 1), :] + block[p : p + 1, :] for p, w in zip(places, wheres)
            ]
            for w, s in zip(wheres, sums):
                table[pl.ds(w, 1), :] = s

        for start in range(0, CAP, batch):
            pl.when(labels[source, start] != ROWS_DEV)(functools.partial(add_batch, start))

    out[...] = table[0:ROWS_DEV, :]


def run_scatter(rows):
    sources, _, width = rows.shape
    whole = pl.BlockSpec(memory_space=pltpu.VMEM)
    return pl.pallas_call(
        scatter_kernel,
        in_specs=[whole],
        out_specs=whole,
        out_shape=jax.ShapeDtypeStruct((ROWS_DEV, width), F32),
        scratch_shapes=[
            pltpu.VMEM((ROWS_DEV + 8, width), F32),
            pltpu.VMEM((CAP, width), F32),
            pltpu.VMEM((sources, 2 * CAP), jnp.int32),
            pltpu.SMEM((sources, 2 * CAP), jnp.int32),
            pltpu.SemaphoreType.DMA,
        ],
        compiler_params=pltpu.CompilerParams(vmem_limit_bytes=32 * 1024 * 1024),
        cost_estimate=pl.CostEstimate(
            flops=2_000_000, bytes_accessed=6_000_000, transcendentals=0
        ),
        name="scatter",
    )(rows)


def ring(array, axis, size, shift):
    return lax.ppermute(array, axis, [(i, (i + shift) % size) for i in range(size)])


def swap_cores(array, count):
    return lax.ppermute(array, "table", [(i, i ^ 1) for i in range(count)])


def table_ring(array, stride, size, shift, count):
    pairs = []
    for i in range(count):
        place = (i // stride) % size
        pairs.append((i, i + (((place + shift) % size) - place) * stride))
    return lax.ppermute(array, "table", pairs)


def small_kernel(body, name, coords, arrays, outs, after=(), through=()):
    def kernel(place, *refs):
        first = len(arrays) + len(after) + len(through)
        body(place, *refs[: len(arrays)], *refs[first : first + len(outs)])

    whole = pl.BlockSpec(memory_space=pltpu.VMEM)
    return pl.pallas_call(
        kernel,
        in_specs=[pl.BlockSpec(memory_space=pltpu.SMEM)]
        + [whole] * len(arrays)
        + [pl.BlockSpec(memory_space=pl.ANY)] * (len(after) + len(through)),
        out_specs=[whole] * len(outs) + [pl.BlockSpec(memory_space=pl.ANY)] * len(through),
        out_shape=[jax.ShapeDtypeStruct(shape, kind) for shape, kind in outs]
        + [jax.ShapeDtypeStruct(a.shape, a.dtype) for a in through],
        input_output_aliases={
            1 + len(arrays) + len(after) + i: len(outs) + i for i in range(len(through))
        },
        compiler_params=pltpu.CompilerParams(vmem_limit_bytes=16 * 1024 * 1024),
        cost_estimate=pl.CostEstimate(
            flops=1_000_000, bytes_accessed=2_000_000, transcendentals=0
        ),
        name=name,
    )(coords, *arrays, *after, *through)


def block_rows(place, offset, rows):
    return pl.ds(pl.multiple_of(lax.rem(place + offset, 4) * rows, rows), rows)


def total(*terms):
    value = terms[0].astype(F32)
    for term in terms[1:]:
        value = value + term.astype(F32)
    return value.astype(BF)


def add_cores(coords, mine, theirs, far_a, far_b, right, left, own):
    me, rows = coords[0], own.shape[0]
    half = rows // 2
    far = block_rows(me, 2, rows)
    both = total(mine[far, :], theirs[far, :])
    far_a[...] = both[:half]
    far_b[...] = both[half:]
    for out, offset in ((right, 1), (left, 3), (own, 0)):
        part = block_rows(me, offset, rows)
        out[...] = total(mine[part, :], theirs[part, :])


def add_far(coords, right, left, from_left, from_right, to_right, to_left):
    half = from_left.shape[0]
    to_right[:half, :] = total(right[:half, :], from_left[...])
    to_right[half:, :] = right[half:, :]
    to_left[:half, :] = left[:half, :]
    to_left[half:, :] = total(left[half:, :], from_right[...])


def add_x(coords, own, from_left, from_right, scratch, right, left, far, mine):
    scratch[...] = total(own[...], from_left[...], from_right[...])
    for out, offset in ((right, 1), (left, 3), (far, 2), (mine, 0)):
        out[...] = scratch[block_rows(coords[2], offset, out.shape[0]), :]


def quarter(place, offset, rows, cols):
    index = lax.rem(place + offset, 4)
    return (
        pl.ds(pl.multiple_of(index // 2 * rows, rows), rows),
        pl.ds(pl.multiple_of(lax.rem(index, 2) * cols, cols), cols),
    )


def add_y(coords, own, from_left, from_right, from_far, scratch, right, left, far, mine):
    scratch[...] = total(own[...], from_left[...], from_right[...], from_far[...])
    for out, offset in ((right, 1), (left, 3), (far, 2), (mine, 0)):
        rows, cols = quarter(coords[3], offset, *out.shape)
        out[...] = scratch[rows, cols]


def add_z(coords, own, from_left, from_right, from_far, out):
    out[...] = total(own[...], from_left[...], from_right[...], from_far[...])


def join_z(coords, own, left, right, far, out):
    for piece, offset in ((own, 0), (left, 3), (right, 1), (far, 2)):
        rows, cols = quarter(coords[3], offset, *piece.shape)
        out[rows, cols] = piece[...]


def join_y(coords, own, left, right, far, out):
    for piece, offset in ((own, 0), (left, 3), (right, 1), (far, 2)):
        out[block_rows(coords[2], offset, piece.shape[0]), :] = piece[...]


def join_cores(factor, coords, own, theirs, share_in, share_out):
    core = coords[1]
    cut = own.shape[1]
    width = share_in.shape[1]

    def put(first, second):
        share_in[:, :cut] = first[...].astype(F32) * factor
        share_in[:, cut:] = second[:, : width - cut].astype(F32) * factor
        share_out[...] = second[:, width - cut :].astype(F32) * factor

    @pl.when(core == 0)
    def _():
        put(own, theirs)

    @pl.when(core == 1)
    def _():
        put(theirs, own)


def three_ways(shift, right, left, far):
    return shift(right, 1), shift(left, -1), shift(far, 2)


def per_device(
    embedded, grad_out, w_in, w_out, lengths, slot_of, local_rows, send_counts, send_offsets
):
    fsdp_count = lax.axis_size("fsdp")
    table_count = lax.axis_size("table")
    fsdp, table = lax.axis_index("fsdp"), lax.axis_index("table")
    core = lax.rem(table, 2)
    coords = jnp.stack([fsdp, core, table // 8, lax.rem(table // 2, 4)]).astype(jnp.int32)
    counts, offsets = send_counts[0], send_offsets[0]

    def along_x(array, shift):
        return ring(array, "fsdp", 4, shift)

    def along_y(array, shift):
        return table_ring(array, 8, 4, shift, table_count)

    def along_z(array, shift):
        return table_ring(array, 2, 4, shift, table_count)

    half = jnp.concatenate(
        [lax.dynamic_slice_in_dim(a, core * 64, 64, 0) for a in (w_in, w_out)], axis=1
    )
    low, high = along_x(half, 1), along_x(half, -1)
    labels = run_labels(counts, offsets, local_rows)
    low, high, labels = lax.optimization_barrier((low, high, labels))
    far_a, far_b = along_x(low[:32], 1), along_x(high[32:], -1)
    normed, turned = run_norm(embedded, labels)
    far_a, far_b, normed = lax.optimization_barrier((far_a, far_b, normed))
    low_o, high_o, far_ao, far_bo = (
        swap_cores(a, table_count) for a in (low, high, far_a, far_b)
    )
    pieces = [w_in, w_out, low, high, low_o, high_o, far_a, far_b, far_ao, far_bo]

    shift = jnp.where(
        slot_of[None, :] >= offsets[1:, None], CAP - counts[:-1, None], 0
    ).sum(axis=0)
    bucket = (slot_of + shift).reshape(1, -1)

    grad_proj, mine, other, w_full = run_layer(
        coords, lengths, normed, turned, grad_out, pieces
    )

    theirs = swap_cores(other, table_count)
    tokens = run_tokens(embedded, grad_out, grad_proj, w_full, other)

    rows, cols = mine.shape
    block, part = rows // 4, rows // 16
    far_a, far_b, right, left, own = small_kernel(
        add_cores,
        "add_cores",
        coords,
        (mine, theirs),
        [((block // 2, cols), BF)] * 2 + [((block, cols), BF)] * 3,
        after=(tokens,),
    )
    from_left, from_right = along_x(far_a, 1), along_x(far_b, -1)
    bucket_rows = run_buckets(bucket, labels, tokens, fsdp_count, own)
    to_right, to_left, bucket_rows = small_kernel(
        add_far,
        "add_far",
        coords,
        (right, left, from_left, from_right),
        [((block, cols), BF)] * 2,
        through=(bucket_rows,),
    )
    from_left, from_right = along_x(to_right, 1), along_x(to_left, -1)

    values = bucket_rows.reshape(fsdp_count * table_count, PACKET, 128)
    got = lax.all_to_all(values, BOTH, split_axis=0, concat_axis=0, tiled=True)

    _, right, left, far, own = small_kernel(
        add_x,
        "add_x",
        coords,
        (own, from_left, from_right),
        [((block, cols), BF)] + [((part, cols), BF)] * 4,
    )
    _, right, left, far, own = small_kernel(
        add_y,
        "add_y",
        coords,
        (own, *three_ways(along_y, right, left, far)),
        [((part, cols), BF)] + [((part // 2, cols // 2), BF)] * 4,
    )
    (own,) = small_kernel(
        add_z,
        "add_z",
        coords,
        (own, *three_ways(along_z, right, left, far)),
        [((part // 2, cols // 2), BF)],
    )
    (own,) = small_kernel(
        join_z,
        "join_z",
        coords,
        (own, *three_ways(along_z, own, own, own)),
        [((part, cols), BF)],
    )
    (own,) = small_kernel(
        join_y,
        "join_y",
        coords,
        (own, *three_ways(along_y, own, own, own)),
        [((block, cols), BF)],
    )
    factor = 1.0 / math.sqrt(embedded.shape[0] * fsdp_count * table_count)
    share_in, share_out = small_kernel(
        functools.partial(join_cores, factor),
        "join_cores",
        coords,
        (own, swap_cores(own, table_count)),
        [((block, 4 * WIDTH), F32), ((block, WIDTH), F32)],
    )

    grad_table = run_scatter(got)
    return (share_in, share_out, grad_table)


def solution(mesh):
    placed = (
        P(BOTH, None),
        P(BOTH, None),
        P("fsdp", None),
        P("fsdp", None),
        P(BOTH),
        P(BOTH),
        P(BOTH),
        P(BOTH, None),
        P(BOTH, None),
    )
    return jax.shard_map(
        per_device,
        mesh=mesh,
        in_specs=placed,
        out_specs=(P("fsdp", None), P("fsdp", None), P("table", "fsdp")),
        check_vma=False,
    )
```

time: 590 us -> 227 us (0.38)
  matrix products: 139 us -> 0 us
  waiting for transfers between devices: 182 us -> 48.8 us
  Pallas kernels: 0 us -> 120 us
  local copies, waits for them, and re-layouts: 121 us -> 8.1 us
  other arithmetic: 93.2 us -> 1.45 us
  starting transfers between devices: 24.2 us -> 45.4 us
  between operations: 14.8 us -> 1.06 us
  blocking collectives: 11.3 us -> 0 us
    psum x1 -> x0, waiting for transfers between devices: 181 us -> none  [per_device(): total_in, total_out = lax.psum((grad_win, grad_wout), ('fsdp', 'table'))]
    dot_general x30 -> x0, matrix products: 139 us -> none  [the longest x12 52.4 us: one_seq(): jnp.einsum('hqk,khd->qhd', weights_b, value_seq, preferred_element_type=j...]
    pallas_call x0 -> x14, Pallas kernels: none -> 120 us  [the longest x1 54.4 us: run_layer(): pl.pallas_call(layer_kernel, grid=(tokens // SEQ,), in_specs=[smem, smem,...]
    ppermute x0 -> x26, waiting for transfers between devices: none -> 48.8 us  [the longest x8 32.4 us: ring(): lax.ppermute(array, axis, [(i, (i + shift) % size) for i in range(size)])]
    scatter-add x1 -> x0, other arithmetic: 46.9 us -> none  [per_device(): jax.ops.segment_sum(flat_values, flat_labels, num_segments=ROWS_DEV + 1)]
    ppermute x0 -> x26, starting transfers between devices: none -> 35.4 us  [the longest x12 14.9 us: table_ring(): return lax.ppermute(array, 'table', pairs)]
    gather x4 -> x0, local copies, waits for them, and re-layouts: 26 us -> none  [the longest x2 14.2 us: per_device(): bucket = jnp.where(in_use[:, :, None], uniq_grad[slot_index], 0.0)]
    unnamed x71 -> x36, local copies, waits for them, and re-layouts: 29.6 us -> 6.25 us
  transfers between devices with their start and end apart: 4 -> 27, of which waited for: 1 -> 11; matrix products, arithmetic and copies ran while one was open for 51% -> 1% of each run, Pallas kernels for 0% -> 21%
where the time goes in v1:
time: 227 us; the launch traced here: 225 us
  Pallas kernels  120 us (53%)
  waiting for transfers between devices  48.8 us (21%)
  starting transfers between devices  45.4 us (20%)
  local copies, waits for them, and re-layouts  8.1 us (4%)
    pallas_call x1, Pallas kernels, run_layer(): pl.pallas_call(layer_kernel, grid=(tokens // SEQ,), in_specs=[smem, smem,...  54.4 us
    ppermute x8, waiting for transfers between devices, ring(): lax.ppermute(array, axis, [(i, (i + shift) % size) for i in range(size)])  32.4 us
    pallas_call x1, Pallas kernels, run_tokens(): pl.pallas_call(token_kernel, grid=(count // SEQ,), in_specs=[by_seq(WIDTH...  17.7 us
    pallas_call x1, Pallas kernels, run_scatter(): pl.pallas_call(scatter_kernel, in_specs=[whole], out_specs=whole, out_sha...  16.5 us
    ppermute x12, starting transfers between devices, table_ring(): return lax.ppermute(array, 'table', pairs)  14.9 us
    ppermute x12, waiting for transfers between devices, table_ring(): return lax.ppermute(array, 'table', pairs)  14.4 us
    ppermute x8, starting transfers between devices, ring(): lax.ppermute(array, axis, [(i, (i + shift) % size) for i in range(size)])  10.5 us
    all_to_all x1, starting transfers between devices, per_device(): got = lax.all_to_all(values, BOTH, split_axis=0, concat_axis=0, tiled=True)  10 us
  transfers between devices with their start and end apart: 27, of which 11 were waited for; matrix products, arithmetic and copies ran while one was open for 1% of the time, Pallas kernels for 21%

profile of v1, /device:TPU:1, one launch (start us, length us, event | category | flops | bytes accessed | tf_op | source)
XLA Modules:
  0.0 225.2 jit_solution(16948238903001124950)
XLA Ops:
  2.5 2.1 collective-permute-start
  6.0 8.2 %labels.1.after = s32[32,128]{1,0:T(8,128)} custom-call(s32[32]{0:T(128)} %bitcast.14, s32[32]{0:T(128)} %bitcast.15, s32[1614]{0:T(1024)} %rows.1), custom_call_target="tpu_custom_call" | custom-call | flops 10000 | bytes 10000 | tf_op jit(solution)/shard_map/labels/pallas_call | solution.py:378
  14.4 2.6 %collective-permute-start.3 = (bf16[32,2560]{1,0:T(8,128)(2,1)S(1)}, bf16[32,2560]{1,0:T(8,128)(2,1)S(1)}, u32[]{:S(2)}, u32[]{:S(2)}) collective-permute-start(bf16[32,2560]{1,0:T(8,128)(2,1)S(1)} %slice.15), channel_id=1, source_target_pairs={{0,96},{32,0},{64,32},{96,64},{1,97},{33,1},{65,33},{97,65},{2,98}... | collective-permute-start | bytes 491528 | tf_op jit(solution)/shard_map/ppermute | solution.py:446
  17.1 1.8 collective-permute-start.4
  18.9 8.5 %norm.1 = (bf16[2048,512]{1,0:T(8,128)(2,1)}, bf16[512,2048]{1,0:T(8,128)(2,1)}) custom-call(bf16[2048,512]{1,0:T(8,128)(2,1)} %emb.3, s32[32,128]{1,0:T(8,128)} %labels.1.after), custom_call_target="tpu_custom_call" | custom-call | flops 20000000 | bytes 6000000 | tf_op jit(solution)/shard_map/norm/pallas_call | solution.py:65
  30.3 54.4 %layer.1 = (bf16[2048,2048]{1,0:T(8,128)(2,1)}, bf16[512,1280]{1,0:T(8,128)(2,1)}, bf16[512,1280]{1,0:T(8,128)(2,1)}, bf16[2048,512]{1,0:T(8,128)(2,1)}) custom-call(s32[4]{0:T(128)} %pad_add_fusion.coords.place, s32[4]{0:T(128)} %lens.1, bf16[2048,512]{1,0:T(8,128)(2,1)} %get-tuple-element.37.normed, bf16[2048,512]{1,0:T(8,128)(2,1)} %go.3, ...), custom_call_target="tpu_custom_call" | custom-call | flops 20000000000 | bytes 20000000 | tf_op jit(solution)/shard_map/layer/pallas_call | solution.py:247
  85.8 17.7 %token_grads.1.refs_2_.tokens = bf16[2048,512]{1,0:T(8,128)(2,1)} custom-call(bf16[2048,512]{1,0:T(8,128)(2,1)} %emb.3, bf16[2048,512]{1,0:T(8,128)(2,1)} %go.3, bf16[2048,2048]{1,0:T(8,128)(2,1)} %get-tuple-element.43.gp, bf16[2048,512]{1,0:T(8,128)(2,1)} %get-tuple-element.44.w, bf16[512,1280]{1,0:T(8,128)(2,1)} %get-tuple-element.42.after), custom_call_target="tpu_custom_call" | custom-call | flops 4300000256 | bytes 16000000 | tf_op jit(solution)/shard_map/token_grads/pallas_call | solution.py:303
  103.6 1.6 copy-done.2
  108.2 7.5 %bucket_rows.1.refs_4_ = bf16[4,32,72,128]{3,2,1,0:T(8,128)(2,1)} custom-call(s32[1,2048]{1,0:T(1,128)} %bitcast.13, s32[32,128]{1,0:T(8,128)} %labels.1.after, bf16[2048,512]{1,0:T(8,128)(2,1)} %token_grads.1.refs_2_.tokens, bf16[128,1280]{1,0:T(8,128)(2,1)} %copy-done.4), custom_call_target="tpu_custom_call" | custom-call | flops 4300000256 | bytes 6000000 | tf_op jit(solution)/shard_map/bucket_rows/pallas_call | solution.py:344
  115.7 1.7 copy-done
  119.4 10.0 %all-to-all-start = ((bf16[128,72,128]{2,1,0:T(8,128)(2,1)}), bf16[128,72,128]{2,1,0:T(8,128)(2,1)S(1)}, u32[]{:S(2)}, u32[]{:S(2)}) async-start(bf16[128,72,128]{2,1,0:T(8,128)(2,1)} %bitcast.12), calls=%async_computation | async-start | bytes 4718592 | tf_op jit(solution)/shard_map/all_to_all | solution.py:644
  132.2 32.4 %collective-permute-done.11.refs_1_ = bf16[128,1280]{1,0:T(8,128)(2,1)S(1)} collective-permute-done((bf16[128,1280]{1,0:T(8,128)(2,1)S(1)}, bf16[128,1280]{1,0:T(8,128)(2,1)S(1)}, u32[]{:S(2)}, u32[]{:S(2)}) %collective-permute-start.11) | collective-permute-done | bytes 327712 | tf_op jit(solution)/shard_map/ppermute | solution.py:446
  168.8 1.5 collective-permute-start.15
  170.6 3.1 %collective-permute-done.15.refs_3_ = bf16[32,1280]{1,0:T(8,128)(2,1)S(1)} collective-permute-done((bf16[32,1280]{1,0:T(8,128)(2,1)S(1)}, bf16[32,1280]{1,0:T(8,128)(2,1)S(1)}, u32[]{:S(2)}, u32[]{:S(2)}) %collective-permute-start.15) | collective-permute-done | bytes 81952 | tf_op jit(solution)/shard_map/ppermute | solution.py:458
  176.3 1.8 collective-permute-start.17
  179.6 2.6 %collective-permute-done.18.refs_3_ = bf16[16,640]{1,0:T(8,128)(2,1)S(1)} collective-permute-done((bf16[16,640]{1,0:T(8,128)(2,1)S(1)}, bf16[16,640]{1,0:T(8,128)(2,1)S(1)}, u32[]{:S(2)}, u32[]{:S(2)}) %collective-permute-start.18) | collective-permute-done | bytes 20512 | tf_op jit(solution)/shard_map/ppermute | solution.py:458
  182.9 2.7 %collective-permute-start.20 = (bf16[16,640]{1,0:T(8,128)(2,1)S(1)}, bf16[16,640]{1,0:T(8,128)(2,1)S(1)}, u32[]{:S(2)}, u32[]{:S(2)}) collective-permute-start(bf16[16,640]{1,0:T(8,128)(2,1)S(1)} %add_z.1.refs_0_), channel_id=1, source_target_pairs={{0,6},{1,7},{2,0},{3,1},{4,2},{5,3},{6,4},{7,5},{8,14},{9,15},{10,... | collective-permute-start | bytes 61448 | tf_op jit(solution)/shard_map/ppermute | solution.py:458
  186.7 3.0 %collective-permute-done.21.refs_3_ = bf16[16,640]{1,0:T(8,128)(2,1)S(1)} collective-permute-done((bf16[16,640]{1,0:T(8,128)(2,1)S(1)}, bf16[16,640]{1,0:T(8,128)(2,1)S(1)}, u32[]{:S(2)}, u32[]{:S(2)}) %collective-permute-start.21) | collective-permute-done | bytes 20512 | tf_op jit(solution)/shard_map/ppermute | solution.py:458
  190.8 2.2 collective-permute-start.23
  193.2 1.6 collective-permute-done.22.refs_1_
  194.8 3.0 %collective-permute-done.24.refs_3_ = bf16[32,1280]{1,0:T(8,128)(2,1)S(1)} collective-permute-done((bf16[32,1280]{1,0:T(8,128)(2,1)S(1)}, bf16[32,1280]{1,0:T(8,128)(2,1)S(1)}, u32[]{:S(2)}, u32[]{:S(2)}) %collective-permute-start.24) | collective-permute-done | bytes 81952 | tf_op jit(solution)/shard_map/ppermute | solution.py:458
  198.4 7.2 %collective-permute-start.25 = (bf16[128,1280]{1,0:T(8,128)(2,1)S(1)}, bf16[128,1280]{1,0:T(8,128)(2,1)S(1)}, u32[]{:S(2)}, u32[]{:S(2)}) collective-permute-start(bf16[128,1280]{1,0:T(8,128)(2,1)S(1)} %join_y.1.refs_0_), channel_id=1, source_target_pairs={{0,1},{1,0},{2,3},{3,2},{4,5},{5,4},{6,7},{7,6},{8,9},{9,8},{10,11... | collective-permute-start | bytes 983048 | tf_op jit(solution)/shard_map/ppermute | solution.py:450
  206.8 1.7 join_cores.1
  208.5 16.5 %scatter.1 = f32[4096,128]{1,0:T(8,128)} custom-call(bf16[128,72,128]{2,1,0:T(8,128)(2,1)S(1)} %all-to-all-done.rows), custom_call_target="tpu_custom_call" | custom-call | flops 2000000 | bytes 6000000 | tf_op jit(solution)/shard_map/scatter/pallas_call | solution.py:425
  (89 shorter events, 28.8 us)
Async XLA Ops:
  2.5 11.7 %collective-permute-start = (bf16[64,2560]{1,0:T(8,128)(2,1)S(1)}, bf16[64,2560]{1,0:T(8,128)(2,1)S(1)}, u32[]{:S(2)}, u32[]{:S(2)}) collective-permute-start(bf16[64,2560]{1,0:T(8,128)(2,1)S(1)} %pad_maximum_fusion), channel_id=1, source_target_pairs={{0,32},{32,64},{64,96},{96,0},{1,33},{33,65},{65,97},{97,1},{2,34}... | collective-permute-start | bytes 983048 | tf_op jit(solution)/shard_map/ppermute | solution.py:446
  4.6 9.6 %collective-permute-start.1 = (bf16[64,2560]{1,0:T(8,128)(2,1)S(1)}, bf16[64,2560]{1,0:T(8,128)(2,1)S(1)}, u32[]{:S(2)}, u32[]{:S(2)}) collective-permute-start(bf16[64,2560]{1,0:T(8,128)(2,1)S(1)} %pad_maximum_fusion), channel_id=1, source_target_pairs={{0,96},{32,0},{64,32},{96,64},{1,97},{33,1},{65,33},{97,65},{2,98}... | collective-permute-start | bytes 983048 | tf_op jit(solution)/shard_map/ppermute | solution.py:446
  14.2 13.2 %collective-permute-start.2 = (bf16[32,2560]{1,0:T(8,128)(2,1)S(1)}, bf16[32,2560]{1,0:T(8,128)(2,1)S(1)}, u32[]{:S(2)}, u32[]{:S(2)}) collective-permute-start(bf16[32,2560]{1,0:T(8,128)(2,1)S(1)} %slice.14), channel_id=1, source_target_pairs={{0,32},{32,64},{64,96},{96,0},{1,33},{33,65},{65,97},{97,1},{2,34}... | collective-permute-start | bytes 491528 | tf_op jit(solution)/shard_map/ppermute | solution.py:446
  14.4 13.0 %collective-permute-start.3 = (bf16[32,2560]{1,0:T(8,128)(2,1)S(1)}, bf16[32,2560]{1,0:T(8,128)(2,1)S(1)}, u32[]{:S(2)}, u32[]{:S(2)}) collective-permute-start(bf16[32,2560]{1,0:T(8,128)(2,1)S(1)} %slice.15), channel_id=1, source_target_pairs={{0,96},{32,0},{64,32},{96,64},{1,97},{33,1},{65,33},{97,65},{2,98}... | collective-permute-start | bytes 491528 | tf_op jit(solution)/shard_map/ppermute | solution.py:446
  17.1 12.4 %collective-permute-start.4 = (bf16[64,2560]{1,0:T(8,128)(2,1)S(1)}, bf16[64,2560]{1,0:T(8,128)(2,1)S(1)}, u32[]{:S(2)}, u32[]{:S(2)}) collective-permute-start(bf16[64,2560]{1,0:T(8,128)(2,1)S(1)} %collective-permute-done.low), channel_id=1, source_target_pairs={{0,1},{1,0},{2,3},{3,2},{4,5},{5,4},{6,7},{7,6},{8,9},{9,8},{10,11... | collective-permute-start | bytes 983048 | tf_op jit(solution)/shard_map/ppermute | solution.py:450
  18.9 10.5 %collective-permute-start.5 = (bf16[64,2560]{1,0:T(8,128)(2,1)S(1)}, bf16[64,2560]{1,0:T(8,128)(2,1)S(1)}, u32[]{:S(2)}, u32[]{:S(2)}) collective-permute-start(bf16[64,2560]{1,0:T(8,128)(2,1)S(1)} %collective-permute-done.1.high), channel_id=1, source_target_pairs={{0,1},{1,0},{2,3},{3,2},{4,5},{5,4},{6,7},{7,6},{8,9},{9,8},{10,11... | collective-permute-start | bytes 983048 | tf_op jit(solution)/shard_map/ppermute | solution.py:450
  84.7 18.8 %collective-permute-start.8 = (bf16[512,1280]{1,0:T(8,128)(2,1)}, bf16[512,1280]{1,0:T(8,128)(2,1)S(1)}, u32[]{:S(2)}, u32[]{:S(2)}) collective-permute-start(bf16[512,1280]{1,0:T(8,128)(2,1)} %get-tuple-element.42.after), channel_id=1, source_target_pairs={{0,1},{1,0},{2,3},{3,2},{4,5},{5,4},{6,7},{7,6},{8,9},{9,8},{10,11... | collective-permute-start | bytes 3932168 | tf_op jit(solution)/shard_map/ppermute | solution.py:450
  106.7 9.0 %collective-permute-start.10 = (bf16[64,1280]{1,0:T(8,128)(2,1)S(1)}, bf16[64,1280]{1,0:T(8,128)(2,1)S(1)}, u32[]{:S(2)}, u32[]{:S(2)}) collective-permute-start(bf16[64,1280]{1,0:T(8,128)(2,1)S(1)} %get-tuple-element.49), channel_id=1, source_target_pairs={{0,96},{32,0},{64,32},{96,64},{1,97},{33,1},{65,33},{97,65},{2,98}... | collective-permute-start | bytes 491528 | tf_op jit(solution)/shard_map/ppermute | solution.py:446
  107.3 8.4 %collective-permute-start.9 = (bf16[64,1280]{1,0:T(8,128)(2,1)S(1)}, bf16[64,1280]{1,0:T(8,128)(2,1)S(1)}, u32[]{:S(2)}, u32[]{:S(2)}) collective-permute-start(bf16[64,1280]{1,0:T(8,128)(2,1)S(1)} %get-tuple-element.48), channel_id=1, source_target_pairs={{0,32},{32,64},{64,96},{96,0},{1,33},{33,65},{65,97},{97,1},{2,34}... | collective-permute-start | bytes 491528 | tf_op jit(solution)/shard_map/ppermute | solution.py:446
  119.4 89.1 %all-to-all-start = ((bf16[128,72,128]{2,1,0:T(8,128)(2,1)}), bf16[128,72,128]{2,1,0:T(8,128)(2,1)S(1)}, u32[]{:S(2)}, u32[]{:S(2)}) async-start(bf16[128,72,128]{2,1,0:T(8,128)(2,1)} %bitcast.12), calls=%async_computation | async-start | bytes 4718592 | tf_op jit(solution)/shard_map/all_to_all | solution.py:644
  129.4 35.2 %collective-permute-start.11 = (bf16[128,1280]{1,0:T(8,128)(2,1)S(1)}, bf16[128,1280]{1,0:T(8,128)(2,1)S(1)}, u32[]{:S(2)}, u32[]{:S(2)}) collective-permute-start(bf16[128,1280]{1,0:T(8,128)(2,1)S(1)} %get-tuple-element.50), channel_id=1, source_target_pairs={{0,32},{32,64},{64,96},{96,0},{1,33},{33,65},{65,97},{97,1},{2,34}... | collective-permute-start | bytes 983048 | tf_op jit(solution)/shard_map/ppermute | solution.py:446
  130.9 33.7 %collective-permute-start.12 = (bf16[128,1280]{1,0:T(8,128)(2,1)S(1)}, bf16[128,1280]{1,0:T(8,128)(2,1)S(1)}, u32[]{:S(2)}, u32[]{:S(2)}) collective-permute-start(bf16[128,1280]{1,0:T(8,128)(2,1)S(1)} %get-tuple-element.51), channel_id=1, source_target_pairs={{0,96},{32,0},{64,32},{96,64},{1,97},{33,1},{65,33},{97,65},{2,98}... | collective-permute-start | bytes 983048 | tf_op jit(solution)/shard_map/ppermute | solution.py:446
  166.1 4.5 %collective-permute-start.13 = (bf16[32,1280]{1,0:T(8,128)(2,1)S(1)}, bf16[32,1280]{1,0:T(8,128)(2,1)S(1)}, u32[]{:S(2)}, u32[]{:S(2)}) collective-permute-start(bf16[32,1280]{1,0:T(8,128)(2,1)S(1)} %get-tuple-element.53), channel_id=1, source_target_pairs={{0,8},{1,9},{2,10},{3,11},{4,12},{5,13},{6,14},{7,15},{8,16},{9,17... | collective-permute-start | bytes 245768 | tf_op jit(solution)/shard_map/ppermute | solution.py:458
  167.3 3.3 %collective-permute-start.14 = (bf16[32,1280]{1,0:T(8,128)(2,1)S(1)}, bf16[32,1280]{1,0:T(8,128)(2,1)S(1)}, u32[]{:S(2)}, u32[]{:S(2)}) collective-permute-start(bf16[32,1280]{1,0:T(8,128)(2,1)S(1)} %get-tuple-element.54), channel_id=1, source_target_pairs={{0,24},{1,25},{2,26},{3,27},{4,28},{5,29},{6,30},{7,31},{8,0},{9,1... | collective-permute-start | bytes 245768 | tf_op jit(solution)/shard_map/ppermute | solution.py:458
  168.8 4.9 %collective-permute-start.15 = (bf16[32,1280]{1,0:T(8,128)(2,1)S(1)}, bf16[32,1280]{1,0:T(8,128)(2,1)S(1)}, u32[]{:S(2)}, u32[]{:S(2)}) collective-permute-start(bf16[32,1280]{1,0:T(8,128)(2,1)S(1)} %get-tuple-element.55), channel_id=1, source_target_pairs={{0,16},{1,17},{2,18},{3,19},{4,20},{5,21},{6,22},{7,23},{8,24},{9,... | collective-permute-start | bytes 245768 | tf_op jit(solution)/shard_map/ppermute | solution.py:458
  174.9 4.7 %collective-permute-start.16 = (bf16[16,640]{1,0:T(8,128)(2,1)S(1)}, bf16[16,640]{1,0:T(8,128)(2,1)S(1)}, u32[]{:S(2)}, u32[]{:S(2)}) collective-permute-start(bf16[16,640]{1,0:T(8,128)(2,1)S(1)} %get-tuple-element.57), channel_id=1, source_target_pairs={{0,2},{1,3},{2,4},{3,5},{4,6},{5,7},{6,0},{7,1},{8,10},{9,11},{10,... | collective-permute-start | bytes 61448 | tf_op jit(solution)/shard_map/ppermute | solution.py:458
  178.1 4.1 %collective-permute-start.18 = (bf16[16,640]{1,0:T(8,128)(2,1)S(1)}, bf16[16,640]{1,0:T(8,128)(2,1)S(1)}, u32[]{:S(2)}, u32[]{:S(2)}) collective-permute-start(bf16[16,640]{1,0:T(8,128)(2,1)S(1)} %get-tuple-element.59), channel_id=1, source_target_pairs={{0,4},{1,5},{2,6},{3,7},{4,0},{5,1},{6,2},{7,3},{8,12},{9,13},{10,... | collective-permute-start | bytes 61448 | tf_op jit(solution)/shard_map/ppermute | solution.py:458
  182.8 3.9 %collective-permute-start.19 = (bf16[16,640]{1,0:T(8,128)(2,1)S(1)}, bf16[16,640]{1,0:T(8,128)(2,1)S(1)}, u32[]{:S(2)}, u32[]{:S(2)}) collective-permute-start(bf16[16,640]{1,0:T(8,128)(2,1)S(1)} %add_z.1.refs_0_), channel_id=1, source_target_pairs={{0,2},{1,3},{2,4},{3,5},{4,6},{5,7},{6,0},{7,1},{8,10},{9,11},{10,... | collective-permute-start | bytes 61448 | tf_op jit(solution)/shard_map/ppermute | solution.py:458
  182.9 3.8 %collective-permute-start.20 = (bf16[16,640]{1,0:T(8,128)(2,1)S(1)}, bf16[16,640]{1,0:T(8,128)(2,1)S(1)}, u32[]{:S(2)}, u32[]{:S(2)}) collective-permute-start(bf16[16,640]{1,0:T(8,128)(2,1)S(1)} %add_z.1.refs_0_), channel_id=1, source_target_pairs={{0,6},{1,7},{2,0},{3,1},{4,2},{5,3},{6,4},{7,5},{8,14},{9,15},{10,... | collective-permute-start | bytes 61448 | tf_op jit(solution)/shard_map/ppermute | solution.py:458
  185.5 4.1 %collective-permute-start.21 = (bf16[16,640]{1,0:T(8,128)(2,1)S(1)}, bf16[16,640]{1,0:T(8,128)(2,1)S(1)}, u32[]{:S(2)}, u32[]{:S(2)}) collective-permute-start(bf16[16,640]{1,0:T(8,128)(2,1)S(1)} %add_z.1.refs_0_), channel_id=1, source_target_pairs={{0,4},{1,5},{2,6},{3,7},{4,0},{5,1},{6,2},{7,3},{8,12},{9,13},{10,... | collective-permute-start | bytes 61448 | tf_op jit(solution)/shard_map/ppermute | solution.py:458
  190.3 4.6 %collective-permute-start.22 = (bf16[32,1280]{1,0:T(8,128)(2,1)S(1)}, bf16[32,1280]{1,0:T(8,128)(2,1)S(1)}, u32[]{:S(2)}, u32[]{:S(2)}) collective-permute-start(bf16[32,1280]{1,0:T(8,128)(2,1)S(1)} %join_z.1.refs_0_), channel_id=1, source_target_pairs={{0,8},{1,9},{2,10},{3,11},{4,12},{5,13},{6,14},{7,15},{8,16},{9,17... | collective-permute-start | bytes 245768 | tf_op jit(solution)/shard_map/ppermute | solution.py:458
  190.8 4.1 %collective-permute-start.23 = (bf16[32,1280]{1,0:T(8,128)(2,1)S(1)}, bf16[32,1280]{1,0:T(8,128)(2,1)S(1)}, u32[]{:S(2)}, u32[]{:S(2)}) collective-permute-start(bf16[32,1280]{1,0:T(8,128)(2,1)S(1)} %join_z.1.refs_0_), channel_id=1, source_target_pairs={{0,24},{1,25},{2,26},{3,27},{4,28},{5,29},{6,30},{7,31},{8,0},{9,1... | collective-permute-start | bytes 245768 | tf_op jit(solution)/shard_map/ppermute | solution.py:458
  193.0 4.8 %collective-permute-start.24 = (bf16[32,1280]{1,0:T(8,128)(2,1)S(1)}, bf16[32,1280]{1,0:T(8,128)(2,1)S(1)}, u32[]{:S(2)}, u32[]{:S(2)}) collective-permute-start(bf16[32,1280]{1,0:T(8,128)(2,1)S(1)} %join_z.1.refs_0_), channel_id=1, source_target_pairs={{0,16},{1,17},{2,18},{3,19},{4,20},{5,21},{6,22},{7,23},{8,24},{9,... | collective-permute-start | bytes 245768 | tf_op jit(solution)/shard_map/ppermute | solution.py:458
  198.4 8.4 %collective-permute-start.25 = (bf16[128,1280]{1,0:T(8,128)(2,1)S(1)}, bf16[128,1280]{1,0:T(8,128)(2,1)S(1)}, u32[]{:S(2)}, u32[]{:S(2)}) collective-permute-start(bf16[128,1280]{1,0:T(8,128)(2,1)S(1)} %join_y.1.refs_0_), channel_id=1, source_target_pairs={{0,1},{1,0},{2,3},{3,2},{4,5},{5,4},{6,7},{7,6},{8,9},{9,8},{10,11... | collective-permute-start | bytes 983048 | tf_op jit(solution)/shard_map/ppermute | solution.py:450
  (21 other events, 294.1 us)

commit v2 on v1

--- a/solution.py
+++ b/solution.py
@@ -49,14 +49,8 @@
 
 
 def norm_kernel(emb, after, normed, turned):
-    chunk = 64
-
-    @pl.loop(0, SEQ // chunk)
-    def _(i):
-        rows = pl.ds(pl.multiple_of(i * chunk, chunk), chunk)
-        xhat, _ = normalise(emb[rows, :].astype(F32))
-        normed[rows, :] = xhat.astype(BF)
-
+    xhat, _ = normalise(emb[...].astype(F32))
+    normed[...] = xhat.astype(BF)
     turned[...] = normed[...].T
 
 
@@ -89,7 +83,7 @@
     coords, lens, normed, go, turned, own_in, own_out,
     low, high, low_o, high_o, far_a, far_b, far_ao, far_bo,
     gp, mine, other, w_turned,
-    w, proj, slope, hidden, probs, rates, mixed, cot, seq_sum, gp_all, gwout,
+    w, slope, hidden, probs, rates, mixed, cot, seq_sum, gp_all, gwout,
 ):
     step = pl.program_id(0)
 
@@ -119,22 +113,13 @@
             cols = pl.ds(pl.multiple_of(i * WIDTH, WIDTH), WIDTH)
             w_turned[cols, :] = w[:, cols].T
 
-    chunk = 64
-
-    def rows_of(i, size=chunk):
-        return pl.ds(pl.multiple_of(i * size, size), size)
-
     for block in range(4):
         cols = slice(block * WIDTH, (block + 1) * WIDTH)
-        proj[...] = dot_nn(normed[...], w[:, cols])
-
-        @pl.loop(0, SEQ // chunk)
-        def _(i):
-            half = 0.5 * proj[rows_of(i), :]
-            t = jnp.tanh(half)
-            ht = half * t
-            hidden[rows_of(i), cols] = (half + ht).astype(BF)
-            slope[rows_of(i), cols] = 0.5 * ((1.0 + half) + t * (1.0 - ht))
+        half = 0.5 * dot_nn(normed[...], w[:, cols])
+        t = jnp.tanh(half)
+        ht = half * t
+        hidden[:, cols] = (half + ht).astype(BF)
+        slope[:, cols] = 0.5 * ((1.0 + half) + t * (1.0 - ht))
 
     factor = 0.5 / math.sqrt(HEAD_DIM)
 
@@ -165,25 +150,18 @@
                 probs[head, q_rows, seen], hidden[seen, v_cols]
             )
 
-    proj[...] = dot_nt(go[...], w[:, 4 * WIDTH :])
-    seq_len = lens[step]
-
-    @pl.loop(0, SEQ // chunk)
-    def _(i):
-        rows = rows_of(i)
-        place = lax.broadcasted_iota(jnp.int32, (chunk, 1), 0) + i * chunk
-        keep = place < seq_len
-        raw = jnp.where(keep, mixed[rows, :] * (1.0 / SEQ), 0.0)
-        xhat, rstd = normalise(raw)
-        gate = hidden[rows, 0:WIDTH].astype(F32)
-        down = proj[rows, :].astype(BF).astype(F32)
-        seq_sum[rows, :] = (xhat * gate).astype(BF)
-        grad_gate = ((down * xhat).astype(BF).astype(F32) * slope[rows, 0:WIDTH]).astype(BF)
-        gp[rows, 0:WIDTH] = grad_gate
-        gp_all[pl.ds(pl.multiple_of(step * SEQ + i * chunk, chunk), chunk), 0:WIDTH] = grad_gate
-        back = norm_back(xhat, rstd, down * gate)
-        cot[rows, :] = jnp.where(keep, back * (1.0 / SEQ), 0.0).astype(BF)
-
+    here = pl.ds(pl.multiple_of(step * SEQ, SEQ), SEQ)
+    keep = lax.broadcasted_iota(jnp.int32, (SEQ, 1), 0) < lens[step]
+    raw = jnp.where(keep, mixed[...] * (1.0 / SEQ), 0.0)
+    xhat, rstd = normalise(raw)
+    gate = hidden[:, 0:WIDTH].astype(F32)
+    down = dot_nt(go[...], w[:, 4 * WIDTH :]).astype(BF).astype(F32)
+    seq_sum[...] = (xhat * gate).astype(BF)
+    grad_gate = ((down * xhat).astype(BF).astype(F32) * slope[:, 0:WIDTH]).astype(BF)
+    gp[:, 0:WIDTH] = grad_gate
+    gp_all[here, 0:WIDTH] = grad_gate
+    back = norm_back(xhat, rstd, down * gate)
+    cot[...] = jnp.where(keep, back * (1.0 / SEQ), 0.0).astype(BF)
     gwout[...] += dot_tn(seq_sum[...], go[...])
 
     def finish(value, rows, cols):
@@ -263,7 +241,6 @@
         ],
         scratch_shapes=[
             pltpu.VMEM((WIDTH, 5 * WIDTH), BF),
-            pltpu.VMEM((SEQ, WIDTH), F32),
             pltpu.VMEM((SEQ, 4 * WIDTH), F32),
             pltpu.VMEM((SEQ, 4 * WIDTH), BF),
             pltpu.VMEM((HEADS, SEQ, SEQ), BF),
@@ -282,27 +259,21 @@
     )(coords, lengths, normed, grad_out, turned, *pieces)
 
 
-def token_kernel(emb, go, gp, w, after, tokens, grads):
-    chunk = 64
-    grads[...] = dot_nn(gp[...], w[...])
-
-    @pl.loop(0, SEQ // chunk)
-    def _(i):
-        rows = pl.ds(pl.multiple_of(i * chunk, chunk), chunk)
-        xhat, rstd = normalise(emb[rows, :].astype(F32))
-        back = norm_back(xhat, rstd, grads[rows, :])
-        tokens[rows, :] = (back + go[rows, :].astype(F32)).astype(BF)
-
-
-def run_tokens(embedded, grad_out, grad_proj, w, after):
-    count = embedded.shape[0]
-
+def token_kernel(emb, go, gp, w, after, tokens, done):
+    grads = dot_nn(gp[...], w[...])
+    xhat, rstd = normalise(emb[...].astype(F32))
+    back = norm_back(xhat, rstd, grads)
+    tokens[...] = (back + go[...].astype(F32)).astype(BF)
+    done[...] = jnp.zeros_like(done)
+
+
+def run_tokens(embedded, grad_out, grad_proj, w, first, steps, after):
     def by_seq(cols):
-        return pl.BlockSpec((SEQ, cols), lambda i: (i, 0))
+        return pl.BlockSpec((SEQ, cols), lambda i: (i + first, 0))
 
     return pl.pallas_call(
         token_kernel,
-        grid=(count // SEQ,),
+        grid=(steps,),
         in_specs=[
             by_seq(WIDTH),
             by_seq(WIDTH),
@@ -310,24 +281,35 @@
             pl.BlockSpec((4 * WIDTH, WIDTH), lambda i: (0, 0)),
             pl.BlockSpec(memory_space=pl.ANY),
         ],
-        out_specs=by_seq(WIDTH),
-        out_shape=jax.ShapeDtypeStruct((count, WIDTH), BF),
-        scratch_shapes=[pltpu.VMEM((SEQ, WIDTH), F32)],
+        out_specs=[
+            pl.BlockSpec((SEQ, WIDTH), lambda i: (i, 0)),
+            pl.BlockSpec((8, 128), lambda i: (0, 0)),
+        ],
+        out_shape=[
+            jax.ShapeDtypeStruct((steps * SEQ, WIDTH), BF),
+            jax.ShapeDtypeStruct((8, 128), F32),
+        ],
         compiler_params=pltpu.CompilerParams(vmem_limit_bytes=56 * 1024 * 1024),
         cost_estimate=pl.CostEstimate(
-            flops=4_300_000_000, bytes_accessed=16_000_000, transcendentals=2048
+            flops=1_000_000_000, bytes_accessed=4_000_000, transcendentals=2048
         ),
         name="token_grads",
     )(embedded, grad_out, grad_proj, w, after)
 
 
-def bucket_kernel(bucket, labels, tokens, after, out):
-    owners, total = out.shape[1], tokens.shape[0]
-    tile = owners * CAP
-    slot = lax.broadcasted_iota(jnp.int32, (tile, total), 0) + pl.program_id(0) * tile
-    pick = jnp.where(slot == bucket[...], 1.0, 0.0).astype(BF)
-    sums = dot_nn(pick, tokens[...]).astype(BF)
-    marks = labels[...].astype(F32).astype(BF)
+def bucket_kernel(bucket, labels, early, late, after, out):
+    owners = out.shape[1]
+    tile, count = owners * CAP, early.shape[0]
+    slot = lax.broadcasted_iota(jnp.int32, (tile, count), 0) + pl.program_id(0) * tile
+
+    def pick(start):
+        return jnp.where(slot == bucket[:, start : start + count], 1.0, 0.0).astype(BF)
+
+    sums = (dot_nn(pick(0), early[...]) + dot_nn(pick(count), late[...])).astype(BF)
+    upper = lax.shift_right_logical(labels[...], 6)
+    lower = jnp.bitwise_and(labels[...], 63)
+    lane = lax.broadcasted_iota(jnp.int32, labels.shape, 1)
+    marks = jnp.where(lane < CAP, upper, pltpu.roll(lower, CAP, 1)).astype(F32).astype(BF)
     for part in range(out.shape[0]):
         for owner in range(owners):
             cols = slice(part * 128, (part + 1) * 128)
@@ -337,27 +319,29 @@
             )
 
 
-def run_buckets(bucket, labels, tokens, parts, after):
-    count, width = tokens.shape
+def run_buckets(bucket, labels, early, late, parts, after):
+    count, width = early.shape
     owners = labels.shape[0]
     per_step = 8
+    whole = pl.BlockSpec((count, width), lambda i: (0, 0))
     return pl.pallas_call(
         bucket_kernel,
         grid=(owners // per_step,),
         in_specs=[
-            pl.BlockSpec((1, count), lambda i: (0, 0)),
+            pl.BlockSpec((1, 2 * count), lambda i: (0, 0)),
             pl.BlockSpec((per_step, 128), lambda i: (i, 0)),
-            pl.BlockSpec((count, width), lambda i: (0, 0)),
+            whole,
+            whole,
             pl.BlockSpec(memory_space=pl.ANY),
         ],
         out_specs=pl.BlockSpec((parts, per_step, PACKET, 128), lambda i: (0, i, 0, 0)),
         out_shape=jax.ShapeDtypeStruct((parts, owners, PACKET, 128), BF),
         compiler_params=pltpu.CompilerParams(vmem_limit_bytes=56 * 1024 * 1024),
         cost_estimate=pl.CostEstimate(
-            flops=4_300_000_000, bytes_accessed=6_000_000, transcendentals=0
+            flops=200_000_000, bytes_accessed=1_000_000, transcendentals=0
         ),
         name="bucket_rows",
-    )(bucket, labels, tokens, after)
+    )(bucket, labels, early, late, after)
 
 
 def label_kernel(counts, offsets, rows, out):
@@ -368,9 +352,7 @@
         count, first = counts[owner], offsets[owner]
         for place in range(CAP):
             row = rows[jnp.minimum(first + place, last)]
-            row = jnp.where(place < count, row, ROWS_DEV)
-            out[owner, place] = lax.shift_right_logical(row, 6)
-            out[owner, CAP + place] = jnp.bitwise_and(row, 63)
+            out[owner, place] = jnp.where(place < count, row, ROWS_DEV)
 
 
 def run_labels(counts, offsets, rows):
@@ -385,69 +367,88 @@
     )(counts, offsets, rows)
 
 
-def scatter_kernel(rows, out, table, block, words, labels, sem):
+def scatter_kernel(first, last, rows, *refs):
+    if first:
+        even_in, odd_in, _, *refs = refs
+    if last:
+        out, token, even, odd, even_block, odd_block, words, labels, sem = refs
+    else:
+        even, odd, token, even_block, odd_block, words, labels, sem = refs
     batch = 16
     marks = rows[:, CAP, :].astype(F32)
     marks = marks * 64.0 + pltpu.roll(marks, CAP, 1)
     words[...] = marks.astype(jnp.int32)
     copy = pltpu.make_async_copy(words, labels, sem)
     copy.start()
-
-    @pl.loop(0, ROWS_DEV // 128)
-    def _(i):
-        table[pl.ds(pl.multiple_of(i * 128, 128), 128), :] = jnp.zeros((128, 128), F32)
-
-    table[ROWS_DEV : ROWS_DEV + 8, :] = jnp.zeros((8, 128), F32)
+    if first:
+        even[...] = even_in[...]
+        odd[...] = odd_in[...]
+    else:
+        even[...] = jnp.zeros_like(even)
+        odd[...] = jnp.zeros_like(odd)
     copy.wait()
 
-    @pl.loop(0, rows.shape[0])
-    def _(source):
-        block[...] = rows[source, 0:CAP, :].astype(F32)
+    @pl.loop(0, rows.shape[0] // 2)
+    def _(pair):
+        both = ((2 * pair, even, even_block), (2 * pair + 1, odd, odd_block))
+        for source, _, block in both:
+            block[...] = rows[source, 0:CAP, :].astype(F32)
 
         def add_batch(start):
-            places = range(start, start + batch)
-            wheres = [labels[source, p] for p in places]
-            sums = [
-                table[pl.ds(w, 1), :] + block[p : p + 1, :] for p, w in zip(places, wheres)
-            ]
-            for w, s in zip(wheres, sums):
-                table[pl.ds(w, 1), :] = s
+            todo = []
+            for source, table, block in both:
+                for place in range(start, start + batch):
+                    here = pl.ds(labels[source, place], 1)
+                    todo.append((table, here, table[here, :] + block[place : place + 1, :]))
+            for table, here, value in todo:
+                table[here, :] = value
 
         for start in range(0, CAP, batch):
-            pl.when(labels[source, start] != ROWS_DEV)(functools.partial(add_batch, start))
-
-    out[...] = table[0:ROWS_DEV, :]
-
-
-def run_scatter(rows):
-    sources, _, width = rows.shape
+            used = jnp.minimum(labels[2 * pair, start], labels[2 * pair + 1, start])
+            pl.when(used != ROWS_DEV)(functools.partial(add_batch, start))
+
+    if last:
+        out[...] = even[0:ROWS_DEV, :] + odd[0:ROWS_DEV, :]
+    token[...] = jnp.zeros_like(token)
+
+
+def run_scatter(rows, piece, pieces, tables=None, after=None):
+    sources, packet, width = rows.shape
+    count = sources // pieces
+    first, last = piece > 0, piece == pieces - 1
     whole = pl.BlockSpec(memory_space=pltpu.VMEM)
+    table = jax.ShapeDtypeStruct((ROWS_DEV + 8, width), F32)
+    scratch = [
+        pltpu.VMEM((CAP, width), F32),
+        pltpu.VMEM((CAP, width), F32),
+        pltpu.VMEM((count, 2 * CAP), jnp.int32),
+        pltpu.SMEM((count, 2 * CAP), jnp.int32),
+        pltpu.SemaphoreType.DMA,
+    ]
+    if last:
+        out_shape = [jax.ShapeDtypeStruct((ROWS_DEV, width), F32)]
+        scratch = [pltpu.VMEM(table.shape, F32), pltpu.VMEM(table.shape, F32)] + scratch
+    else:
+        out_shape = [table, table]
+    out_shape.append(jax.ShapeDtypeStruct((8, 128), F32))
     return pl.pallas_call(
-        scatter_kernel,
-        in_specs=[whole],
-        out_specs=whole,
-        out_shape=jax.ShapeDtypeStruct((ROWS_DEV, width), F32),
-        scratch_shapes=[
-            pltpu.VMEM((ROWS_DEV + 8, width), F32),
-            pltpu.VMEM((CAP, width), F32),
-            pltpu.VMEM((sources, 2 * CAP), jnp.int32),
-            pltpu.SMEM((sources, 2 * CAP), jnp.int32),
-            pltpu.SemaphoreType.DMA,
-        ],
-        compiler_params=pltpu.CompilerParams(vmem_limit_bytes=32 * 1024 * 1024),
+        functools.partial(scatter_kernel, first, last),
+        grid=(1,),
+        in_specs=[pl.BlockSpec((count, packet, width), lambda i: (piece, 0, 0))]
+        + ([whole, whole, pl.BlockSpec(memory_space=pl.ANY)] if first else []),
+        out_specs=[whole] * len(out_shape),
+        out_shape=out_shape,
+        scratch_shapes=scratch,
+        compiler_params=pltpu.CompilerParams(vmem_limit_bytes=24 * 1024 * 1024),
         cost_estimate=pl.CostEstimate(
             flops=2_000_000, bytes_accessed=6_000_000, transcendentals=0
         ),
         name="scatter",
-    )(rows)
+    )(rows, *((*tables, after) if first else ()))
 
 
 def ring(array, axis, size, shift):
     return lax.ppermute(array, axis, [(i, (i + shift) % size) for i in range(size)])
-
-
-def swap_cores(array, count):
-    return lax.ppermute(array, "table", [(i, i ^ 1) for i in range(count)])
 
 
 def table_ring(array, stride, size, shift, count):
@@ -458,7 +459,11 @@
     return lax.ppermute(array, "table", pairs)
 
 
-def small_kernel(body, name, coords, arrays, outs, after=(), through=()):
+def swap(array, bit, count):
+    return lax.ppermute(array, "table", [(i, i ^ bit) for i in range(count)])
+
+
+def small_kernel(body, name, coords, arrays, outs, after=(), through=(), limit=16):
     def kernel(place, *refs):
         first = len(arrays) + len(after) + len(through)
         body(place, *refs[: len(arrays)], *refs[first : first + len(outs)])
@@ -475,7 +480,7 @@
         input_output_aliases={
             1 + len(arrays) + len(after) + i: len(outs) + i for i in range(len(through))
         },
-        compiler_params=pltpu.CompilerParams(vmem_limit_bytes=16 * 1024 * 1024),
+        compiler_params=pltpu.CompilerParams(vmem_limit_bytes=limit * 1024 * 1024),
         cost_estimate=pl.CostEstimate(
             flops=1_000_000, bytes_accessed=2_000_000, transcendentals=0
         ),
@@ -494,55 +499,22 @@
     return value.astype(BF)
 
 
-def add_cores(coords, mine, theirs, far_a, far_b, right, left, own):
-    me, rows = coords[0], own.shape[0]
-    half = rows // 2
-    far = block_rows(me, 2, rows)
-    both = total(mine[far, :], theirs[far, :])
-    far_a[...] = both[:half]
-    far_b[...] = both[half:]
-    for out, offset in ((right, 1), (left, 3), (own, 0)):
-        part = block_rows(me, offset, rows)
+def add_cores(coords, mine, theirs, right, left, far, own, done):
+    done[...] = jnp.zeros_like(done)
+    rows = own.shape[0]
+    for out, offset in ((right, 1), (left, 3), (far, 2), (own, 0)):
+        part = block_rows(coords[0], offset, rows)
         out[...] = total(mine[part, :], theirs[part, :])
 
 
-def add_far(coords, right, left, from_left, from_right, to_right, to_left):
-    half = from_left.shape[0]
-    to_right[:half, :] = total(right[:half, :], from_left[...])
-    to_right[half:, :] = right[half:, :]
-    to_left[:half, :] = left[:half, :]
-    to_left[half:, :] = total(left[half:, :], from_right[...])
-
-
-def add_x(coords, own, from_left, from_right, scratch, right, left, far, mine):
-    scratch[...] = total(own[...], from_left[...], from_right[...])
+def add_x(coords, own, from_left, from_right, from_far, scratch, right, left, far, mine):
+    scratch[...] = total(own[...], from_left[...], from_right[...], from_far[...])
     for out, offset in ((right, 1), (left, 3), (far, 2), (mine, 0)):
         out[...] = scratch[block_rows(coords[2], offset, out.shape[0]), :]
 
 
-def quarter(place, offset, rows, cols):
-    index = lax.rem(place + offset, 4)
-    return (
-        pl.ds(pl.multiple_of(index // 2 * rows, rows), rows),
-        pl.ds(pl.multiple_of(lax.rem(index, 2) * cols, cols), cols),
-    )
-
-
-def add_y(coords, own, from_left, from_right, from_far, scratch, right, left, far, mine):
-    scratch[...] = total(own[...], from_left[...], from_right[...], from_far[...])
-    for out, offset in ((right, 1), (left, 3), (far, 2), (mine, 0)):
-        rows, cols = quarter(coords[3], offset, *out.shape)
-        out[...] = scratch[rows, cols]
-
-
-def add_z(coords, own, from_left, from_right, from_far, out):
-    out[...] = total(own[...], from_left[...], from_right[...], from_far[...])
-
-
-def join_z(coords, own, left, right, far, out):
-    for piece, offset in ((own, 0), (left, 3), (right, 1), (far, 2)):
-        rows, cols = quarter(coords[3], offset, *piece.shape)
-        out[rows, cols] = piece[...]
+def add_all(coords, *refs):
+    refs[-1][...] = total(*(ref[...] for ref in refs[:-1]))
 
 
 def join_y(coords, own, left, right, far, out):
@@ -567,10 +539,6 @@
     @pl.when(core == 1)
     def _():
         put(theirs, own)
-
-
-def three_ways(shift, right, left, far):
-    return shift(right, 1), shift(left, -1), shift(far, 2)
 
 
 def per_device(
@@ -589,8 +557,8 @@
     def along_y(array, shift):
         return table_ring(array, 8, 4, shift, table_count)
 
-    def along_z(array, shift):
-        return table_ring(array, 2, 4, shift, table_count)
+    def three_ways(along, right, left, far):
+        return along(right, 1), along(left, -1), along(far, 2)
 
     half = jnp.concatenate(
         [lax.dynamic_slice_in_dim(a, core * 64, 64, 0) for a in (w_in, w_out)], axis=1
@@ -602,7 +570,7 @@
     normed, turned = run_norm(embedded, labels)
     far_a, far_b, normed = lax.optimization_barrier((far_a, far_b, normed))
     low_o, high_o, far_ao, far_bo = (
-        swap_cores(a, table_count) for a in (low, high, far_a, far_b)
+        swap(a, 1, table_count) for a in (low, high, far_a, far_b)
     )
     pieces = [w_in, w_out, low, high, low_o, high_o, far_a, far_b, far_ao, far_bo]
 
@@ -615,79 +583,62 @@
         coords, lengths, normed, turned, grad_out, pieces
     )
 
-    theirs = swap_cores(other, table_count)
-    tokens = run_tokens(embedded, grad_out, grad_proj, w_full, other)
+    theirs = swap(other, 1, table_count)
+    half = embedded.shape[0] // SEQ // 2
+    early, done = run_tokens(embedded, grad_out, grad_proj, w_full, 0, half, other)
 
     rows, cols = mine.shape
-    block, part = rows // 4, rows // 16
-    far_a, far_b, right, left, own = small_kernel(
+    block = rows // 4
+    mark = ((8, 128), F32)
+    right, left, far, own, done = small_kernel(
         add_cores,
         "add_cores",
         coords,
         (mine, theirs),
-        [((block // 2, cols), BF)] * 2 + [((block, cols), BF)] * 3,
-        after=(tokens,),
-    )
-    from_left, from_right = along_x(far_a, 1), along_x(far_b, -1)
-    bucket_rows = run_buckets(bucket, labels, tokens, fsdp_count, own)
-    to_right, to_left, bucket_rows = small_kernel(
-        add_far,
-        "add_far",
-        coords,
-        (right, left, from_left, from_right),
-        [((block, cols), BF)] * 2,
-        through=(bucket_rows,),
-    )
-    from_left, from_right = along_x(to_right, 1), along_x(to_left, -1)
-
-    values = bucket_rows.reshape(fsdp_count * table_count, PACKET, 128)
-    got = lax.all_to_all(values, BOTH, split_axis=0, concat_axis=0, tiled=True)
-
-    _, right, left, far, own = small_kernel(
+        [((block, cols), BF)] * 4 + [mark],
+        after=(done,),
+    )
+    from_x = three_ways(along_x, right, left, far)
+    late, done = run_tokens(embedded, grad_out, grad_proj, w_full, half, half, done)
+    bucket_rows = run_buckets(bucket, labels, early, late, fsdp_count, done)
+    part = block // 4
+    _, right, left, far, own, bucket_rows = small_kernel(
         add_x,
         "add_x",
         coords,
-        (own, from_left, from_right),
+        (own, *from_x),
         [((block, cols), BF)] + [((part, cols), BF)] * 4,
-    )
-    _, right, left, far, own = small_kernel(
-        add_y,
-        "add_y",
-        coords,
-        (own, *three_ways(along_y, right, left, far)),
-        [((part, cols), BF)] + [((part // 2, cols // 2), BF)] * 4,
-    )
+        through=(bucket_rows,),
+        limit=58,
+    )
+    from_y = three_ways(along_y, right, left, far)
+    one = [((part, cols), BF)]
+    values = bucket_rows.reshape(fsdp_count * table_count, PACKET, 128)
+    got = lax.all_to_all(values, BOTH, split_axis=0, concat_axis=0, tiled=True)
+
+    (own,) = small_kernel(add_all, "add_y", coords, (own, *from_y), one)
+    from_z = swap(own, 2, table_count)
+    *tables, token = run_scatter(got, 0, 4)
+    (own,) = small_kernel(add_all, "add_z_low", coords, (own, from_z), one, after=(token,))
+    from_z = swap(own, 4, table_count)
+    *tables, token = run_scatter(got, 1, 4, tables, own)
+    (own,) = small_kernel(add_all, "add_z_high", coords, (own, from_z), one, after=(token,))
+    from_y = three_ways(along_y, own, own, own)
+    *tables, token = run_scatter(got, 2, 4, tables, own)
     (own,) = small_kernel(
-        add_z,
-        "add_z",
-        coords,
-        (own, *three_ways(along_z, right, left, far)),
-        [((part // 2, cols // 2), BF)],
-    )
-    (own,) = small_kernel(
-        join_z,
-        "join_z",
-        coords,
-        (own, *three_ways(along_z, own, own, own)),
-        [((part, cols), BF)],
-    )
-    (own,) = small_kernel(
-        join_y,
-        "join_y",
-        coords,
-        (own, *three_ways(along_y, own, own, own)),
-        [((block, cols), BF)],
-    )
+        join_y, "join_y", coords, (own, *from_y), [((block, cols), BF)], after=(token,)
+    )
+    theirs = swap(own, 1, table_count)
+    (grad_table, token) = run_scatter(got, 3, 4, tables, own)
     factor = 1.0 / math.sqrt(embedded.shape[0] * fsdp_count * table_count)
     share_in, share_out = small_kernel(
         functools.partial(join_cores, factor),
         "join_cores",
         coords,
-        (own, swap_cores(own, table_count)),
+        (own, theirs),
         [((block, 4 * WIDTH), F32), ((block, WIDTH), F32)],
-    )
-
-    grad_table = run_scatter(got)
+        after=(token,),
+    )
     return (share_in, share_out, grad_table)
 
 

time: 227 us -> 171 us (0.75)
  Pallas kernels: 120 us -> 94.1 us
  waiting for transfers between devices: 48.8 us -> 32.8 us
  starting transfers between devices: 45.4 us -> 35.8 us
  local copies, waits for them, and re-layouts: 8.1 us -> 5.49 us
    ppermute x8 -> x7, waiting for transfers between devices: 32.4 us -> 3.2 us  [ring(): lax.ppermute(array, axis, [(i, (i + shift) % size) for i in range(size)])]
    pallas_call x1, Pallas kernels: 54.4 us -> 39.2 us  [run_layer(): pl.pallas_call(layer_kernel, grid=(tokens // SEQ,), in_specs=[smem, smem,...]
    ppermute x12 -> x6, waiting for transfers between devices: 14.4 us -> 28.9 us  [table_ring(): return lax.ppermute(array, 'table', pairs)]
    ppermute x12 -> x6, starting transfers between devices: 14.9 us -> 7.18 us  [table_ring(): return lax.ppermute(array, 'table', pairs)]
    pallas_call x2 -> x6, Pallas kernels: 34.2 us -> 29.4 us  [the longest x4 15.7 us: run_scatter(): pl.pallas_call(functools.partial(scatter_kernel, first, last), grid=(1,),...]
    pallas_call x1, Pallas kernels: 8.52 us -> 4.81 us  [run_norm(): pl.pallas_call(norm_kernel, grid=(tokens // SEQ,), in_specs=[pl.BlockSpec...]
    unnamed x36 -> x48, local copies, waits for them, and re-layouts: 6.25 us -> 3.64 us
    ppermute x8 -> x7, starting transfers between devices: 10.5 us -> 8.38 us  [ring(): lax.ppermute(array, axis, [(i, (i + shift) % size) for i in range(size)])]
  transfers between devices with their start and end apart: 27 -> 22, of which waited for: 11 -> 7; matrix products, arithmetic and copies ran while one was open for 1% -> 1% of each run, Pallas kernels for 21% -> 28%
where the time goes in v2:
time: 171 us
  Pallas kernels  94.1 us (55%)
  starting transfers between devices  35.8 us (21%)
  waiting for transfers between devices  32.8 us (19%)
  local copies, waits for them, and re-layouts  5.49 us (3%)
    pallas_call x1, Pallas kernels, run_layer(): pl.pallas_call(layer_kernel, grid=(tokens // SEQ,), in_specs=[smem, smem,...  39.2 us
    ppermute x6, waiting for transfers between devices, table_ring(): return lax.ppermute(array, 'table', pairs)  28.9 us
    pallas_call x4, Pallas kernels, run_scatter(): pl.pallas_call(functools.partial(scatter_kernel, first, last), grid=(1,),...  15.7 us
    pallas_call x2, Pallas kernels, run_tokens(): pl.pallas_call(token_kernel, grid=(steps,), in_specs=[by_seq(WIDTH), by_s...  13.7 us
    ppermute x8, starting transfers between devices, swap(): return lax.ppermute(array, 'table', [(i, i ^ bit) for i in range(count)])  11 us
    all_to_all x1, starting transfers between devices, per_device(): got = lax.all_to_all(values, BOTH, split_axis=0, concat_axis=0, tiled=True)  9.21 us
    ppermute x7, starting transfers between devices, ring(): lax.ppermute(array, axis, [(i, (i + shift) % size) for i in range(size)])  8.38 us
    pallas_call x1, Pallas kernels, run_buckets(): pl.pallas_call(bucket_kernel, grid=(owners // per_step,), in_specs=[pl.Bl...  7.45 us
  transfers between devices with their start and end apart: 22, of which 7 were waited for; matrix products, arithmetic and copies ran while one was open for 1% of the time, Pallas kernels for 28%

profile of v2, /device:TPU:1, one launch (start us, length us, event | category | flops | bytes accessed | tf_op | source)
XLA Modules:
  0.0 170.5 jit_solution(10604946438712673552)
XLA Ops:
  2.5 2.1 %collective-permute-start = (bf16[64,2560]{1,0:T(8,128)(2,1)S(1)}, bf16[64,2560]{1,0:T(8,128)(2,1)S(1)}, u32[]{:S(2)}, u32[]{:S(2)}) collective-permute-start(bf16[64,2560]{1,0:T(8,128)(2,1)S(1)} %pad_maximum_fusion), channel_id=1, source_target_pairs={{0,32},{32,64},{64,96},{96,0},{1,33},{33,65},{65,97},{97,1},{2,34}... | collective-permute-start | bytes 983048 | tf_op jit(solution)/shard_map/ppermute | solution.py:451
  6.0 6.0 %labels.1.after = s32[32,128]{1,0:T(8,128)} custom-call(s32[32]{0:T(128)} %bitcast.14, s32[32]{0:T(128)} %bitcast.15, s32[1614]{0:T(1024)} %rows.1), custom_call_target="tpu_custom_call" | custom-call | flops 10000 | bytes 10000 | tf_op jit(solution)/shard_map/labels/pallas_call | solution.py:360
  14.2 1.5 collective-permute-start.3
  15.7 2.4 %collective-permute-start.4 = (bf16[64,2560]{1,0:T(8,128)(2,1)S(1)}, bf16[64,2560]{1,0:T(8,128)(2,1)S(1)}, u32[]{:S(2)}, u32[]{:S(2)}) collective-permute-start(bf16[64,2560]{1,0:T(8,128)(2,1)S(1)} %collective-permute-done.low), channel_id=1, source_target_pairs={{0,1},{1,0},{2,3},{3,2},{4,5},{5,4},{6,7},{7,6},{8,9},{9,8},{10,11... | collective-permute-start | bytes 983048 | tf_op jit(solution)/shard_map/ppermute | solution.py:463
  18.1 4.8 %norm.1 = (bf16[2048,512]{1,0:T(8,128)(2,1)}, bf16[512,2048]{1,0:T(8,128)(2,1)}) custom-call(bf16[2048,512]{1,0:T(8,128)(2,1)} %emb.5, s32[32,128]{1,0:T(8,128)} %labels.1.after), custom_call_target="tpu_custom_call" | custom-call | flops 20000000 | bytes 6000000 | tf_op jit(solution)/shard_map/norm/pallas_call | solution.py:59
  25.9 39.2 %layer.1 = (bf16[2048,2048]{1,0:T(8,128)(2,1)}, bf16[512,1280]{1,0:T(8,128)(2,1)}, bf16[512,1280]{1,0:T(8,128)(2,1)}, bf16[2048,512]{1,0:T(8,128)(2,1)}) custom-call(s32[4]{0:T(128)} %pad_add_fusion.coords.place, s32[4]{0:T(128)} %lens.1, bf16[2048,512]{1,0:T(8,128)(2,1)} %get-tuple-element.46.normed, bf16[2048,512]{1,0:T(8,128)(2,1)} %go.5, ...), custom_call_target="tpu_custom_call" | custom-call | flops 20000000000 | bytes 20000000 | tf_op jit(solution)/shard_map/layer/pallas_call | solution.py:225
  65.5 6.9 %token_grads.2 = (bf16[1024,512]{1,0:T(8,128)(2,1)}, f32[8,128]{1,0:T(8,128)}) custom-call(bf16[2048,512]{1,0:T(8,128)(2,1)} %emb.5, bf16[2048,512]{1,0:T(8,128)(2,1)} %go.5, bf16[2048,2048]{1,0:T(8,128)(2,1)} %get-tuple-element.52.gp, bf16[2048,512]{1,0:T(8,128)(2,1)} %get-tuple-element.53.w, bf16[512,1280]{1,0:T(8,128)(2,1)} %get-tuple-element.51.after), custom_call_target="tpu_custom_call" | custom-call | flops 1000000000 | bytes 4000000 | tf_op jit(solution)/shard_map/token_grads/pallas_call | solution.py:274
  78.3 6.8 %token_grads.3 = (bf16[1024,512]{1,0:T(8,128)(2,1)}, f32[8,128]{1,0:T(8,128)}) custom-call(bf16[2048,512]{1,0:T(8,128)(2,1)} %emb.5, bf16[2048,512]{1,0:T(8,128)(2,1)} %go.5, bf16[2048,2048]{1,0:T(8,128)(2,1)} %get-tuple-element.52.gp, bf16[2048,512]{1,0:T(8,128)(2,1)} %get-tuple-element.53.w, f32[8,128]{1,0:T(8,128)} %copy-done.6), custom_call_target="tpu_custom_call" | custom-call | flops 1000000000 | bytes 4000000 | tf_op jit(solution)/shard_map/token_grads/pallas_call | solution.py:274
  85.1 7.5 %bucket_rows.1.refs_4_ = bf16[4,32,72,128]{3,2,1,0:T(8,128)(2,1)} custom-call(s32[1,2048]{1,0:T(1,128)} %bitcast.13, s32[32,128]{1,0:T(8,128)} %labels.1.after, bf16[1024,512]{1,0:T(8,128)(2,1)} %get-tuple-element.59.early, bf16[1024,512]{1,0:T(8,128)(2,1)} %get-tuple-element.61.late, f32[8,128]{1,0:T(8,128)} %get-tuple-element.62.after), custom_call_target="tpu_custom_call" | custom-call | flops 200000000 | bytes 1000000 | tf_op jit(solution)/shard_map/bucket_rows/pallas_call | solution.py:327
  92.6 2.3 %collective-permute-done.9.refs_1_ = bf16[128,1280]{1,0:T(8,128)(2,1)S(1)} collective-permute-done((bf16[128,1280]{1,0:T(8,128)(2,1)S(1)}, bf16[128,1280]{1,0:T(8,128)(2,1)S(1)}, u32[]{:S(2)}, u32[]{:S(2)}) %collective-permute-start.9) | collective-permute-done | bytes 327712 | tf_op jit(solution)/shard_map/ppermute | solution.py:451
  95.6 2.4 %add_x.1 = (bf16[128,1280]{1,0:T(8,128)(2,1)}, bf16[32,1280]{1,0:T(8,128)(2,1)}, bf16[32,1280]{1,0:T(8,128)(2,1)}, bf16[32,1280]{1,0:T(8,128)(2,1)}, bf16[32,128...) custom-call(s32[4]{0:T(128)} %pad_add_fusion.coords.place, ...), custom_call_target="tpu_custom_call", output_to_operand_aliasing={{5}: (5, {})} | custom-call | flops 1000000 | bytes 2000000 | tf_op jit(solution)/shard_map/add_x/pallas_call | solution.py:472
  98.0 9.2 %all-to-all-start = ((bf16[128,72,128]{2,1,0:T(8,128)(2,1)}), bf16[128,72,128]{2,1,0:T(8,128)(2,1)S(1)}, u32[]{:S(2)}, u32[]{:S(2)}) async-start(bf16[128,72,128]{2,1,0:T(8,128)(2,1)} %bitcast.12), calls=%async_computation | async-start | bytes 4718592 | tf_op jit(solution)/shard_map/all_to_all | solution.py:617
  107.2 1.5 collective-permute-start.12
  110.0 1.6 collective-permute-start.14
  111.7 22.3 %collective-permute-done.12.refs_1_ = bf16[32,1280]{1,0:T(8,128)(2,1)S(1)} collective-permute-done((bf16[32,1280]{1,0:T(8,128)(2,1)S(1)}, bf16[32,1280]{1,0:T(8,128)(2,1)S(1)}, u32[]{:S(2)}, u32[]{:S(2)}) %collective-permute-start.12) | collective-permute-done | bytes 81952 | tf_op jit(solution)/shard_map/ppermute | solution.py:459
  134.0 5.2 %collective-permute-done.14.refs_3_ = bf16[32,1280]{1,0:T(8,128)(2,1)S(1)} collective-permute-done((bf16[32,1280]{1,0:T(8,128)(2,1)S(1)}, bf16[32,1280]{1,0:T(8,128)(2,1)S(1)}, u32[]{:S(2)}, u32[]{:S(2)}) %collective-permute-start.14) | collective-permute-done | bytes 81952 | tf_op jit(solution)/shard_map/ppermute | solution.py:459
  141.1 3.6 %scatter.4 = (f32[4104,128]{1,0:T(8,128)S(1)}, f32[4104,128]{1,0:T(8,128)S(1)}, f32[8,128]{1,0:T(8,128)S(1)}) custom-call(bf16[128,72,128]{2,1,0:T(8,128)(2,1)S(1)} %all-to-all-done.rows), custom_call_target="tpu_custom_call" | custom-call | flops 2000000 | bytes 6000000 | tf_op jit(solution)/shard_map/scatter/pallas_call | solution.py:434
  145.3 3.0 %collective-permute-start.16 = (bf16[32,1280]{1,0:T(8,128)(2,1)S(1)}, bf16[32,1280]{1,0:T(8,128)(2,1)S(1)}, u32[]{:S(2)}, u32[]{:S(2)}) collective-permute-start(bf16[32,1280]{1,0:T(8,128)(2,1)S(1)} %add_z_low.1.refs_2_.refs_0_), channel_id=1, source_target_pairs={{0,4},{1,5},{2,6},{3,7},{4,0},{5,1},{6,2},{7,3},{8,12},{9,13},{10,... | collective-permute-start | bytes 245768 | tf_op jit(solution)/shard_map/ppermute | solution.py:463
  148.3 3.5 %scatter.5 = (f32[4104,128]{1,0:T(8,128)S(1)}, f32[4104,128]{1,0:T(8,128)S(1)}, f32[8,128]{1,0:T(8,128)S(1)}) custom-call(bf16[128,72,128]{2,1,0:T(8,128)(2,1)S(1)} %all-to-all-done.rows, f32[4104,128]{1,0:T(8,128)S(1)} %get-tuple-element.69.refs_0_, f32[4104,128]{1,0:T(8,128)S(1)} %get-tuple-element.70.refs_1_, bf16[32,1280]{1,0:T(8,128)(2,1)S(1)} %add_z_low.1.refs_2_.refs_0_), custom_call_target="tpu_custom_call" | custom-call | flops 2000000 | bytes 6000000 | tf_op jit(solution)/shard_map/scatter/pallas_call | solution.py:434
  152.6 2.5 %collective-permute-start.18 = (bf16[32,1280]{1,0:T(8,128)(2,1)S(1)}, bf16[32,1280]{1,0:T(8,128)(2,1)S(1)}, u32[]{:S(2)}, u32[]{:S(2)}) collective-permute-start(bf16[32,1280]{1,0:T(8,128)(2,1)S(1)} %add_z_high.1.refs_2_.refs_0_), channel_id=1, source_target_pairs={{0,24},{1,25},{2,26},{3,27},{4,28},{5,29},{6,30},{7,31},{8,0},{9,1... | collective-permute-start | bytes 245768 | tf_op jit(solution)/shard_map/ppermute | solution.py:459
  155.2 3.4 %scatter.6 = (f32[4104,128]{1,0:T(8,128)S(1)}, f32[4104,128]{1,0:T(8,128)S(1)}, f32[8,128]{1,0:T(8,128)S(1)}) custom-call(bf16[128,72,128]{2,1,0:T(8,128)(2,1)S(1)} %all-to-all-done.rows, f32[4104,128]{1,0:T(8,128)S(1)} %get-tuple-element.72.refs_0_, f32[4104,128]{1,0:T(8,128)S(1)} %get-tuple-element.73.refs_1_, bf16[32,1280]{1,0:T(8,128)(2,1)S(1)} %add_z_high.1.refs_2_.refs_0_), custom_call_target="tpu_custom_call" | custom-call | flops 2000000 | bytes 6000000 | tf_op jit(solution)/shard_map/scatter/pallas_call | solution.py:434
  160.6 3.1 %collective-permute-start.20 = (bf16[128,1280]{1,0:T(8,128)(2,1)S(1)}, bf16[128,1280]{1,0:T(8,128)(2,1)S(1)}, u32[]{:S(2)}, u32[]{:S(2)}) collective-permute-start(bf16[128,1280]{1,0:T(8,128)(2,1)S(1)} %join_y.1.refs_2_.refs_0_), channel_id=1, source_target_pairs={{0,1},{1,0},{2,3},{3,2},{4,5},{5,4},{6,7},{7,6},{8,9},{9,8},{10,11... | collective-permute-start | bytes 983048 | tf_op jit(solution)/shard_map/ppermute | solution.py:463
  163.6 5.2 %scatter.7 = (f32[4096,128]{1,0:T(8,128)}, f32[8,128]{1,0:T(8,128)S(1)}) custom-call(bf16[128,72,128]{2,1,0:T(8,128)(2,1)S(1)} %all-to-all-done.rows, f32[4104,128]{1,0:T(8,128)S(1)} %get-tuple-element.75.refs_0_, f32[4104,128]{1,0:T(8,128)S(1)} %get-tuple-element.76.refs_1_, bf16[128,1280]{1,0:T(8,128)(2,1)S(1)} %join_y.1.refs_2_.refs_0_), custom_call_target="tpu_custom_call" | custom-call | flops 2000000 | bytes 6000000 | tf_op jit(solution)/shard_map/scatter/pallas_call | solution.py:434
  168.9 1.7 join_cores.1
  (94 shorter events, 21.8 us)
Async XLA Ops:
  2.5 10.4 %collective-permute-start = (bf16[64,2560]{1,0:T(8,128)(2,1)S(1)}, bf16[64,2560]{1,0:T(8,128)(2,1)S(1)}, u32[]{:S(2)}, u32[]{:S(2)}) collective-permute-start(bf16[64,2560]{1,0:T(8,128)(2,1)S(1)} %pad_maximum_fusion), channel_id=1, source_target_pairs={{0,32},{32,64},{64,96},{96,0},{1,33},{33,65},{65,97},{97,1},{2,34}... | collective-permute-start | bytes 983048 | tf_op jit(solution)/shard_map/ppermute | solution.py:451
  4.6 8.3 %collective-permute-start.1 = (bf16[64,2560]{1,0:T(8,128)(2,1)S(1)}, bf16[64,2560]{1,0:T(8,128)(2,1)S(1)}, u32[]{:S(2)}, u32[]{:S(2)}) collective-permute-start(bf16[64,2560]{1,0:T(8,128)(2,1)S(1)} %pad_maximum_fusion), channel_id=1, source_target_pairs={{0,96},{32,0},{64,32},{96,64},{1,97},{33,1},{65,33},{97,65},{2,98}... | collective-permute-start | bytes 983048 | tf_op jit(solution)/shard_map/ppermute | solution.py:451
  12.9 10.1 %collective-permute-start.2 = (bf16[32,2560]{1,0:T(8,128)(2,1)S(1)}, bf16[32,2560]{1,0:T(8,128)(2,1)S(1)}, u32[]{:S(2)}, u32[]{:S(2)}) collective-permute-start(bf16[32,2560]{1,0:T(8,128)(2,1)S(1)} %slice.14), channel_id=1, source_target_pairs={{0,32},{32,64},{64,96},{96,0},{1,33},{33,65},{65,97},{97,1},{2,34}... | collective-permute-start | bytes 491528 | tf_op jit(solution)/shard_map/ppermute | solution.py:451
  14.2 8.8 %collective-permute-start.3 = (bf16[32,2560]{1,0:T(8,128)(2,1)S(1)}, bf16[32,2560]{1,0:T(8,128)(2,1)S(1)}, u32[]{:S(2)}, u32[]{:S(2)}) collective-permute-start(bf16[32,2560]{1,0:T(8,128)(2,1)S(1)} %slice.15), channel_id=1, source_target_pairs={{0,96},{32,0},{64,32},{96,64},{1,97},{33,1},{65,33},{97,65},{2,98}... | collective-permute-start | bytes 491528 | tf_op jit(solution)/shard_map/ppermute | solution.py:451
  15.7 9.2 %collective-permute-start.4 = (bf16[64,2560]{1,0:T(8,128)(2,1)S(1)}, bf16[64,2560]{1,0:T(8,128)(2,1)S(1)}, u32[]{:S(2)}, u32[]{:S(2)}) collective-permute-start(bf16[64,2560]{1,0:T(8,128)(2,1)S(1)} %collective-permute-done.low), channel_id=1, source_target_pairs={{0,1},{1,0},{2,3},{3,2},{4,5},{5,4},{6,7},{7,6},{8,9},{9,8},{10,11... | collective-permute-start | bytes 983048 | tf_op jit(solution)/shard_map/ppermute | solution.py:463
  18.1 6.8 %collective-permute-start.5 = (bf16[64,2560]{1,0:T(8,128)(2,1)S(1)}, bf16[64,2560]{1,0:T(8,128)(2,1)S(1)}, u32[]{:S(2)}, u32[]{:S(2)}) collective-permute-start(bf16[64,2560]{1,0:T(8,128)(2,1)S(1)} %collective-permute-done.1.high), channel_id=1, source_target_pairs={{0,1},{1,0},{2,3},{3,2},{4,5},{5,4},{6,7},{7,6},{8,9},{9,8},{10,11... | collective-permute-start | bytes 983048 | tf_op jit(solution)/shard_map/ppermute | solution.py:463
  23.0 1.6 collective-permute-start.6
  23.6 1.4 collective-permute-start.7
  65.0 7.4 %collective-permute-start.8 = (bf16[512,1280]{1,0:T(8,128)(2,1)}, bf16[512,1280]{1,0:T(8,128)(2,1)S(1)}, u32[]{:S(2)}, u32[]{:S(2)}) collective-permute-start(bf16[512,1280]{1,0:T(8,128)(2,1)} %get-tuple-element.51.after), channel_id=1, source_target_pairs={{0,1},{1,0},{2,3},{3,2},{4,5},{5,4},{6,7},{7,6},{8,9},{9,8},{10,11... | collective-permute-start | bytes 3932168 | tf_op jit(solution)/shard_map/ppermute | solution.py:463
  75.4 17.2 %collective-permute-start.10 = (bf16[128,1280]{1,0:T(8,128)(2,1)S(1)}, bf16[128,1280]{1,0:T(8,128)(2,1)S(1)}, u32[]{:S(2)}, u32[]{:S(2)}) collective-permute-start(bf16[128,1280]{1,0:T(8,128)(2,1)S(1)} %get-tuple-element.57), channel_id=1, source_target_pairs={{0,96},{32,0},{64,32},{96,64},{1,97},{33,1},{65,33},{97,65},{2,98}... | collective-permute-start | bytes 983048 | tf_op jit(solution)/shard_map/ppermute | solution.py:451
  76.7 15.8 %collective-permute-start.11 = (bf16[128,1280]{1,0:T(8,128)(2,1)S(1)}, bf16[128,1280]{1,0:T(8,128)(2,1)S(1)}, u32[]{:S(2)}, u32[]{:S(2)}) collective-permute-start(bf16[128,1280]{1,0:T(8,128)(2,1)S(1)} %get-tuple-element.58), channel_id=1, source_target_pairs={{0,64},{32,96},{64,0},{96,32},{1,65},{33,97},{65,1},{97,33},{2,66}... | collective-permute-start | bytes 983048 | tf_op jit(solution)/shard_map/ppermute | solution.py:451
  77.2 17.7 %collective-permute-start.9 = (bf16[128,1280]{1,0:T(8,128)(2,1)S(1)}, bf16[128,1280]{1,0:T(8,128)(2,1)S(1)}, u32[]{:S(2)}, u32[]{:S(2)}) collective-permute-start(bf16[128,1280]{1,0:T(8,128)(2,1)S(1)} %get-tuple-element.56), channel_id=1, source_target_pairs={{0,32},{32,64},{64,96},{96,0},{1,33},{33,65},{65,97},{97,1},{2,34}... | collective-permute-start | bytes 983048 | tf_op jit(solution)/shard_map/ppermute | solution.py:451
  98.0 41.2 %copy-start.2 = (bf16[32,1280]{1,0:T(8,128)(2,1)S(1)}, bf16[32,1280]{1,0:T(8,128)(2,1)}, u32[]{:S(2)}) copy-start(bf16[32,1280]{1,0:T(8,128)(2,1)} %get-tuple-element.63.refs_0_) | copy-start | bytes 245764
  98.0 41.2 %copy-start.4 = (s32[4]{0:T(128)S(1)}, s32[4]{0:T(128)}, u32[]{:S(2)}) copy-start(s32[4]{0:T(128)} %pad_add_fusion.coords.place) | copy-start | bytes 52
  98.0 43.1 %all-to-all-start = ((bf16[128,72,128]{2,1,0:T(8,128)(2,1)}), bf16[128,72,128]{2,1,0:T(8,128)(2,1)S(1)}, u32[]{:S(2)}, u32[]{:S(2)}) async-start(bf16[128,72,128]{2,1,0:T(8,128)(2,1)} %bitcast.12), calls=%async_computation | async-start | bytes 4718592 | tf_op jit(solution)/shard_map/all_to_all | solution.py:617
  107.2 26.8 %collective-permute-start.12 = (bf16[32,1280]{1,0:T(8,128)(2,1)S(1)}, bf16[32,1280]{1,0:T(8,128)(2,1)S(1)}, u32[]{:S(2)}, u32[]{:S(2)}) collective-permute-start(bf16[32,1280]{1,0:T(8,128)(2,1)S(1)} %copy-done.23), channel_id=1, source_target_pairs={{0,8},{1,9},{2,10},{3,11},{4,12},{5,13},{6,14},{7,15},{8,16},{9,17... | collective-permute-start | bytes 245768 | tf_op jit(solution)/shard_map/ppermute | solution.py:459
  108.7 25.3 %collective-permute-start.13 = (bf16[32,1280]{1,0:T(8,128)(2,1)S(1)}, bf16[32,1280]{1,0:T(8,128)(2,1)S(1)}, u32[]{:S(2)}, u32[]{:S(2)}) collective-permute-start(bf16[32,1280]{1,0:T(8,128)(2,1)S(1)} %copy-done.22), channel_id=1, source_target_pairs={{0,24},{1,25},{2,26},{3,27},{4,28},{5,29},{6,30},{7,31},{8,0},{9,1... | collective-permute-start | bytes 245768 | tf_op jit(solution)/shard_map/ppermute | solution.py:459
  110.0 29.2 %collective-permute-start.14 = (bf16[32,1280]{1,0:T(8,128)(2,1)S(1)}, bf16[32,1280]{1,0:T(8,128)(2,1)S(1)}, u32[]{:S(2)}, u32[]{:S(2)}) collective-permute-start(bf16[32,1280]{1,0:T(8,128)(2,1)S(1)} %copy-done.21), channel_id=1, source_target_pairs={{0,16},{1,17},{2,18},{3,19},{4,20},{5,21},{6,22},{7,23},{8,24},{9,... | collective-permute-start | bytes 245768 | tf_op jit(solution)/shard_map/ppermute | solution.py:459
  139.8 4.9 %collective-permute-start.15 = (bf16[32,1280]{1,0:T(8,128)(2,1)S(1)}, bf16[32,1280]{1,0:T(8,128)(2,1)S(1)}, u32[]{:S(2)}, u32[]{:S(2)}) collective-permute-start(bf16[32,1280]{1,0:T(8,128)(2,1)S(1)} %add_y.1.refs_0_), channel_id=1, source_target_pairs={{0,2},{1,3},{2,0},{3,1},{4,6},{5,7},{6,4},{7,5},{8,10},{9,11},{10,... | collective-permute-start | bytes 245768 | tf_op jit(solution)/shard_map/ppermute | solution.py:463
  145.3 6.5 %collective-permute-start.16 = (bf16[32,1280]{1,0:T(8,128)(2,1)S(1)}, bf16[32,1280]{1,0:T(8,128)(2,1)S(1)}, u32[]{:S(2)}, u32[]{:S(2)}) collective-permute-start(bf16[32,1280]{1,0:T(8,128)(2,1)S(1)} %add_z_low.1.refs_2_.refs_0_), channel_id=1, source_target_pairs={{0,4},{1,5},{2,6},{3,7},{4,0},{5,1},{6,2},{7,3},{8,12},{9,13},{10,... | collective-permute-start | bytes 245768 | tf_op jit(solution)/shard_map/ppermute | solution.py:463
  152.4 6.1 %collective-permute-start.17 = (bf16[32,1280]{1,0:T(8,128)(2,1)S(1)}, bf16[32,1280]{1,0:T(8,128)(2,1)S(1)}, u32[]{:S(2)}, u32[]{:S(2)}) collective-permute-start(bf16[32,1280]{1,0:T(8,128)(2,1)S(1)} %add_z_high.1.refs_2_.refs_0_), channel_id=1, source_target_pairs={{0,8},{1,9},{2,10},{3,11},{4,12},{5,13},{6,14},{7,15},{8,16},{9,17... | collective-permute-start | bytes 245768 | tf_op jit(solution)/shard_map/ppermute | solution.py:459
  152.6 5.9 %collective-permute-start.18 = (bf16[32,1280]{1,0:T(8,128)(2,1)S(1)}, bf16[32,1280]{1,0:T(8,128)(2,1)S(1)}, u32[]{:S(2)}, u32[]{:S(2)}) collective-permute-start(bf16[32,1280]{1,0:T(8,128)(2,1)S(1)} %add_z_high.1.refs_2_.refs_0_), channel_id=1, source_target_pairs={{0,24},{1,25},{2,26},{3,27},{4,28},{5,29},{6,30},{7,31},{8,0},{9,1... | collective-permute-start | bytes 245768 | tf_op jit(solution)/shard_map/ppermute | solution.py:459
  155.2 4.8 %collective-permute-start.19 = (bf16[32,1280]{1,0:T(8,128)(2,1)S(1)}, bf16[32,1280]{1,0:T(8,128)(2,1)S(1)}, u32[]{:S(2)}, u32[]{:S(2)}) collective-permute-start(bf16[32,1280]{1,0:T(8,128)(2,1)S(1)} %add_z_high.1.refs_2_.refs_0_), channel_id=1, source_target_pairs={{0,16},{1,17},{2,18},{3,19},{4,20},{5,21},{6,22},{7,23},{8,24},{9,... | collective-permute-start | bytes 245768 | tf_op jit(solution)/shard_map/ppermute | solution.py:459
  160.6 8.3 %collective-permute-start.20 = (bf16[128,1280]{1,0:T(8,128)(2,1)S(1)}, bf16[128,1280]{1,0:T(8,128)(2,1)S(1)}, u32[]{:S(2)}, u32[]{:S(2)}) collective-permute-start(bf16[128,1280]{1,0:T(8,128)(2,1)S(1)} %join_y.1.refs_2_.refs_0_), channel_id=1, source_target_pairs={{0,1},{1,0},{2,3},{3,2},{4,5},{5,4},{6,7},{7,6},{8,9},{9,8},{10,11... | collective-permute-start | bytes 983048 | tf_op jit(solution)/shard_map/ppermute | solution.py:463
  (22 other events, 106.7 us)

commit v3 on v2

--- a/solution.py
+++ b/solution.py
@@ -48,42 +48,45 @@
     )
 
 
-def norm_kernel(emb, after, normed, turned):
+def norm_kernel(emb, *refs):
+    normed, turned = refs[-2:]
     xhat, _ = normalise(emb[...].astype(F32))
     normed[...] = xhat.astype(BF)
     turned[...] = normed[...].T
 
 
-def run_norm(embedded, after):
+def run_norm(embedded, after, half, given=()):
     tokens = embedded.shape[0]
+    steps = tokens // SEQ // 2
+    first = half * steps
+    anywhere = pl.BlockSpec(memory_space=pl.ANY)
     return pl.pallas_call(
         norm_kernel,
-        grid=(tokens // SEQ,),
-        in_specs=[
-            pl.BlockSpec((SEQ, WIDTH), lambda i: (i, 0)),
-            pl.BlockSpec(memory_space=pl.ANY),
-        ],
+        grid=(steps,),
+        in_specs=[pl.BlockSpec((SEQ, WIDTH), lambda i: (i + first, 0)), anywhere]
+        + [anywhere] * len(given),
         out_specs=[
-            pl.BlockSpec((SEQ, WIDTH), lambda i: (i, 0)),
-            pl.BlockSpec((WIDTH, SEQ), lambda i: (0, i)),
+            pl.BlockSpec((SEQ, WIDTH), lambda i: (i + first, 0)),
+            pl.BlockSpec((WIDTH, SEQ), lambda i: (0, i + first)),
         ],
         out_shape=[
             jax.ShapeDtypeStruct((tokens, WIDTH), BF),
             jax.ShapeDtypeStruct((WIDTH, tokens), BF),
         ],
+        input_output_aliases={2 + i: i for i in range(len(given))},
         compiler_params=pltpu.CompilerParams(vmem_limit_bytes=56 * 1024 * 1024),
         cost_estimate=pl.CostEstimate(
-            flops=20_000_000, bytes_accessed=6_000_000, transcendentals=2048
+            flops=10_000_000, bytes_accessed=3_000_000, transcendentals=1024
         ),
         name="norm",
-    )(embedded, after)
+    )(embedded, after, *given)
 
 
 def layer_kernel(
-    coords, lens, normed, go, turned, own_in, own_out,
+    coords, lens, normed, go, emb, own_in, own_out,
     low, high, low_o, high_o, far_a, far_b, far_ao, far_bo,
-    gp, mine, other, w_turned,
-    w, slope, hidden, probs, rates, mixed, cot, seq_sum, gp_all, gwout,
+    gp, tokens, gwout,
+    w, w_turned, slope, hidden, probs, rates, mixed, cot, seq_sum,
 ):
     step = pl.program_id(0)
 
@@ -150,7 +153,6 @@
                 probs[head, q_rows, seen], hidden[seen, v_cols]
             )
 
-    here = pl.ds(pl.multiple_of(step * SEQ, SEQ), SEQ)
     keep = lax.broadcasted_iota(jnp.int32, (SEQ, 1), 0) < lens[step]
     raw = jnp.where(keep, mixed[...] * (1.0 / SEQ), 0.0)
     xhat, rstd = normalise(raw)
@@ -159,7 +161,6 @@
     seq_sum[...] = (xhat * gate).astype(BF)
     grad_gate = ((down * xhat).astype(BF).astype(F32) * slope[:, 0:WIDTH]).astype(BF)
     gp[:, 0:WIDTH] = grad_gate
-    gp_all[here, 0:WIDTH] = grad_gate
     back = norm_back(xhat, rstd, down * gate)
     cot[...] = jnp.where(keep, back * (1.0 / SEQ), 0.0).astype(BF)
     gwout[...] += dot_tn(seq_sum[...], go[...])
@@ -167,8 +168,6 @@
     def finish(value, rows, cols):
         grad = (value.astype(BF).astype(F32) * slope[rows, cols]).astype(BF)
         gp[rows, cols] = grad
-        here = pl.ds(pl.multiple_of(step * SEQ + rows.start, HALF), rows.stop - rows.start)
-        gp_all[here, cols] = grad
 
     top, low_half, whole = slice(0, HALF), slice(HALF, SEQ), slice(0, SEQ)
     for head in range(HEADS):
@@ -187,32 +186,12 @@
                 k_cols,
             )
 
-    @pl.when(step == pl.num_programs(0) - 1)
-    def _():
-        tile, per_half = 256, 5
-        core = coords[1]
-
-        def place(half, col, value):
-            cols = pl.ds(pl.multiple_of(col, tile), value.shape[1])
-
-            @pl.when(half == core)
-            def _():
-                mine[:, cols] = value
-
-            @pl.when(half != core)
-            def _():
-                other[:, cols] = value
-
-        @pl.loop(0, 4 * WIDTH // tile)
-        def _(j):
-            cols = pl.ds(pl.multiple_of(j * tile, tile), tile)
-            value = dot_nn(turned[...], gp_all[:, cols]).astype(BF)
-            place(j // per_half, lax.rem(j, per_half) * tile, value)
-
-        place(1, 4 * WIDTH - per_half * tile, gwout[...].astype(BF))
-
-
-def run_layer(coords, lengths, normed, turned, grad_out, pieces):
+    xhat, rstd = normalise(emb[...].astype(F32))
+    back = norm_back(xhat, rstd, dot_nn(gp[...], w_turned[...]))
+    tokens[...] = (back + go[...].astype(F32)).astype(BF)
+
+
+def run_layer(coords, lengths, normed, embedded, grad_out, pieces):
     tokens = normed.shape[0]
     smem = pl.BlockSpec(memory_space=pltpu.SMEM)
 
@@ -225,22 +204,16 @@
     return pl.pallas_call(
         layer_kernel,
         grid=(tokens // SEQ,),
-        in_specs=[smem, smem, by_seq(WIDTH), by_seq(WIDTH)]
-        + [whole(p.shape) for p in (turned, *pieces)],
-        out_specs=[
-            by_seq(4 * WIDTH),
-            whole((WIDTH, 5 * WIDTH // 2)),
-            whole((WIDTH, 5 * WIDTH // 2)),
-            whole((4 * WIDTH, WIDTH)),
-        ],
+        in_specs=[smem, smem] + [by_seq(WIDTH)] * 3 + [whole(p.shape) for p in pieces],
+        out_specs=[by_seq(4 * WIDTH), by_seq(WIDTH), whole((WIDTH, WIDTH))],
         out_shape=[
             jax.ShapeDtypeStruct((tokens, 4 * WIDTH), BF),
-            jax.ShapeDtypeStruct((WIDTH, 5 * WIDTH // 2), BF),
-            jax.ShapeDtypeStruct((WIDTH, 5 * WIDTH // 2), BF),
-            jax.ShapeDtypeStruct((4 * WIDTH, WIDTH), BF),
+            jax.ShapeDtypeStruct((tokens, WIDTH), BF),
+            jax.ShapeDtypeStruct((WIDTH, WIDTH), F32),
         ],
         scratch_shapes=[
             pltpu.VMEM((WIDTH, 5 * WIDTH), BF),
+            pltpu.VMEM((4 * WIDTH, WIDTH), BF),
             pltpu.VMEM((SEQ, 4 * WIDTH), F32),
             pltpu.VMEM((SEQ, 4 * WIDTH), BF),
             pltpu.VMEM((HEADS, SEQ, SEQ), BF),
@@ -248,64 +221,66 @@
             pltpu.VMEM((SEQ, WIDTH), F32),
             pltpu.VMEM((SEQ, WIDTH), BF),
             pltpu.VMEM((SEQ, WIDTH), BF),
-            pltpu.VMEM((tokens, 4 * WIDTH), BF),
-            pltpu.VMEM((WIDTH, WIDTH), F32),
         ],
         compiler_params=pltpu.CompilerParams(vmem_limit_bytes=56 * 1024 * 1024),
         cost_estimate=pl.CostEstimate(
             flops=20_000_000_000, bytes_accessed=20_000_000, transcendentals=8_000_000
         ),
         name="layer",
-    )(coords, lengths, normed, grad_out, turned, *pieces)
-
-
-def token_kernel(emb, go, gp, w, after, tokens, done):
-    grads = dot_nn(gp[...], w[...])
-    xhat, rstd = normalise(emb[...].astype(F32))
-    back = norm_back(xhat, rstd, grads)
-    tokens[...] = (back + go[...].astype(F32)).astype(BF)
-    done[...] = jnp.zeros_like(done)
-
-
-def run_tokens(embedded, grad_out, grad_proj, w, first, steps, after):
-    def by_seq(cols):
-        return pl.BlockSpec((SEQ, cols), lambda i: (i + first, 0))
-
+    )(coords, lengths, normed, grad_out, embedded, *pieces)
+
+
+def weight_kernel(coords, turned, gp, gwout, after, mine, other):
+    step = pl.program_id(0)
+    core, half = coords[1], step // 2
+    cols = pl.ds(pl.multiple_of(lax.rem(step, 2) * WIDTH, WIDTH), WIDTH)
+    value = dot_nn(turned[...], gp[...]).astype(BF)
+
+    @pl.when(half == core)
+    def _():
+        mine[:, cols] = value
+
+    @pl.when(half != core)
+    def _():
+        other[:, cols] = value
+
+    @pl.when(step == 0)
+    def _():
+        sides = gwout[...].astype(BF)
+        first, second = sides[:, : WIDTH // 2], sides[:, WIDTH // 2 :]
+        mine[:, 2 * WIDTH :] = jnp.where(core == 0, first, second)
+        other[:, 2 * WIDTH :] = jnp.where(core == 0, second, first)
+
+
+def run_weights(coords, turned, grad_proj, gwout, after):
+    tokens = turned.shape[1]
+    half = pl.BlockSpec((WIDTH, 5 * WIDTH // 2), lambda i: (0, 0))
     return pl.pallas_call(
-        token_kernel,
-        grid=(steps,),
+        weight_kernel,
+        grid=(4,),
         in_specs=[
-            by_seq(WIDTH),
-            by_seq(WIDTH),
-            by_seq(4 * WIDTH),
-            pl.BlockSpec((4 * WIDTH, WIDTH), lambda i: (0, 0)),
+            pl.BlockSpec(memory_space=pltpu.SMEM),
+            pl.BlockSpec((WIDTH, tokens), lambda i: (0, 0)),
+            pl.BlockSpec((tokens, WIDTH), lambda i: (0, i)),
+            pl.BlockSpec((WIDTH, WIDTH), lambda i: (0, 0)),
             pl.BlockSpec(memory_space=pl.ANY),
         ],
-        out_specs=[
-            pl.BlockSpec((SEQ, WIDTH), lambda i: (i, 0)),
-            pl.BlockSpec((8, 128), lambda i: (0, 0)),
-        ],
-        out_shape=[
-            jax.ShapeDtypeStruct((steps * SEQ, WIDTH), BF),
-            jax.ShapeDtypeStruct((8, 128), F32),
-        ],
+        out_specs=[half, half],
+        out_shape=[jax.ShapeDtypeStruct((WIDTH, 5 * WIDTH // 2), BF)] * 2,
         compiler_params=pltpu.CompilerParams(vmem_limit_bytes=56 * 1024 * 1024),
         cost_estimate=pl.CostEstimate(
-            flops=1_000_000_000, bytes_accessed=4_000_000, transcendentals=2048
+            flops=4_300_000_000, bytes_accessed=13_000_000, transcendentals=0
         ),
-        name="token_grads",
-    )(embedded, grad_out, grad_proj, w, after)
-
-
-def bucket_kernel(bucket, labels, early, late, after, out):
+        name="weight_grads",
+    )(coords, turned, grad_proj, gwout, after)
+
+
+def bucket_kernel(bucket, labels, tokens, out):
     owners = out.shape[1]
-    tile, count = owners * CAP, early.shape[0]
+    tile, count = owners * CAP, tokens.shape[0]
     slot = lax.broadcasted_iota(jnp.int32, (tile, count), 0) + pl.program_id(0) * tile
-
-    def pick(start):
-        return jnp.where(slot == bucket[:, start : start + count], 1.0, 0.0).astype(BF)
-
-    sums = (dot_nn(pick(0), early[...]) + dot_nn(pick(count), late[...])).astype(BF)
+    pick = jnp.where(slot == bucket[...], 1.0, 0.0).astype(BF)
+    sums = dot_nn(pick, tokens[...]).astype(BF)
     upper = lax.shift_right_logical(labels[...], 6)
     lower = jnp.bitwise_and(labels[...], 63)
     lane = lax.broadcasted_iota(jnp.int32, labels.shape, 1)
@@ -319,20 +294,17 @@
             )
 
 
-def run_buckets(bucket, labels, early, late, parts, after):
-    count, width = early.shape
+def run_buckets(bucket, labels, tokens, parts):
+    count, width = tokens.shape
     owners = labels.shape[0]
     per_step = 8
-    whole = pl.BlockSpec((count, width), lambda i: (0, 0))
     return pl.pallas_call(
         bucket_kernel,
         grid=(owners // per_step,),
         in_specs=[
-            pl.BlockSpec((1, 2 * count), lambda i: (0, 0)),
+            pl.BlockSpec((1, count), lambda i: (0, 0)),
             pl.BlockSpec((per_step, 128), lambda i: (i, 0)),
-            whole,
-            whole,
-            pl.BlockSpec(memory_space=pl.ANY),
+            pl.BlockSpec((count, width), lambda i: (0, 0)),
         ],
         out_specs=pl.BlockSpec((parts, per_step, PACKET, 128), lambda i: (0, i, 0, 0)),
         out_shape=jax.ShapeDtypeStruct((parts, owners, PACKET, 128), BF),
@@ -341,26 +313,28 @@
             flops=200_000_000, bytes_accessed=1_000_000, transcendentals=0
         ),
         name="bucket_rows",
-    )(bucket, labels, early, late, after)
+    )(bucket, labels, tokens)
 
 
 def label_kernel(counts, offsets, rows, out):
-    last = rows.shape[0] - 1
-
-    @pl.loop(0, counts.shape[0])
-    def _(owner):
+    lane = lax.broadcasted_iota(jnp.int32, (8, 128), 1)
+    for owner in range(out.shape[0]):
         count, first = counts[owner], offsets[owner]
-        for place in range(CAP):
-            row = rows[jnp.minimum(first + place, last)]
-            out[owner, place] = jnp.where(place < count, row, ROWS_DEV)
+        start = lax.rem(first, 128)
+        near = pltpu.roll(rows[pl.ds(first // 128, 8), :], lax.rem(128 - start, 128), 1)
+        taken = jnp.where(lane[0:1] < 128 - start, near[0:1], near[1:2])
+        out[owner : owner + 1, :] = jnp.where(lane[0:1] < count, taken, ROWS_DEV)
 
 
 def run_labels(counts, offsets, rows):
     smem = pl.BlockSpec(memory_space=pltpu.SMEM)
+    whole = pl.BlockSpec(memory_space=pltpu.VMEM)
+    lines = -(-rows.shape[0] // 128) + 8
+    rows = jnp.pad(rows, (0, lines * 128 - rows.shape[0])).reshape(lines, 128)
     return pl.pallas_call(
         label_kernel,
-        in_specs=[smem] * 3,
-        out_specs=smem,
+        in_specs=[smem, smem, whole],
+        out_specs=whole,
         out_shape=jax.ShapeDtypeStruct((counts.shape[0], 2 * CAP), jnp.int32),
         cost_estimate=pl.CostEstimate(flops=10_000, bytes_accessed=10_000, transcendentals=0),
         name="labels",
@@ -412,10 +386,9 @@
     token[...] = jnp.zeros_like(token)
 
 
-def run_scatter(rows, piece, pieces, tables=None, after=None):
+def run_scatter(rows, start, count, tables=None, after=None):
     sources, packet, width = rows.shape
-    count = sources // pieces
-    first, last = piece > 0, piece == pieces - 1
+    first, last = start > 0, start + count == sources
     whole = pl.BlockSpec(memory_space=pltpu.VMEM)
     table = jax.ShapeDtypeStruct((ROWS_DEV + 8, width), F32)
     scratch = [
@@ -434,7 +407,7 @@
     return pl.pallas_call(
         functools.partial(scatter_kernel, first, last),
         grid=(1,),
-        in_specs=[pl.BlockSpec((count, packet, width), lambda i: (piece, 0, 0))]
+        in_specs=[pl.BlockSpec((count, packet, width), lambda i: (start // count, 0, 0))]
         + ([whole, whole, pl.BlockSpec(memory_space=pl.ANY)] if first else []),
         out_specs=[whole] * len(out_shape),
         out_shape=out_shape,
@@ -499,8 +472,7 @@
     return value.astype(BF)
 
 
-def add_cores(coords, mine, theirs, right, left, far, own, done):
-    done[...] = jnp.zeros_like(done)
+def add_cores(coords, mine, theirs, right, left, far, own):
     rows = own.shape[0]
     for out, offset in ((right, 1), (left, 3), (far, 2), (own, 0)):
         part = block_rows(coords[0], offset, rows)
@@ -524,21 +496,16 @@
 
 def join_cores(factor, coords, own, theirs, share_in, share_out):
     core = coords[1]
-    cut = own.shape[1]
-    width = share_in.shape[1]
-
-    def put(first, second):
-        share_in[:, :cut] = first[...].astype(F32) * factor
-        share_in[:, cut:] = second[:, : width - cut].astype(F32) * factor
-        share_out[...] = second[:, width - cut :].astype(F32) * factor
-
-    @pl.when(core == 0)
-    def _():
-        put(own, theirs)
-
-    @pl.when(core == 1)
-    def _():
-        put(theirs, own)
+    cut = share_in.shape[1] // 2
+    side = share_out.shape[1] // 2
+
+    def put(half, piece):
+        share_in[:, half * cut : (half + 1) * cut] = piece[:, :cut].astype(F32) * factor
+        share_out[:, half * side : (half + 1) * side] = piece[:, cut:].astype(F32) * factor
+
+    for half in range(2):
+        pl.when(core == half)(functools.partial(put, half, own))
+        pl.when(core != half)(functools.partial(put, half, theirs))
 
 
 def per_device(
@@ -557,6 +524,9 @@
     def along_y(array, shift):
         return table_ring(array, 8, 4, shift, table_count)
 
+    def along_z(array, shift):
+        return table_ring(array, 2, 4, shift, table_count)
+
     def three_ways(along, right, left, far):
         return along(right, 1), along(left, -1), along(far, 2)
 
@@ -565,13 +535,13 @@
     )
     low, high = along_x(half, 1), along_x(half, -1)
     labels = run_labels(counts, offsets, local_rows)
-    low, high, labels = lax.optimization_barrier((low, high, labels))
+    given = run_norm(embedded, labels, 0)
+    low, high, *given = lax.optimization_barrier((low, high, *given))
     far_a, far_b = along_x(low[:32], 1), along_x(high[32:], -1)
-    normed, turned = run_norm(embedded, labels)
-    far_a, far_b, normed = lax.optimization_barrier((far_a, far_b, normed))
-    low_o, high_o, far_ao, far_bo = (
-        swap(a, 1, table_count) for a in (low, high, far_a, far_b)
-    )
+    low_o, high_o = swap(low, 1, table_count), swap(high, 1, table_count)
+    normed, turned = run_norm(embedded, labels, 1, given)
+    far_a, far_b, normed, turned = lax.optimization_barrier((far_a, far_b, normed, turned))
+    far_ao, far_bo = swap(far_a, 1, table_count), swap(far_b, 1, table_count)
     pieces = [w_in, w_out, low, high, low_o, high_o, far_a, far_b, far_ao, far_bo]
 
     shift = jnp.where(
@@ -579,57 +549,47 @@
     ).sum(axis=0)
     bucket = (slot_of + shift).reshape(1, -1)
 
-    grad_proj, mine, other, w_full = run_layer(
-        coords, lengths, normed, turned, grad_out, pieces
-    )
-
-    theirs = swap(other, 1, table_count)
-    half = embedded.shape[0] // SEQ // 2
-    early, done = run_tokens(embedded, grad_out, grad_proj, w_full, 0, half, other)
-
+    grad_proj, tokens, gwout = run_layer(
+        coords, lengths, normed, embedded, grad_out, pieces
+    )
+    bucket_rows = run_buckets(bucket, labels, tokens, fsdp_count)
+    values = bucket_rows.reshape(fsdp_count * table_count, PACKET, 128)
+    got = lax.all_to_all(values, BOTH, split_axis=0, concat_axis=0, tiled=True)
+
+    mine, other = run_weights(coords, turned, grad_proj, gwout, bucket_rows)
     rows, cols = mine.shape
-    block = rows // 4
-    mark = ((8, 128), F32)
-    right, left, far, own, done = small_kernel(
+    block, part = rows // 4, rows // 16
+    right, left, far, own = small_kernel(
         add_cores,
         "add_cores",
         coords,
-        (mine, theirs),
-        [((block, cols), BF)] * 4 + [mark],
-        after=(done,),
+        (mine, swap(other, 1, table_count)),
+        [((block, cols), BF)] * 4,
     )
     from_x = three_ways(along_x, right, left, far)
-    late, done = run_tokens(embedded, grad_out, grad_proj, w_full, half, half, done)
-    bucket_rows = run_buckets(bucket, labels, early, late, fsdp_count, done)
-    part = block // 4
-    _, right, left, far, own, bucket_rows = small_kernel(
+    *tables, token = run_scatter(got, 0, 32)
+    _, right, left, far, own = small_kernel(
         add_x,
         "add_x",
         coords,
         (own, *from_x),
         [((block, cols), BF)] + [((part, cols), BF)] * 4,
-        through=(bucket_rows,),
-        limit=58,
-    )
+        after=(token,),
+    )
+    one = [((part, cols), BF)]
     from_y = three_ways(along_y, right, left, far)
-    one = [((part, cols), BF)]
-    values = bucket_rows.reshape(fsdp_count * table_count, PACKET, 128)
-    got = lax.all_to_all(values, BOTH, split_axis=0, concat_axis=0, tiled=True)
-
-    (own,) = small_kernel(add_all, "add_y", coords, (own, *from_y), one)
-    from_z = swap(own, 2, table_count)
-    *tables, token = run_scatter(got, 0, 4)
-    (own,) = small_kernel(add_all, "add_z_low", coords, (own, from_z), one, after=(token,))
-    from_z = swap(own, 4, table_count)
-    *tables, token = run_scatter(got, 1, 4, tables, own)
-    (own,) = small_kernel(add_all, "add_z_high", coords, (own, from_z), one, after=(token,))
+    *tables, token = run_scatter(got, 32, 32, tables, own)
+    (own,) = small_kernel(add_all, "add_y", coords, (own, *from_y), one, after=(token,))
+    from_z = three_ways(along_z, own, own, own)
+    *tables, token = run_scatter(got, 64, 32, tables, own)
+    (own,) = small_kernel(add_all, "add_z", coords, (own, *from_z), one, after=(token,))
     from_y = three_ways(along_y, own, own, own)
-    *tables, token = run_scatter(got, 2, 4, tables, own)
+    *tables, token = run_scatter(got, 96, 16, tables, own)
     (own,) = small_kernel(
         join_y, "join_y", coords, (own, *from_y), [((block, cols), BF)], after=(token,)
     )
     theirs = swap(own, 1, table_count)
-    (grad_table, token) = run_scatter(got, 3, 4, tables, own)
+    grad_table, token = run_scatter(got, 112, 16, tables, own)
     factor = 1.0 / math.sqrt(embedded.shape[0] * fsdp_count * table_count)
     share_in, share_out = small_kernel(
         functools.partial(join_cores, factor),

time: 171 us -> 160 us (0.936)
  Pallas kernels: 94.1 us -> 83.5 us
  waiting for transfers between devices: 32.8 us -> 25.9 us
  starting transfers between devices: 35.8 us -> 42.1 us
    ppermute x6 -> x9, waiting for transfers between devices: 28.9 us -> 2.42 us  [table_ring(): return lax.ppermute(array, 'table', pairs)]
    all_to_all x1, waiting for transfers between devices: 0.01 us -> 13 us  [per_device(): got = lax.all_to_all(values, BOTH, split_axis=0, concat_axis=0, tiled=True)]
    pallas_call x5, Pallas kernels: 63.7 us -> 52.6 us  [the longest x1 35.6 us: run_layer(): pl.pallas_call(layer_kernel, grid=(tokens // SEQ,), in_specs=[smem, smem]...]
    ppermute x6 -> x9, starting transfers between devices: 7.18 us -> 12.2 us  [table_ring(): return lax.ppermute(array, 'table', pairs)]
    ppermute x7, waiting for transfers between devices: 3.2 us -> 7.52 us  [ring(): lax.ppermute(array, axis, [(i, (i + shift) % size) for i in range(size)])]
    ppermute x8 -> x6, waiting for transfers between devices: 0.67 us -> 2.89 us  [swap(): return lax.ppermute(array, 'table', [(i, i ^ bit) for i in range(count)])]
    ppermute x8 -> x6, starting transfers between devices: 11 us -> 9.95 us  [swap(): return lax.ppermute(array, 'table', [(i, i ^ bit) for i in range(count)])]
    unnamed x48 -> x26, local copies, waits for them, and re-layouts: 3.64 us -> 2.86 us
  transfers between devices with their start and end apart: 22 -> 23, of which waited for: 7 -> 7; matrix products, arithmetic and copies ran while one was open for 1% -> 2% of each run, Pallas kernels for 28% -> 22%
where the time goes in v3:
time: 160 us
  Pallas kernels  83.5 us (52%)
  starting transfers between devices  42.1 us (26%)
  waiting for transfers between devices  25.9 us (16%)
  local copies, waits for them, and re-layouts  6 us (4%)
    pallas_call x1, Pallas kernels, run_layer(): pl.pallas_call(layer_kernel, grid=(tokens // SEQ,), in_specs=[smem, smem]...  35.6 us
    pallas_call x5, Pallas kernels, run_scatter(): pl.pallas_call(functools.partial(scatter_kernel, first, last), grid=(1,),...  16.2 us
    all_to_all x1, waiting for transfers between devices, per_device(): got = lax.all_to_all(values, BOTH, split_axis=0, concat_axis=0, tiled=True)  13 us
    ppermute x9, starting transfers between devices, table_ring(): return lax.ppermute(array, 'table', pairs)  12.2 us
    all_to_all x1, starting transfers between devices, per_device(): got = lax.all_to_all(values, BOTH, split_axis=0, concat_axis=0, tiled=True)  10.2 us
    ppermute x6, starting transfers between devices, swap(): return lax.ppermute(array, 'table', [(i, i ^ bit) for i in range(count)])  9.95 us
    ppermute x7, starting transfers between devices, ring(): lax.ppermute(array, axis, [(i, (i + shift) % size) for i in range(size)])  9.86 us
    pallas_call x1, Pallas kernels, run_weights(): pl.pallas_call(weight_kernel, grid=(4,), in_specs=[pl.BlockSpec(memory_sp...  9.71 us
  transfers between devices with their start and end apart: 23, of which 7 were waited for; matrix products, arithmetic and copies ran while one was open for 2% of the time, Pallas kernels for 22%

profile of v3, /device:TPU:1, one launch (start us, length us, event | category | flops | bytes accessed | tf_op | source)
XLA Modules:
  0.0 159.8 jit_solution(6675232330974375943)
XLA Ops:
  2.5 2.1 %collective-permute-start = (bf16[64,2560]{1,0:T(8,128)(2,1)S(1)}, bf16[64,2560]{1,0:T(8,128)(2,1)S(1)}, u32[]{:S(2)}, u32[]{:S(2)}) collective-permute-start(bf16[64,2560]{1,0:T(8,128)(2,1)S(1)} %pad_maximum_fusion), channel_id=1, source_target_pairs={{0,32},{32,64},{64,96},{96,0},{1,33},{33,65},{65,97},{97,1},{2,34}... | collective-permute-start | bytes 983048 | tf_op jit(solution)/shard_map/ppermute | solution.py:424
  8.9 2.9 %norm.2 = (bf16[2048,512]{1,0:T(8,128)(2,1)}, bf16[512,2048]{1,0:T(8,128)(2,1)}) custom-call(bf16[2048,512]{1,0:T(8,128)(2,1)} %emb.5, s32[32,128]{1,0:T(8,128)} %labels.1.refs_0_), custom_call_target="tpu_custom_call" | custom-call | flops 10000000 | bytes 3000000 | tf_op jit(solution)/shard_map/norm/pallas_call | solution.py:63
  12.9 1.9 %collective-permute-start.4 = (bf16[64,2560]{1,0:T(8,128)(2,1)S(1)}, bf16[64,2560]{1,0:T(8,128)(2,1)S(1)}, u32[]{:S(2)}, u32[]{:S(2)}) collective-permute-start(bf16[64,2560]{1,0:T(8,128)(2,1)S(1)} %collective-permute-done.low), channel_id=1, source_target_pairs={{0,1},{1,0},{2,3},{3,2},{4,5},{5,4},{6,7},{7,6},{8,9},{9,8},{10,11... | collective-permute-start | bytes 983048 | tf_op jit(solution)/shard_map/ppermute | solution.py:436
  17.8 2.9 %norm.3 = (bf16[2048,512]{1,0:T(8,128)(2,1)}, bf16[512,2048]{1,0:T(8,128)(2,1)}) custom-call(bf16[2048,512]{1,0:T(8,128)(2,1)} %emb.5, s32[32,128]{1,0:T(8,128)} %labels.1.refs_0_, bf16[2048,512]{1,0:T(8,128)(2,1)} %get-tuple-element.48.refs_1_, bf16[512,2048]{1,0:T(8,128)(2,1)} %get-tuple-element.49.refs_2_), custom_call_target="tpu_custom_call", output_to_operand_aliasing={{0}: (2, {}), {1}: (3, {})} | custom-call | flops 10000000 | bytes 3000000 | tf_op jit(solution)/shard_map/norm/pallas_call | solution.py:63
  26.1 35.6 %layer.1 = (bf16[2048,2048]{1,0:T(8,128)(2,1)}, bf16[2048,512]{1,0:T(8,128)(2,1)}, f32[512,512]{1,0:T(8,128)}) custom-call(s32[4]{0:T(128)} %pad_add_fusion.coords.place, s32[4]{0:T(128)} %lens.1, bf16[2048,512]{1,0:T(8,128)(2,1)} %get-tuple-element.53.normed, bf16[2048,512]{1,0:T(8,128)(2,1)} %go.1, bf16[2048,512]{1,0:T(8,128)(2,1)} %emb.5, ...), custom_call_target="tpu_custom_call" | custom-call | flops 20000000000 | bytes 20000000 | tf_op jit(solution)/shard_map/layer/pallas_call | solution.py:204
  61.7 7.5 %bucket_rows.1.after = bf16[4,32,72,128]{3,2,1,0:T(8,128)(2,1)} custom-call(s32[1,2048]{1,0:T(1,128)} %bitcast.15, s32[32,128]{1,0:T(8,128)} %labels.1.refs_0_, bf16[2048,512]{1,0:T(8,128)(2,1)} %get-tuple-element.58.tokens), custom_call_target="tpu_custom_call" | custom-call | flops 200000000 | bytes 1000000 | tf_op jit(solution)/shard_map/bucket_rows/pallas_call | solution.py:301
  69.2 10.2 %all-to-all-start = ((bf16[128,72,128]{2,1,0:T(8,128)(2,1)}), bf16[128,72,128]{2,1,0:T(8,128)(2,1)S(1)}, u32[]{:S(2)}, u32[]{:S(2)}) async-start(bf16[128,72,128]{2,1,0:T(8,128)(2,1)} %bitcast.14), calls=%async_computation | async-start | bytes 4718592 | tf_op jit(solution)/shard_map/all_to_all | solution.py:557
  79.4 9.7 %weight_grads.1 = (bf16[512,1280]{1,0:T(8,128)(2,1)}, bf16[512,1280]{1,0:T(8,128)(2,1)}) custom-call(s32[4]{0:T(128)} %pad_add_fusion.coords.place, bf16[512,2048]{1,0:T(8,128)(2,1)} %get-tuple-element.52.turned, bf16[2048,2048]{1,0:T(8,128)(2,1)} %get-tuple-element.56.gp, f32[512,512]{1,0:T(8,128)} %get-tuple-element.57.gwout, ...), custom_call_target="tpu_custom_call" | custom-call | flops 4300000256 | bytes 13000000 | tf_op jit(solution)/shard_map/weight_grads/pallas_call | solution.py:258
  90.2 2.9 %collective-permute-done.8.refs_1_ = bf16[512,1280]{1,0:T(8,128)(2,1)S(1)} collective-permute-done((bf16[512,1280]{1,0:T(8,128)(2,1)}, bf16[512,1280]{1,0:T(8,128)(2,1)S(1)}, u32[]{:S(2)}, u32[]{:S(2)}) %collective-permute-start.8) | collective-permute-done | bytes 1310752 | tf_op jit(solution)/shard_map/ppermute | solution.py:436
  94.4 1.6 %add_cores.1 = (bf16[128,1280]{1,0:T(8,128)(2,1)}, bf16[128,1280]{1,0:T(8,128)(2,1)}, bf16[128,1280]{1,0:T(8,128)(2,1)}, bf16[128,1280]{1,0:T(8,128)(2,1)S(1)}) custom-call(s32[4]{0:T(128)S(1)} %copy-done.1, bf16[512,1280]{1,0:T(8,128)(2,1)S(1)} %copy-done, bf16[512,1280]{1,0:T(8,128)(2,1)S(1)} %collective-permute-done.8.refs_1_), custom_call_target="tpu_custom_call" | custom-call | flops 1000000 | bytes 2000000 | tf_op jit(solution)/shard_map/add_cores/pallas_call | solution.py:445
  96.7 2.0 %collective-permute-start.10 = (bf16[128,1280]{1,0:T(8,128)(2,1)}, bf16[128,1280]{1,0:T(8,128)(2,1)S(1)}, u32[]{:S(2)}, u32[]{:S(2)}) collective-permute-start(bf16[128,1280]{1,0:T(8,128)(2,1)} %get-tuple-element.63), channel_id=1, source_target_pairs={{0,96},{32,0},{64,32},{96,64},{1,97},{33,1},{65,33},{97,65},{2,98}... | collective-permute-start | bytes 983048 | tf_op jit(solution)/shard_map/ppermute | solution.py:424
  99.7 13.0 %all-to-all-done.rows = bf16[128,72,128]{2,1,0:T(8,128)(2,1)S(1)} async-done(((bf16[128,72,128]{2,1,0:T(8,128)(2,1)}), bf16[128,72,128]{2,1,0:T(8,128)(2,1)S(1)}, u32[]{:S(2)}, u32[]{:S(2)}) %all-to-all-start) | async-done | bytes 2359328 | tf_op jit(solution)/shard_map/all_to_all | solution.py:557
  112.7 3.6 %scatter.5 = (f32[4104,128]{1,0:T(8,128)S(1)}, f32[4104,128]{1,0:T(8,128)S(1)}, f32[8,128]{1,0:T(8,128)S(1)}) custom-call(bf16[128,72,128]{2,1,0:T(8,128)(2,1)S(1)} %all-to-all-done.rows), custom_call_target="tpu_custom_call" | custom-call | flops 2000000 | bytes 6000000 | tf_op jit(solution)/shard_map/scatter/pallas_call | solution.py:407
  116.4 5.4 %collective-permute-done.11.refs_3_ = bf16[128,1280]{1,0:T(8,128)(2,1)} collective-permute-done((bf16[128,1280]{1,0:T(8,128)(2,1)}, bf16[128,1280]{1,0:T(8,128)(2,1)}, u32[]{:S(2)}, u32[]{:S(2)}) %collective-permute-start.11) | collective-permute-done | bytes 327712 | tf_op jit(solution)/shard_map/ppermute | solution.py:424
  121.8 2.0 %add_x.1 = (bf16[128,1280]{1,0:T(8,128)(2,1)}, bf16[32,1280]{1,0:T(8,128)(2,1)S(1)}, bf16[32,1280]{1,0:T(8,128)(2,1)S(1)}, bf16[32,1280]{1,0:T(8,128)(2,1)S(1)}, bf16[32,1280]{1,0:T(8,128)(2,1)S(1)}) custom-call(s32[4]{0:T(128)S(1)} %copy-done.1, bf16[128,1280]{1,0:T(8,128)(2,1)S(1)} %get-tuple-element.61.refs_0_, ...), custom_call_target="tpu_custom_call" | custom-call | flops 1000000 | bytes 2000000 | tf_op jit(solution)/shard_map/add_x/pallas_call | solution.py:445
  128.0 3.4 %scatter.6 = (f32[4104,128]{1,0:T(8,128)S(1)}, f32[4104,128]{1,0:T(8,128)S(1)}, f32[8,128]{1,0:T(8,128)S(1)}) custom-call(bf16[128,72,128]{2,1,0:T(8,128)(2,1)S(1)} %all-to-all-done.rows, f32[4104,128]{1,0:T(8,128)S(1)} %get-tuple-element.70.refs_0_, f32[4104,128]{1,0:T(8,128)S(1)} %get-tuple-element.71.refs_1_, ...), custom_call_target="tpu_custom_call" | custom-call | flops 2000000 | bytes 6000000 | tf_op jit(solution)/shard_map/scatter/pallas_call | solution.py:407
  133.6 1.8 %collective-permute-start.16 = (bf16[32,1280]{1,0:T(8,128)(2,1)S(1)}, bf16[32,1280]{1,0:T(8,128)(2,1)S(1)}, u32[]{:S(2)}, u32[]{:S(2)}) collective-permute-start(bf16[32,1280]{1,0:T(8,128)(2,1)S(1)} %add_y.1.refs_2_.refs_0_), channel_id=1, source_target_pairs={{0,6},{1,7},{2,0},{3,1},{4,2},{5,3},{6,4},{7,5},{8,14},{9,15},{10,... | collective-permute-start | bytes 245768 | tf_op jit(solution)/shard_map/ppermute | solution.py:432
  136.9 3.5 %scatter.7 = (f32[4104,128]{1,0:T(8,128)S(1)}, f32[4104,128]{1,0:T(8,128)S(1)}, f32[8,128]{1,0:T(8,128)S(1)}) custom-call(bf16[128,72,128]{2,1,0:T(8,128)(2,1)S(1)} %all-to-all-done.rows, f32[4104,128]{1,0:T(8,128)S(1)} %get-tuple-element.73.refs_0_, f32[4104,128]{1,0:T(8,128)S(1)} %get-tuple-element.74.refs_1_, bf16[32,1280]{1,0:T(8,128)(2,1)S(1)} %add_y.1.refs_2_.refs_0_), custom_call_target="tpu_custom_call" | custom-call | flops 2000000 | bytes 6000000 | tf_op jit(solution)/shard_map/scatter/pallas_call | solution.py:407
  141.5 2.3 %collective-permute-start.19 = (bf16[32,1280]{1,0:T(8,128)(2,1)S(1)}, bf16[32,1280]{1,0:T(8,128)(2,1)S(1)}, u32[]{:S(2)}, u32[]{:S(2)}) collective-permute-start(bf16[32,1280]{1,0:T(8,128)(2,1)S(1)} %add_z.1.refs_2_.refs_0_), channel_id=1, source_target_pairs={{0,24},{1,25},{2,26},{3,27},{4,28},{5,29},{6,30},{7,31},{8,0},{9,1... | collective-permute-start | bytes 245768 | tf_op jit(solution)/shard_map/ppermute | solution.py:432
  144.3 2.0 %scatter.8 = (f32[4104,128]{1,0:T(8,128)S(1)}, f32[4104,128]{1,0:T(8,128)S(1)}, f32[8,128]{1,0:T(8,128)S(1)}) custom-call(bf16[128,72,128]{2,1,0:T(8,128)(2,1)S(1)} %all-to-all-done.rows, f32[4104,128]{1,0:T(8,128)S(1)} %get-tuple-element.76.refs_0_, f32[4104,128]{1,0:T(8,128)S(1)} %get-tuple-element.77.refs_1_, bf16[32,1280]{1,0:T(8,128)(2,1)S(1)} %add_z.1.refs_2_.refs_0_), custom_call_target="tpu_custom_call" | custom-call | flops 2000000 | bytes 6000000 | tf_op jit(solution)/shard_map/scatter/pallas_call | solution.py:407
  146.3 2.3 %collective-permute-done.20.refs_3_ = bf16[32,1280]{1,0:T(8,128)(2,1)S(1)} collective-permute-done((bf16[32,1280]{1,0:T(8,128)(2,1)S(1)}, bf16[32,1280]{1,0:T(8,128)(2,1)S(1)}, u32[]{:S(2)}, u32[]{:S(2)}) %collective-permute-start.20) | collective-permute-done | bytes 81952 | tf_op jit(solution)/shard_map/ppermute | solution.py:432
  149.2 5.2 %collective-permute-start.21 = (bf16[128,1280]{1,0:T(8,128)(2,1)S(1)}, bf16[128,1280]{1,0:T(8,128)(2,1)S(1)}, u32[]{:S(2)}, u32[]{:S(2)}) collective-permute-start(bf16[128,1280]{1,0:T(8,128)(2,1)S(1)} %join_y.1.refs_2_.refs_0_), channel_id=1, source_target_pairs={{0,1},{1,0},{2,3},{3,2},{4,5},{5,4},{6,7},{7,6},{8,9},{9,8},{10,11... | collective-permute-start | bytes 983048 | tf_op jit(solution)/shard_map/ppermute | solution.py:436
  154.4 3.6 %scatter.9 = (f32[4096,128]{1,0:T(8,128)}, f32[8,128]{1,0:T(8,128)S(1)}) custom-call(bf16[128,72,128]{2,1,0:T(8,128)(2,1)S(1)} %all-to-all-done.rows, f32[4104,128]{1,0:T(8,128)S(1)} %get-tuple-element.79.refs_0_, f32[4104,128]{1,0:T(8,128)S(1)} %get-tuple-element.80.refs_1_, bf16[128,1280]{1,0:T(8,128)(2,1)S(1)} %join_y.1.refs_2_.refs_0_), custom_call_target="tpu_custom_call" | custom-call | flops 2000000 | bytes 6000000 | tf_op jit(solution)/shard_map/scatter/pallas_call | solution.py:407
  158.1 1.7 %join_cores.1 = (f32[128,2048]{1,0:T(8,128)}, f32[128,512]{1,0:T(8,128)}) custom-call(s32[4]{0:T(128)S(1)} %copy-done.1, bf16[128,1280]{1,0:T(8,128)(2,1)S(1)} %join_y.1.refs_2_.refs_0_, bf16[128,1280]{1,0:T(8,128)(2,1)S(1)} %collective-permute-done.21.refs_1_, f32[8,128]{1,0:T(8,128)S(1)} %get-tuple-element.81.refs_2_), custom_call_target="tpu_custom_call" | custom-call | flops 1000000 | bytes 2000000 | tf_op jit(solution)/shard_map/join_cores/pallas_call | solution.py:445
  (75 shorter events, 29.5 us)
Async XLA Ops:
  0.6 17.1 %copy-start.5 = (s32[1,32]{1,0:T(1,128)S(1)}, s32[1,32]{1,0:T(1,128)}, u32[]{:S(2)}) copy-start(s32[1,32]{1,0:T(1,128)} %param.16) | copy-start | bytes 388
  2.5 10.4 %collective-permute-start = (bf16[64,2560]{1,0:T(8,128)(2,1)S(1)}, bf16[64,2560]{1,0:T(8,128)(2,1)S(1)}, u32[]{:S(2)}, u32[]{:S(2)}) collective-permute-start(bf16[64,2560]{1,0:T(8,128)(2,1)S(1)} %pad_maximum_fusion), channel_id=1, source_target_pairs={{0,32},{32,64},{64,96},{96,0},{1,33},{33,65},{65,97},{97,1},{2,34}... | collective-permute-start | bytes 983048 | tf_op jit(solution)/shard_map/ppermute | solution.py:424
  4.6 8.3 %collective-permute-start.1 = (bf16[64,2560]{1,0:T(8,128)(2,1)S(1)}, bf16[64,2560]{1,0:T(8,128)(2,1)S(1)}, u32[]{:S(2)}, u32[]{:S(2)}) collective-permute-start(bf16[64,2560]{1,0:T(8,128)(2,1)S(1)} %pad_maximum_fusion), channel_id=1, source_target_pairs={{0,96},{32,0},{64,32},{96,64},{1,97},{33,1},{65,33},{97,65},{2,98}... | collective-permute-start | bytes 983048 | tf_op jit(solution)/shard_map/ppermute | solution.py:424
  12.9 11.6 %collective-permute-start.4 = (bf16[64,2560]{1,0:T(8,128)(2,1)S(1)}, bf16[64,2560]{1,0:T(8,128)(2,1)S(1)}, u32[]{:S(2)}, u32[]{:S(2)}) collective-permute-start(bf16[64,2560]{1,0:T(8,128)(2,1)S(1)} %collective-permute-done.low), channel_id=1, source_target_pairs={{0,1},{1,0},{2,3},{3,2},{4,5},{5,4},{6,7},{7,6},{8,9},{9,8},{10,11... | collective-permute-start | bytes 983048 | tf_op jit(solution)/shard_map/ppermute | solution.py:436
  14.9 9.7 %collective-permute-start.5 = (bf16[64,2560]{1,0:T(8,128)(2,1)S(1)}, bf16[64,2560]{1,0:T(8,128)(2,1)S(1)}, u32[]{:S(2)}, u32[]{:S(2)}) collective-permute-start(bf16[64,2560]{1,0:T(8,128)(2,1)S(1)} %collective-permute-done.1.high), channel_id=1, source_target_pairs={{0,1},{1,0},{2,3},{3,2},{4,5},{5,4},{6,7},{7,6},{8,9},{9,8},{10,11... | collective-permute-start | bytes 983048 | tf_op jit(solution)/shard_map/ppermute | solution.py:436
  15.0 6.6 %collective-permute-start.2 = (bf16[32,2560]{1,0:T(8,128)(2,1)S(1)}, bf16[32,2560]{1,0:T(8,128)(2,1)S(1)}, u32[]{:S(2)}, u32[]{:S(2)}) collective-permute-start(bf16[32,2560]{1,0:T(8,128)(2,1)S(1)} %slice.14), channel_id=1, source_target_pairs={{0,32},{32,64},{64,96},{96,0},{1,33},{33,65},{65,97},{97,1},{2,34}... | collective-permute-start | bytes 491528 | tf_op jit(solution)/shard_map/ppermute | solution.py:424
  16.2 5.4 %collective-permute-start.3 = (bf16[32,2560]{1,0:T(8,128)(2,1)S(1)}, bf16[32,2560]{1,0:T(8,128)(2,1)S(1)}, u32[]{:S(2)}, u32[]{:S(2)}) collective-permute-start(bf16[32,2560]{1,0:T(8,128)(2,1)S(1)} %slice.15), channel_id=1, source_target_pairs={{0,96},{32,0},{64,32},{96,64},{1,97},{33,1},{65,33},{97,65},{2,98}... | collective-permute-start | bytes 491528 | tf_op jit(solution)/shard_map/ppermute | solution.py:424
  21.6 3.0 %collective-permute-start.6 = (bf16[32,2560]{1,0:T(8,128)(2,1)S(1)}, bf16[32,2560]{1,0:T(8,128)(2,1)S(1)}, u32[]{:S(2)}, u32[]{:S(2)}) collective-permute-start(bf16[32,2560]{1,0:T(8,128)(2,1)S(1)} %collective-permute-done.2.far_a), channel_id=1, source_target_pairs={{0,1},{1,0},{2,3},{3,2},{4,5},{5,4},{6,7},{7,6},{8,9},{9,8},{10,11... | collective-permute-start | bytes 491528 | tf_op jit(solution)/shard_map/ppermute | solution.py:436
  22.9 1.6 %collective-permute-start.7 = (bf16[32,2560]{1,0:T(8,128)(2,1)S(1)}, bf16[32,2560]{1,0:T(8,128)(2,1)S(1)}, u32[]{:S(2)}, u32[]{:S(2)}) collective-permute-start(bf16[32,2560]{1,0:T(8,128)(2,1)S(1)} %collective-permute-done.3.far_b), channel_id=1, source_target_pairs={{0,1},{1,0},{2,3},{3,2},{4,5},{5,4},{6,7},{7,6},{8,9},{9,8},{10,11... | collective-permute-start | bytes 491528 | tf_op jit(solution)/shard_map/ppermute | solution.py:436
  69.2 43.5 %all-to-all-start = ((bf16[128,72,128]{2,1,0:T(8,128)(2,1)}), bf16[128,72,128]{2,1,0:T(8,128)(2,1)S(1)}, u32[]{:S(2)}, u32[]{:S(2)}) async-start(bf16[128,72,128]{2,1,0:T(8,128)(2,1)} %bitcast.14), calls=%async_computation | async-start | bytes 4718592 | tf_op jit(solution)/shard_map/all_to_all | solution.py:557
  89.1 3.9 %collective-permute-start.8 = (bf16[512,1280]{1,0:T(8,128)(2,1)}, bf16[512,1280]{1,0:T(8,128)(2,1)S(1)}, u32[]{:S(2)}, u32[]{:S(2)}) collective-permute-start(bf16[512,1280]{1,0:T(8,128)(2,1)} %get-tuple-element.60), channel_id=1, source_target_pairs={{0,1},{1,0},{2,3},{3,2},{4,5},{5,4},{6,7},{7,6},{8,9},{9,8},{10,11... | collective-permute-start | bytes 3932168 | tf_op jit(solution)/shard_map/ppermute | solution.py:436
  96.0 20.4 %collective-permute-start.9 = (bf16[128,1280]{1,0:T(8,128)(2,1)}, bf16[128,1280]{1,0:T(8,128)(2,1)S(1)}, u32[]{:S(2)}, u32[]{:S(2)}) collective-permute-start(bf16[128,1280]{1,0:T(8,128)(2,1)} %get-tuple-element.62), channel_id=1, source_target_pairs={{0,32},{32,64},{64,96},{96,0},{1,33},{33,65},{65,97},{97,1},{2,34}... | collective-permute-start | bytes 983048 | tf_op jit(solution)/shard_map/ppermute | solution.py:424
  96.7 19.7 %collective-permute-start.10 = (bf16[128,1280]{1,0:T(8,128)(2,1)}, bf16[128,1280]{1,0:T(8,128)(2,1)S(1)}, u32[]{:S(2)}, u32[]{:S(2)}) collective-permute-start(bf16[128,1280]{1,0:T(8,128)(2,1)} %get-tuple-element.63), channel_id=1, source_target_pairs={{0,96},{32,0},{64,32},{96,64},{1,97},{33,1},{65,33},{97,65},{2,98}... | collective-permute-start | bytes 983048 | tf_op jit(solution)/shard_map/ppermute | solution.py:424
  98.7 23.1 %collective-permute-start.11 = (bf16[128,1280]{1,0:T(8,128)(2,1)}, bf16[128,1280]{1,0:T(8,128)(2,1)}, u32[]{:S(2)}, u32[]{:S(2)}) collective-permute-start(bf16[128,1280]{1,0:T(8,128)(2,1)} %get-tuple-element.64), channel_id=1, source_target_pairs={{0,64},{32,96},{64,0},{96,32},{1,65},{33,97},{65,1},{97,33},{2,66}... | collective-permute-start | bytes 983048 | tf_op jit(solution)/shard_map/ppermute | solution.py:424
  123.8 7.6 %collective-permute-start.12 = (bf16[32,1280]{1,0:T(8,128)(2,1)S(1)}, bf16[32,1280]{1,0:T(8,128)(2,1)S(1)}, u32[]{:S(2)}, u32[]{:S(2)}) collective-permute-start(bf16[32,1280]{1,0:T(8,128)(2,1)S(1)} %get-tuple-element.67), channel_id=1, source_target_pairs={{0,8},{1,9},{2,10},{3,11},{4,12},{5,13},{6,14},{7,15},{8,16},{9,17... | collective-permute-start | bytes 245768 | tf_op jit(solution)/shard_map/ppermute | solution.py:432
  125.0 6.4 %collective-permute-start.13 = (bf16[32,1280]{1,0:T(8,128)(2,1)S(1)}, bf16[32,1280]{1,0:T(8,128)(2,1)S(1)}, u32[]{:S(2)}, u32[]{:S(2)}) collective-permute-start(bf16[32,1280]{1,0:T(8,128)(2,1)S(1)} %get-tuple-element.68), channel_id=1, source_target_pairs={{0,24},{1,25},{2,26},{3,27},{4,28},{5,29},{6,30},{7,31},{8,0},{9,1... | collective-permute-start | bytes 245768 | tf_op jit(solution)/shard_map/ppermute | solution.py:432
  126.5 5.0 %collective-permute-start.14 = (bf16[32,1280]{1,0:T(8,128)(2,1)S(1)}, bf16[32,1280]{1,0:T(8,128)(2,1)S(1)}, u32[]{:S(2)}, u32[]{:S(2)}) collective-permute-start(bf16[32,1280]{1,0:T(8,128)(2,1)S(1)} %get-tuple-element.69), channel_id=1, source_target_pairs={{0,16},{1,17},{2,18},{3,19},{4,20},{5,21},{6,22},{7,23},{8,24},{9,... | collective-permute-start | bytes 245768 | tf_op jit(solution)/shard_map/ppermute | solution.py:432
  132.1 8.3 %collective-permute-start.15 = (bf16[32,1280]{1,0:T(8,128)(2,1)S(1)}, bf16[32,1280]{1,0:T(8,128)(2,1)S(1)}, u32[]{:S(2)}, u32[]{:S(2)}) collective-permute-start(bf16[32,1280]{1,0:T(8,128)(2,1)S(1)} %add_y.1.refs_2_.refs_0_), channel_id=1, source_target_pairs={{0,2},{1,3},{2,4},{3,5},{4,6},{5,7},{6,0},{7,1},{8,10},{9,11},{10,... | collective-permute-start | bytes 245768 | tf_op jit(solution)/shard_map/ppermute | solution.py:432
  133.6 6.8 %collective-permute-start.16 = (bf16[32,1280]{1,0:T(8,128)(2,1)S(1)}, bf16[32,1280]{1,0:T(8,128)(2,1)S(1)}, u32[]{:S(2)}, u32[]{:S(2)}) collective-permute-start(bf16[32,1280]{1,0:T(8,128)(2,1)S(1)} %add_y.1.refs_2_.refs_0_), channel_id=1, source_target_pairs={{0,6},{1,7},{2,0},{3,1},{4,2},{5,3},{6,4},{7,5},{8,14},{9,15},{10,... | collective-permute-start | bytes 245768 | tf_op jit(solution)/shard_map/ppermute | solution.py:432
  135.5 5.0 %collective-permute-start.17 = (bf16[32,1280]{1,0:T(8,128)(2,1)S(1)}, bf16[32,1280]{1,0:T(8,128)(2,1)S(1)}, u32[]{:S(2)}, u32[]{:S(2)}) collective-permute-start(bf16[32,1280]{1,0:T(8,128)(2,1)S(1)} %add_y.1.refs_2_.refs_0_), channel_id=1, source_target_pairs={{0,4},{1,5},{2,6},{3,7},{4,0},{5,1},{6,2},{7,3},{8,12},{9,13},{10,... | collective-permute-start | bytes 245768 | tf_op jit(solution)/shard_map/ppermute | solution.py:432
  141.0 5.3 %collective-permute-start.18 = (bf16[32,1280]{1,0:T(8,128)(2,1)S(1)}, bf16[32,1280]{1,0:T(8,128)(2,1)S(1)}, u32[]{:S(2)}, u32[]{:S(2)}) collective-permute-start(bf16[32,1280]{1,0:T(8,128)(2,1)S(1)} %add_z.1.refs_2_.refs_0_), channel_id=1, source_target_pairs={{0,8},{1,9},{2,10},{3,11},{4,12},{5,13},{6,14},{7,15},{8,16},{9,17... | collective-permute-start | bytes 245768 | tf_op jit(solution)/shard_map/ppermute | solution.py:432
  141.5 4.8 %collective-permute-start.19 = (bf16[32,1280]{1,0:T(8,128)(2,1)S(1)}, bf16[32,1280]{1,0:T(8,128)(2,1)S(1)}, u32[]{:S(2)}, u32[]{:S(2)}) collective-permute-start(bf16[32,1280]{1,0:T(8,128)(2,1)S(1)} %add_z.1.refs_2_.refs_0_), channel_id=1, source_target_pairs={{0,24},{1,25},{2,26},{3,27},{4,28},{5,29},{6,30},{7,31},{8,0},{9,1... | collective-permute-start | bytes 245768 | tf_op jit(solution)/shard_map/ppermute | solution.py:432
  143.8 4.8 %collective-permute-start.20 = (bf16[32,1280]{1,0:T(8,128)(2,1)S(1)}, bf16[32,1280]{1,0:T(8,128)(2,1)S(1)}, u32[]{:S(2)}, u32[]{:S(2)}) collective-permute-start(bf16[32,1280]{1,0:T(8,128)(2,1)S(1)} %add_z.1.refs_2_.refs_0_), channel_id=1, source_target_pairs={{0,16},{1,17},{2,18},{3,19},{4,20},{5,21},{6,22},{7,23},{8,24},{9,... | collective-permute-start | bytes 245768 | tf_op jit(solution)/shard_map/ppermute | solution.py:432
  149.2 8.9 %collective-permute-start.21 = (bf16[128,1280]{1,0:T(8,128)(2,1)S(1)}, bf16[128,1280]{1,0:T(8,128)(2,1)S(1)}, u32[]{:S(2)}, u32[]{:S(2)}) collective-permute-start(bf16[128,1280]{1,0:T(8,128)(2,1)S(1)} %join_y.1.refs_2_.refs_0_), channel_id=1, source_target_pairs={{0,1},{1,0},{2,3},{3,2},{4,5},{5,4},{6,7},{7,6},{8,9},{9,8},{10,11... | collective-permute-start | bytes 983048 | tf_op jit(solution)/shard_map/ppermute | solution.py:436
  (12 other events, 62.1 us)

commit v4 on v3

--- a/solution.py
+++ b/solution.py
@@ -479,10 +479,10 @@
         out[...] = total(mine[part, :], theirs[part, :])
 
 
-def add_x(coords, own, from_left, from_right, from_far, scratch, right, left, far, mine):
-    scratch[...] = total(own[...], from_left[...], from_right[...], from_far[...])
+def add_x(coords, own, from_left, from_right, from_far, right, left, far, mine):
     for out, offset in ((right, 1), (left, 3), (far, 2), (mine, 0)):
-        out[...] = scratch[block_rows(coords[2], offset, out.shape[0]), :]
+        rows = block_rows(coords[2], offset, out.shape[0])
+        out[...] = total(own[rows, :], from_left[rows, :], from_right[rows, :], from_far[rows, :])
 
 
 def add_all(coords, *refs):
@@ -539,15 +539,16 @@
     low, high, *given = lax.optimization_barrier((low, high, *given))
     far_a, far_b = along_x(low[:32], 1), along_x(high[32:], -1)
     low_o, high_o = swap(low, 1, table_count), swap(high, 1, table_count)
-    normed, turned = run_norm(embedded, labels, 1, given)
-    far_a, far_b, normed, turned = lax.optimization_barrier((far_a, far_b, normed, turned))
-    far_ao, far_bo = swap(far_a, 1, table_count), swap(far_b, 1, table_count)
-    pieces = [w_in, w_out, low, high, low_o, high_o, far_a, far_b, far_ao, far_bo]
-
     shift = jnp.where(
         slot_of[None, :] >= offsets[1:, None], CAP - counts[:-1, None], 0
     ).sum(axis=0)
     bucket = (slot_of + shift).reshape(1, -1)
+    normed, turned = run_norm(embedded, labels, 1, given)
+    far_a, far_b, normed, turned, coords, bucket = lax.optimization_barrier(
+        (far_a, far_b, normed, turned, coords, bucket)
+    )
+    far_ao, far_bo = swap(far_a, 1, table_count), swap(far_b, 1, table_count)
+    pieces = [w_in, w_out, low, high, low_o, high_o, far_a, far_b, far_ao, far_bo]
 
     grad_proj, tokens, gwout = run_layer(
         coords, lengths, normed, embedded, grad_out, pieces
@@ -567,29 +568,27 @@
         [((block, cols), BF)] * 4,
     )
     from_x = three_ways(along_x, right, left, far)
-    *tables, token = run_scatter(got, 0, 32)
-    _, right, left, far, own = small_kernel(
+    *tables, token = run_scatter(got, 0, 96)
+    right, left, far, own = small_kernel(
         add_x,
         "add_x",
         coords,
         (own, *from_x),
-        [((block, cols), BF)] + [((part, cols), BF)] * 4,
+        [((part, cols), BF)] * 4,
         after=(token,),
     )
     one = [((part, cols), BF)]
     from_y = three_ways(along_y, right, left, far)
-    *tables, token = run_scatter(got, 32, 32, tables, own)
-    (own,) = small_kernel(add_all, "add_y", coords, (own, *from_y), one, after=(token,))
+    (own,) = small_kernel(add_all, "add_y", coords, (own, *from_y), one)
     from_z = three_ways(along_z, own, own, own)
-    *tables, token = run_scatter(got, 64, 32, tables, own)
+    *tables, token = run_scatter(got, 96, 16, tables, own)
     (own,) = small_kernel(add_all, "add_z", coords, (own, *from_z), one, after=(token,))
     from_y = three_ways(along_y, own, own, own)
-    *tables, token = run_scatter(got, 96, 16, tables, own)
+    grad_table, token = run_scatter(got, 112, 16, tables, own)
     (own,) = small_kernel(
         join_y, "join_y", coords, (own, *from_y), [((block, cols), BF)], after=(token,)
     )
     theirs = swap(own, 1, table_count)
-    grad_table, token = run_scatter(got, 112, 16, tables, own)
     factor = 1.0 / math.sqrt(embedded.shape[0] * fsdp_count * table_count)
     share_in, share_out = small_kernel(
         functools.partial(join_cores, factor),
@@ -597,7 +596,6 @@
         coords,
         (own, theirs),
         [((block, 4 * WIDTH), F32), ((block, WIDTH), F32)],
-        after=(token,),
     )
     return (share_in, share_out, grad_table)
 

time: 160 us -> 157 us (0.981)
  starting transfers between devices: 42.1 us -> 37.9 us
  waiting for transfers between devices: 25.9 us -> 29.5 us
  Pallas kernels: 83.5 us -> 81 us
    ppermute x9, waiting for transfers between devices: 2.42 us -> 6.58 us  [table_ring(): return lax.ppermute(array, 'table', pairs)]
    ppermute x7, waiting for transfers between devices: 7.52 us -> 4.35 us  [ring(): lax.ppermute(array, axis, [(i, (i + shift) % size) for i in range(size)])]
    ppermute x6, waiting for transfers between devices: 2.89 us -> 5.52 us  [swap(): return lax.ppermute(array, 'table', [(i, i ^ bit) for i in range(count)])]
    all_to_all x1, starting transfers between devices: 10.2 us -> 7.98 us  [per_device(): got = lax.all_to_all(values, BOTH, split_axis=0, concat_axis=0, tiled=True)]
    pallas_call x5 -> x3, Pallas kernels: 16.2 us -> 14.6 us  [run_scatter(): pl.pallas_call(functools.partial(scatter_kernel, first, last), grid=(1,),...]
  transfers between devices with their start and end apart: 23 -> 23, of which waited for: 7 -> 12; matrix products, arithmetic and copies ran while one was open for 2% -> 2% of each run, Pallas kernels for 22% -> 21%
where the time goes in v4:
time: 157 us
  Pallas kernels  81 us (52%)
  starting transfers between devices  37.9 us (24%)
  waiting for transfers between devices  29.5 us (19%)
  local copies, waits for them, and re-layouts  6 us (4%)
    pallas_call x1, Pallas kernels, run_layer(): pl.pallas_call(layer_kernel, grid=(tokens // SEQ,), in_specs=[smem, smem]...  35.6 us
    pallas_call x3, Pallas kernels, run_scatter(): pl.pallas_call(functools.partial(scatter_kernel, first, last), grid=(1,),...  14.6 us
    all_to_all x1, waiting for transfers between devices, per_device(): got = lax.all_to_all(values, BOTH, split_axis=0, concat_axis=0, tiled=True)  13 us
    ppermute x9, starting transfers between devices, table_ring(): return lax.ppermute(array, 'table', pairs)  11.5 us
    ppermute x6, starting transfers between devices, swap(): return lax.ppermute(array, 'table', [(i, i ^ bit) for i in range(count)])  9.86 us
    pallas_call x1, Pallas kernels, run_weights(): pl.pallas_call(weight_kernel, grid=(4,), in_specs=[pl.BlockSpec(memory_sp...  9.72 us
    ppermute x7, starting transfers between devices, ring(): lax.ppermute(array, axis, [(i, (i + shift) % size) for i in range(size)])  8.56 us
    all_to_all x1, starting transfers between devices, per_device(): got = lax.all_to_all(values, BOTH, split_axis=0, concat_axis=0, tiled=True)  7.98 us
  transfers between devices with their start and end apart: 23, of which 12 were waited for; matrix products, arithmetic and copies ran while one was open for 2% of the time, Pallas kernels for 21%

profile of v4, /device:TPU:1, one launch (start us, length us, event | category | flops | bytes accessed | tf_op | source)
XLA Modules:
  0.0 156.7 jit_solution(16089999777009014439)
XLA Ops:
  2.5 3.4 %collective-permute-start.1 = (bf16[64,2560]{1,0:T(8,128)(2,1)S(1)}, bf16[64,2560]{1,0:T(8,128)(2,1)S(1)}, u32[]{:S(2)}, u32[]{:S(2)}) collective-permute-start(bf16[64,2560]{1,0:T(8,128)(2,1)S(1)} %pad_maximum_fusion), channel_id=1, source_target_pairs={{0,96},{32,0},{64,32},{96,64},{1,97},{33,1},{65,33},{97,65},{2,98}... | collective-permute-start | bytes 983048 | tf_op jit(solution)/shard_map/ppermute | solution.py:424
  7.2 1.6 %labels.1.refs_0_ = s32[32,128]{1,0:T(8,128)} custom-call(s32[32]{0:T(128)} %bitcast.16, s32[32]{0:T(128)} %bitcast.17, s32[21,128]{1,0:T(8,128)} %pad_bitcast_fusion.rows), custom_call_target="tpu_custom_call" | custom-call | flops 10000 | bytes 10000 | tf_op jit(solution)/shard_map/labels/pallas_call | solution.py:334
  8.8 2.9 %norm.2 = (bf16[2048,512]{1,0:T(8,128)(2,1)}, bf16[512,2048]{1,0:T(8,128)(2,1)}) custom-call(bf16[2048,512]{1,0:T(8,128)(2,1)} %emb.5, s32[32,128]{1,0:T(8,128)} %labels.1.refs_0_), custom_call_target="tpu_custom_call" | custom-call | flops 10000000 | bytes 3000000 | tf_op jit(solution)/shard_map/norm/pallas_call | solution.py:63
  12.3 3.1 %collective-permute-done.low = bf16[64,2560]{1,0:T(8,128)(2,1)S(1)} collective-permute-done((bf16[64,2560]{1,0:T(8,128)(2,1)S(1)}, bf16[64,2560]{1,0:T(8,128)(2,1)S(1)}, u32[]{:S(2)}, u32[]{:S(2)}) %collective-permute-start) | collective-permute-done | bytes 327712 | tf_op jit(solution)/shard_map/ppermute | solution.py:424
  15.4 1.9 %collective-permute-start.4 = (bf16[64,2560]{1,0:T(8,128)(2,1)S(1)}, bf16[64,2560]{1,0:T(8,128)(2,1)S(1)}, u32[]{:S(2)}, u32[]{:S(2)}) collective-permute-start(bf16[64,2560]{1,0:T(8,128)(2,1)S(1)} %collective-permute-done.low), channel_id=1, source_target_pairs={{0,1},{1,0},{2,3},{3,2},{4,5},{5,4},{6,7},{7,6},{8,9},{9,8},{10,11... | collective-permute-start | bytes 983048 | tf_op jit(solution)/shard_map/ppermute | solution.py:436
  20.3 2.9 %norm.3 = (bf16[2048,512]{1,0:T(8,128)(2,1)}, bf16[512,2048]{1,0:T(8,128)(2,1)}) custom-call(bf16[2048,512]{1,0:T(8,128)(2,1)} %emb.5, s32[32,128]{1,0:T(8,128)} %labels.1.refs_0_, bf16[2048,512]{1,0:T(8,128)(2,1)} %get-tuple-element.44.refs_1_, bf16[512,2048]{1,0:T(8,128)(2,1)} %get-tuple-element.45.refs_2_), custom_call_target="tpu_custom_call", output_to_operand_aliasing={{0}: (2, {}), {1}: (3, {})} | custom-call | flops 10000000 | bytes 3000000 | tf_op jit(solution)/shard_map/norm/pallas_call | solution.py:63
  23.9 1.5 collective-permute-start.6
  28.4 35.6 %layer.1 = (bf16[2048,2048]{1,0:T(8,128)(2,1)}, bf16[2048,512]{1,0:T(8,128)(2,1)}, f32[512,512]{1,0:T(8,128)}) custom-call(s32[4]{0:T(128)} %pad_add_fusion.coords.place, s32[4]{0:T(128)} %lens.1, bf16[2048,512]{1,0:T(8,128)(2,1)} %get-tuple-element.50.normed, bf16[2048,512]{1,0:T(8,128)(2,1)} %go.1, bf16[2048,512]{1,0:T(8,128)(2,1)} %emb.5, ...), custom_call_target="tpu_custom_call" | custom-call | flops 20000000000 | bytes 20000000 | tf_op jit(solution)/shard_map/layer/pallas_call | solution.py:204
  64.0 7.5 %bucket_rows.1.after = bf16[4,32,72,128]{3,2,1,0:T(8,128)(2,1)} custom-call(s32[1,2048]{1,0:T(1,128)} %bitcast.15, s32[32,128]{1,0:T(8,128)} %labels.1.refs_0_, bf16[2048,512]{1,0:T(8,128)(2,1)} %get-tuple-element.56.tokens), custom_call_target="tpu_custom_call" | custom-call | flops 200000000 | bytes 1000000 | tf_op jit(solution)/shard_map/bucket_rows/pallas_call | solution.py:301
  71.5 8.0 %all-to-all-start = ((bf16[128,72,128]{2,1,0:T(8,128)(2,1)}), bf16[128,72,128]{2,1,0:T(8,128)(2,1)S(1)}, u32[]{:S(2)}, u32[]{:S(2)}) async-start(bf16[128,72,128]{2,1,0:T(8,128)(2,1)} %bitcast.14), calls=%async_computation | async-start | bytes 4718592 | tf_op jit(solution)/shard_map/all_to_all | solution.py:558
  79.5 9.7 %weight_grads.1 = (bf16[512,1280]{1,0:T(8,128)(2,1)}, bf16[512,1280]{1,0:T(8,128)(2,1)}) custom-call(s32[4]{0:T(128)} %pad_add_fusion.coords.place, bf16[512,2048]{1,0:T(8,128)(2,1)} %get-tuple-element.49.turned, bf16[2048,2048]{1,0:T(8,128)(2,1)} %get-tuple-element.53.gp, f32[512,512]{1,0:T(8,128)} %get-tuple-element.54.gwout, ...), custom_call_target="tpu_custom_call" | custom-call | flops 4300000256 | bytes 13000000 | tf_op jit(solution)/shard_map/weight_grads/pallas_call | solution.py:258
  90.3 2.9 %collective-permute-done.8.refs_1_ = bf16[512,1280]{1,0:T(8,128)(2,1)S(1)} collective-permute-done((bf16[512,1280]{1,0:T(8,128)(2,1)}, bf16[512,1280]{1,0:T(8,128)(2,1)S(1)}, u32[]{:S(2)}, u32[]{:S(2)}) %collective-permute-start.8) | collective-permute-done | bytes 1310752 | tf_op jit(solution)/shard_map/ppermute | solution.py:436
  94.5 1.6 %add_cores.1 = (bf16[128,1280]{1,0:T(8,128)(2,1)}, bf16[128,1280]{1,0:T(8,128)(2,1)}, bf16[128,1280]{1,0:T(8,128)(2,1)}, bf16[128,1280]{1,0:T(8,128)(2,1)S(1)}) custom-call(s32[4]{0:T(128)S(1)} %copy-done.1, bf16[512,1280]{1,0:T(8,128)(2,1)S(1)} %copy-done, bf16[512,1280]{1,0:T(8,128)(2,1)S(1)} %collective-permute-done.8.refs_1_), custom_call_target="tpu_custom_call" | custom-call | flops 1000000 | bytes 2000000 | tf_op jit(solution)/shard_map/add_cores/pallas_call | solution.py:445
  96.8 2.0 %collective-permute-start.10 = (bf16[128,1280]{1,0:T(8,128)(2,1)}, bf16[128,1280]{1,0:T(8,128)(2,1)S(1)}, u32[]{:S(2)}, u32[]{:S(2)}) collective-permute-start(bf16[128,1280]{1,0:T(8,128)(2,1)} %get-tuple-element.61), channel_id=1, source_target_pairs={{0,96},{32,0},{64,32},{96,64},{1,97},{33,1},{65,33},{97,65},{2,98}... | collective-permute-start | bytes 983048 | tf_op jit(solution)/shard_map/ppermute | solution.py:424
  99.8 13.0 %all-to-all-done.rows = bf16[128,72,128]{2,1,0:T(8,128)(2,1)S(1)} async-done(((bf16[128,72,128]{2,1,0:T(8,128)(2,1)}), bf16[128,72,128]{2,1,0:T(8,128)(2,1)S(1)}, u32[]{:S(2)}, u32[]{:S(2)}) %all-to-all-start) | async-done | bytes 2359328 | tf_op jit(solution)/shard_map/all_to_all | solution.py:558
  112.8 9.1 %scatter.3 = (f32[4104,128]{1,0:T(8,128)S(1)}, f32[4104,128]{1,0:T(8,128)S(1)}, f32[8,128]{1,0:T(8,128)S(1)}) custom-call(bf16[128,72,128]{2,1,0:T(8,128)(2,1)S(1)} %all-to-all-done.rows), custom_call_target="tpu_custom_call" | custom-call | flops 2000000 | bytes 6000000 | tf_op jit(solution)/shard_map/scatter/pallas_call | solution.py:407
  124.3 1.5 collective-permute-start.13
  127.7 3.2 %collective-permute-done.14.refs_3_ = bf16[32,1280]{1,0:T(8,128)(2,1)S(1)} collective-permute-done((bf16[32,1280]{1,0:T(8,128)(2,1)S(1)}, bf16[32,1280]{1,0:T(8,128)(2,1)S(1)}, u32[]{:S(2)}, u32[]{:S(2)}) %collective-permute-start.14) | collective-permute-done | bytes 81952 | tf_op jit(solution)/shard_map/ppermute | solution.py:432
  131.4 3.3 %collective-permute-start.17 = (bf16[32,1280]{1,0:T(8,128)(2,1)S(1)}, bf16[32,1280]{1,0:T(8,128)(2,1)S(1)}, u32[]{:S(2)}, u32[]{:S(2)}) collective-permute-start(bf16[32,1280]{1,0:T(8,128)(2,1)S(1)} %add_y.1.refs_2_.refs_0_), channel_id=1, source_target_pairs={{0,4},{1,5},{2,6},{3,7},{4,0},{5,1},{6,2},{7,3},{8,12},{9,13},{10,... | collective-permute-start | bytes 245768 | tf_op jit(solution)/shard_map/ppermute | solution.py:432
  136.2 2.0 %scatter.4 = (f32[4104,128]{1,0:T(8,128)S(1)}, f32[4104,128]{1,0:T(8,128)S(1)}, f32[8,128]{1,0:T(8,128)S(1)}) custom-call(bf16[128,72,128]{2,1,0:T(8,128)(2,1)S(1)} %all-to-all-done.rows, f32[4104,128]{1,0:T(8,128)S(1)} %get-tuple-element.68.refs_0_, f32[4104,128]{1,0:T(8,128)S(1)} %get-tuple-element.69.refs_1_, bf16[32,1280]{1,0:T(8,128)(2,1)S(1)} %add_y.1.refs_2_.refs_0_), custom_call_target="tpu_custom_call" | custom-call | flops 2000000 | bytes 6000000 | tf_op jit(solution)/shard_map/scatter/pallas_call | solution.py:407
  138.2 2.5 %collective-permute-done.15.refs_1_ = bf16[32,1280]{1,0:T(8,128)(2,1)S(1)} collective-permute-done((bf16[32,1280]{1,0:T(8,128)(2,1)S(1)}, bf16[32,1280]{1,0:T(8,128)(2,1)S(1)}, u32[]{:S(2)}, u32[]{:S(2)}) %collective-permute-start.15) | collective-permute-done | bytes 81952 | tf_op jit(solution)/shard_map/ppermute | solution.py:432
  143.9 3.6 %scatter.5 = (f32[4096,128]{1,0:T(8,128)}, f32[8,128]{1,0:T(8,128)S(1)}) custom-call(bf16[128,72,128]{2,1,0:T(8,128)(2,1)S(1)} %all-to-all-done.rows, f32[4104,128]{1,0:T(8,128)S(1)} %get-tuple-element.71.refs_0_, f32[4104,128]{1,0:T(8,128)S(1)} %get-tuple-element.72.refs_1_, bf16[32,1280]{1,0:T(8,128)(2,1)S(1)} %add_z.1.refs_2_.refs_0_), custom_call_target="tpu_custom_call" | custom-call | flops 2000000 | bytes 6000000 | tf_op jit(solution)/shard_map/scatter/pallas_call | solution.py:407
  148.6 5.2 %collective-permute-start.21 = (bf16[128,1280]{1,0:T(8,128)(2,1)S(1)}, bf16[128,1280]{1,0:T(8,128)(2,1)S(1)}, u32[]{:S(2)}, u32[]{:S(2)}) collective-permute-start(bf16[128,1280]{1,0:T(8,128)(2,1)S(1)} %join_y.1.refs_0_), channel_id=1, source_target_pairs={{0,1},{1,0},{2,3},{3,2},{4,5},{5,4},{6,7},{7,6},{8,9},{9,8},{10,11... | collective-permute-start | bytes 983048 | tf_op jit(solution)/shard_map/ppermute | solution.py:436
  155.1 1.7 %join_cores.1 = (f32[128,2048]{1,0:T(8,128)}, f32[128,512]{1,0:T(8,128)}) custom-call(s32[4]{0:T(128)S(1)} %copy-done.1, bf16[128,1280]{1,0:T(8,128)(2,1)S(1)} %join_y.1.refs_0_, bf16[128,1280]{1,0:T(8,128)(2,1)S(1)} %collective-permute-done.21.refs_1_), custom_call_target="tpu_custom_call" | custom-call | flops 1000000 | bytes 2000000 | tf_op jit(solution)/shard_map/join_cores/pallas_call | solution.py:445
  (73 shorter events, 26.2 us)
Async XLA Ops:
  0.7 18.3 %copy-start.4 = (s32[2048]{0:T(1024)S(1)}, s32[2048]{0:T(1024)}, u32[]{:S(2)}) copy-start(s32[2048]{0:T(1024)} %param.14) | copy-start | bytes 24580
  2.5 9.8 %collective-permute-start.1 = (bf16[64,2560]{1,0:T(8,128)(2,1)S(1)}, bf16[64,2560]{1,0:T(8,128)(2,1)S(1)}, u32[]{:S(2)}, u32[]{:S(2)}) collective-permute-start(bf16[64,2560]{1,0:T(8,128)(2,1)S(1)} %pad_maximum_fusion), channel_id=1, source_target_pairs={{0,96},{32,0},{64,32},{96,64},{1,97},{33,1},{65,33},{97,65},{2,98}... | collective-permute-start | bytes 983048 | tf_op jit(solution)/shard_map/ppermute | solution.py:424
  5.9 9.5 %collective-permute-start = (bf16[64,2560]{1,0:T(8,128)(2,1)S(1)}, bf16[64,2560]{1,0:T(8,128)(2,1)S(1)}, u32[]{:S(2)}, u32[]{:S(2)}) collective-permute-start(bf16[64,2560]{1,0:T(8,128)(2,1)S(1)} %pad_maximum_fusion), channel_id=1, source_target_pairs={{0,32},{32,64},{64,96},{96,0},{1,33},{33,65},{65,97},{97,1},{2,34}... | collective-permute-start | bytes 983048 | tf_op jit(solution)/shard_map/ppermute | solution.py:424
  15.4 11.4 %collective-permute-start.4 = (bf16[64,2560]{1,0:T(8,128)(2,1)S(1)}, bf16[64,2560]{1,0:T(8,128)(2,1)S(1)}, u32[]{:S(2)}, u32[]{:S(2)}) collective-permute-start(bf16[64,2560]{1,0:T(8,128)(2,1)S(1)} %collective-permute-done.low), channel_id=1, source_target_pairs={{0,1},{1,0},{2,3},{3,2},{4,5},{5,4},{6,7},{7,6},{8,9},{9,8},{10,11... | collective-permute-start | bytes 983048 | tf_op jit(solution)/shard_map/ppermute | solution.py:436
  17.4 9.5 %collective-permute-start.5 = (bf16[64,2560]{1,0:T(8,128)(2,1)S(1)}, bf16[64,2560]{1,0:T(8,128)(2,1)S(1)}, u32[]{:S(2)}, u32[]{:S(2)}) collective-permute-start(bf16[64,2560]{1,0:T(8,128)(2,1)S(1)} %collective-permute-done.1.high), channel_id=1, source_target_pairs={{0,1},{1,0},{2,3},{3,2},{4,5},{5,4},{6,7},{7,6},{8,9},{9,8},{10,11... | collective-permute-start | bytes 983048 | tf_op jit(solution)/shard_map/ppermute | solution.py:436
  17.5 5.8 %collective-permute-start.3 = (bf16[32,2560]{1,0:T(8,128)(2,1)S(1)}, bf16[32,2560]{1,0:T(8,128)(2,1)S(1)}, u32[]{:S(2)}, u32[]{:S(2)}) collective-permute-start(bf16[32,2560]{1,0:T(8,128)(2,1)S(1)} %slice.15), channel_id=1, source_target_pairs={{0,96},{32,0},{64,32},{96,64},{1,97},{33,1},{65,33},{97,65},{2,98}... | collective-permute-start | bytes 491528 | tf_op jit(solution)/shard_map/ppermute | solution.py:424
  17.5 6.4 %collective-permute-start.2 = (bf16[32,2560]{1,0:T(8,128)(2,1)S(1)}, bf16[32,2560]{1,0:T(8,128)(2,1)S(1)}, u32[]{:S(2)}, u32[]{:S(2)}) collective-permute-start(bf16[32,2560]{1,0:T(8,128)(2,1)S(1)} %slice.14), channel_id=1, source_target_pairs={{0,32},{32,64},{64,96},{96,0},{1,33},{33,65},{65,97},{97,1},{2,34}... | collective-permute-start | bytes 491528 | tf_op jit(solution)/shard_map/ppermute | solution.py:424
  23.9 2.5 %collective-permute-start.6 = (bf16[32,2560]{1,0:T(8,128)(2,1)S(1)}, bf16[32,2560]{1,0:T(8,128)(2,1)S(1)}, u32[]{:S(2)}, u32[]{:S(2)}) collective-permute-start(bf16[32,2560]{1,0:T(8,128)(2,1)S(1)} %collective-permute-done.2.far_a), channel_id=1, source_target_pairs={{0,1},{1,0},{2,3},{3,2},{4,5},{5,4},{6,7},{7,6},{8,9},{9,8},{10,11... | collective-permute-start | bytes 491528 | tf_op jit(solution)/shard_map/ppermute | solution.py:436
  25.4 1.4 collective-permute-start.7
  71.5 41.3 %all-to-all-start = ((bf16[128,72,128]{2,1,0:T(8,128)(2,1)}), bf16[128,72,128]{2,1,0:T(8,128)(2,1)S(1)}, u32[]{:S(2)}, u32[]{:S(2)}) async-start(bf16[128,72,128]{2,1,0:T(8,128)(2,1)} %bitcast.14), calls=%async_computation | async-start | bytes 4718592 | tf_op jit(solution)/shard_map/all_to_all | solution.py:558
  89.2 3.9 %collective-permute-start.8 = (bf16[512,1280]{1,0:T(8,128)(2,1)}, bf16[512,1280]{1,0:T(8,128)(2,1)S(1)}, u32[]{:S(2)}, u32[]{:S(2)}) collective-permute-start(bf16[512,1280]{1,0:T(8,128)(2,1)} %get-tuple-element.58), channel_id=1, source_target_pairs={{0,1},{1,0},{2,3},{3,2},{4,5},{5,4},{6,7},{7,6},{8,9},{9,8},{10,11... | collective-permute-start | bytes 3932168 | tf_op jit(solution)/shard_map/ppermute | solution.py:436
  96.1 25.8 %collective-permute-start.9 = (bf16[128,1280]{1,0:T(8,128)(2,1)}, bf16[128,1280]{1,0:T(8,128)(2,1)S(1)}, u32[]{:S(2)}, u32[]{:S(2)}) collective-permute-start(bf16[128,1280]{1,0:T(8,128)(2,1)} %get-tuple-element.60), channel_id=1, source_target_pairs={{0,32},{32,64},{64,96},{96,0},{1,33},{33,65},{65,97},{97,1},{2,34}... | collective-permute-start | bytes 983048 | tf_op jit(solution)/shard_map/ppermute | solution.py:424
  96.8 25.1 %collective-permute-start.10 = (bf16[128,1280]{1,0:T(8,128)(2,1)}, bf16[128,1280]{1,0:T(8,128)(2,1)S(1)}, u32[]{:S(2)}, u32[]{:S(2)}) collective-permute-start(bf16[128,1280]{1,0:T(8,128)(2,1)} %get-tuple-element.61), channel_id=1, source_target_pairs={{0,96},{32,0},{64,32},{96,64},{1,97},{33,1},{65,33},{97,65},{2,98}... | collective-permute-start | bytes 983048 | tf_op jit(solution)/shard_map/ppermute | solution.py:424
  98.8 23.1 %collective-permute-start.11 = (bf16[128,1280]{1,0:T(8,128)(2,1)}, bf16[128,1280]{1,0:T(8,128)(2,1)}, u32[]{:S(2)}, u32[]{:S(2)}) collective-permute-start(bf16[128,1280]{1,0:T(8,128)(2,1)} %get-tuple-element.62), channel_id=1, source_target_pairs={{0,64},{32,96},{64,0},{96,32},{1,65},{33,97},{65,1},{97,33},{2,66}... | collective-permute-start | bytes 983048 | tf_op jit(solution)/shard_map/ppermute | solution.py:424
  123.1 4.6 %collective-permute-start.12 = (bf16[32,1280]{1,0:T(8,128)(2,1)S(1)}, bf16[32,1280]{1,0:T(8,128)(2,1)S(1)}, u32[]{:S(2)}, u32[]{:S(2)}) collective-permute-start(bf16[32,1280]{1,0:T(8,128)(2,1)S(1)} %get-tuple-element.65), channel_id=1, source_target_pairs={{0,8},{1,9},{2,10},{3,11},{4,12},{5,13},{6,14},{7,15},{8,16},{9,17... | collective-permute-start | bytes 245768 | tf_op jit(solution)/shard_map/ppermute | solution.py:432
  124.3 3.3 %collective-permute-start.13 = (bf16[32,1280]{1,0:T(8,128)(2,1)S(1)}, bf16[32,1280]{1,0:T(8,128)(2,1)S(1)}, u32[]{:S(2)}, u32[]{:S(2)}) collective-permute-start(bf16[32,1280]{1,0:T(8,128)(2,1)S(1)} %get-tuple-element.66), channel_id=1, source_target_pairs={{0,24},{1,25},{2,26},{3,27},{4,28},{5,29},{6,30},{7,31},{8,0},{9,1... | collective-permute-start | bytes 245768 | tf_op jit(solution)/shard_map/ppermute | solution.py:432
  125.9 5.0 %collective-permute-start.14 = (bf16[32,1280]{1,0:T(8,128)(2,1)S(1)}, bf16[32,1280]{1,0:T(8,128)(2,1)S(1)}, u32[]{:S(2)}, u32[]{:S(2)}) collective-permute-start(bf16[32,1280]{1,0:T(8,128)(2,1)S(1)} %get-tuple-element.67), channel_id=1, source_target_pairs={{0,16},{1,17},{2,18},{3,19},{4,20},{5,21},{6,22},{7,23},{8,24},{9,... | collective-permute-start | bytes 245768 | tf_op jit(solution)/shard_map/ppermute | solution.py:432
  131.4 6.8 %collective-permute-start.17 = (bf16[32,1280]{1,0:T(8,128)(2,1)S(1)}, bf16[32,1280]{1,0:T(8,128)(2,1)S(1)}, u32[]{:S(2)}, u32[]{:S(2)}) collective-permute-start(bf16[32,1280]{1,0:T(8,128)(2,1)S(1)} %add_y.1.refs_2_.refs_0_), channel_id=1, source_target_pairs={{0,4},{1,5},{2,6},{3,7},{4,0},{5,1},{6,2},{7,3},{8,12},{9,13},{10,... | collective-permute-start | bytes 245768 | tf_op jit(solution)/shard_map/ppermute | solution.py:432
  134.8 3.5 %collective-permute-start.16 = (bf16[32,1280]{1,0:T(8,128)(2,1)S(1)}, bf16[32,1280]{1,0:T(8,128)(2,1)S(1)}, u32[]{:S(2)}, u32[]{:S(2)}) collective-permute-start(bf16[32,1280]{1,0:T(8,128)(2,1)S(1)} %add_y.1.refs_2_.refs_0_), channel_id=1, source_target_pairs={{0,6},{1,7},{2,0},{3,1},{4,2},{5,3},{6,4},{7,5},{8,14},{9,15},{10,... | collective-permute-start | bytes 245768 | tf_op jit(solution)/shard_map/ppermute | solution.py:432
  135.4 5.4 %collective-permute-start.15 = (bf16[32,1280]{1,0:T(8,128)(2,1)S(1)}, bf16[32,1280]{1,0:T(8,128)(2,1)S(1)}, u32[]{:S(2)}, u32[]{:S(2)}) collective-permute-start(bf16[32,1280]{1,0:T(8,128)(2,1)S(1)} %add_y.1.refs_2_.refs_0_), channel_id=1, source_target_pairs={{0,2},{1,3},{2,4},{3,5},{4,6},{5,7},{6,0},{7,1},{8,10},{9,11},{10,... | collective-permute-start | bytes 245768 | tf_op jit(solution)/shard_map/ppermute | solution.py:432
  141.3 6.1 %collective-permute-start.20 = (bf16[32,1280]{1,0:T(8,128)(2,1)S(1)}, bf16[32,1280]{1,0:T(8,128)(2,1)S(1)}, u32[]{:S(2)}, u32[]{:S(2)}) collective-permute-start(bf16[32,1280]{1,0:T(8,128)(2,1)S(1)} %add_z.1.refs_2_.refs_0_), channel_id=1, source_target_pairs={{0,16},{1,17},{2,18},{3,19},{4,20},{5,21},{6,22},{7,23},{8,24},{9,... | collective-permute-start | bytes 245768 | tf_op jit(solution)/shard_map/ppermute | solution.py:432
  142.4 5.1 %collective-permute-start.19 = (bf16[32,1280]{1,0:T(8,128)(2,1)S(1)}, bf16[32,1280]{1,0:T(8,128)(2,1)S(1)}, u32[]{:S(2)}, u32[]{:S(2)}) collective-permute-start(bf16[32,1280]{1,0:T(8,128)(2,1)S(1)} %add_z.1.refs_2_.refs_0_), channel_id=1, source_target_pairs={{0,24},{1,25},{2,26},{3,27},{4,28},{5,29},{6,30},{7,31},{8,0},{9,1... | collective-permute-start | bytes 245768 | tf_op jit(solution)/shard_map/ppermute | solution.py:432
  143.5 4.5 %collective-permute-start.18 = (bf16[32,1280]{1,0:T(8,128)(2,1)S(1)}, bf16[32,1280]{1,0:T(8,128)(2,1)S(1)}, u32[]{:S(2)}, u32[]{:S(2)}) collective-permute-start(bf16[32,1280]{1,0:T(8,128)(2,1)S(1)} %add_z.1.refs_2_.refs_0_), channel_id=1, source_target_pairs={{0,8},{1,9},{2,10},{3,11},{4,12},{5,13},{6,14},{7,15},{8,16},{9,17... | collective-permute-start | bytes 245768 | tf_op jit(solution)/shard_map/ppermute | solution.py:432
  148.6 6.5 %collective-permute-start.21 = (bf16[128,1280]{1,0:T(8,128)(2,1)S(1)}, bf16[128,1280]{1,0:T(8,128)(2,1)S(1)}, u32[]{:S(2)}, u32[]{:S(2)}) collective-permute-start(bf16[128,1280]{1,0:T(8,128)(2,1)S(1)} %join_y.1.refs_0_), channel_id=1, source_target_pairs={{0,1},{1,0},{2,3},{3,2},{4,5},{5,4},{6,7},{7,6},{8,9},{9,8},{10,11... | collective-permute-start | bytes 983048 | tf_op jit(solution)/shard_map/ppermute | solution.py:436
  (12 other events, 65.2 us)

commit v5 on v4

--- a/solution.py
+++ b/solution.py
@@ -82,11 +82,36 @@
     )(embedded, after, *given)
 
 
+def fill_packets(bucket, labels, tokens, packets):
+    parts, owners, _, width = packets.shape
+    group = 8
+    tile, count = group * CAP, tokens.shape[0]
+
+    @pl.loop(0, owners // group)
+    def _(i):
+        slot = lax.broadcasted_iota(jnp.int32, (tile, count), 0) + i * tile
+        pick = jnp.where(slot == bucket[...], 1.0, 0.0).astype(BF)
+        sums = dot_nn(pick, tokens[...]).astype(BF)
+        numbers = labels[pl.ds(pl.multiple_of(i * group, group), group), :]
+        upper = lax.shift_right_logical(numbers, 6)
+        lower = pltpu.roll(jnp.bitwise_and(numbers, 63), CAP, 1)
+        lane = lax.broadcasted_iota(jnp.int32, numbers.shape, 1)
+        marks = jnp.where(lane < CAP, upper, lower).astype(F32).astype(BF)
+        for part in range(parts):
+            cols = slice(part * width, (part + 1) * width)
+            for owner in range(group):
+                place = i * group + owner
+                packets[part, place, 0:CAP, :] = sums[owner * CAP : (owner + 1) * CAP, cols]
+                packets[part, place, CAP:PACKET, :] = jnp.broadcast_to(
+                    marks[owner : owner + 1, :], (PACKET - CAP, width)
+                )
+
+
 def layer_kernel(
-    coords, lens, normed, go, emb, own_in, own_out,
+    coords, lens, bucket, labels, normed, go, emb, own_in, own_out,
     low, high, low_o, high_o, far_a, far_b, far_ao, far_bo,
-    gp, tokens, gwout,
-    w, w_turned, slope, hidden, probs, rates, mixed, cot, seq_sum,
+    gp, gwout, packets,
+    w, w_turned, tokens, slope, hidden, probs, rates, mixed, cot, seq_sum,
 ):
     step = pl.program_id(0)
 
@@ -188,11 +213,17 @@
 
     xhat, rstd = normalise(emb[...].astype(F32))
     back = norm_back(xhat, rstd, dot_nn(gp[...], w_turned[...]))
-    tokens[...] = (back + go[...].astype(F32)).astype(BF)
-
-
-def run_layer(coords, lengths, normed, embedded, grad_out, pieces):
+    here = pl.ds(pl.multiple_of(step * SEQ, SEQ), SEQ)
+    tokens[here, :] = (back + go[...].astype(F32)).astype(BF)
+
+    @pl.when(step == pl.num_programs(0) - 1)
+    def _():
+        fill_packets(bucket, labels, tokens, packets)
+
+
+def run_layer(coords, lengths, bucket, labels, normed, embedded, grad_out, pieces, parts):
     tokens = normed.shape[0]
+    packets = (parts, labels.shape[0], PACKET, WIDTH // parts)
     smem = pl.BlockSpec(memory_space=pltpu.SMEM)
 
     def whole(shape):
@@ -204,16 +235,23 @@
     return pl.pallas_call(
         layer_kernel,
         grid=(tokens // SEQ,),
-        in_specs=[smem, smem] + [by_seq(WIDTH)] * 3 + [whole(p.shape) for p in pieces],
-        out_specs=[by_seq(4 * WIDTH), by_seq(WIDTH), whole((WIDTH, WIDTH))],
+        in_specs=[smem, smem, whole(bucket.shape), whole(labels.shape)]
+        + [by_seq(WIDTH)] * 3
+        + [whole(p.shape) for p in pieces],
+        out_specs=[
+            by_seq(4 * WIDTH),
+            whole((WIDTH, WIDTH)),
+            pl.BlockSpec(packets, lambda i: (0, 0, 0, 0)),
+        ],
         out_shape=[
             jax.ShapeDtypeStruct((tokens, 4 * WIDTH), BF),
-            jax.ShapeDtypeStruct((tokens, WIDTH), BF),
             jax.ShapeDtypeStruct((WIDTH, WIDTH), F32),
+            jax.ShapeDtypeStruct(packets, BF),
         ],
         scratch_shapes=[
             pltpu.VMEM((WIDTH, 5 * WIDTH), BF),
             pltpu.VMEM((4 * WIDTH, WIDTH), BF),
+            pltpu.VMEM((tokens, WIDTH), BF),
             pltpu.VMEM((SEQ, 4 * WIDTH), F32),
             pltpu.VMEM((SEQ, 4 * WIDTH), BF),
             pltpu.VMEM((HEADS, SEQ, SEQ), BF),
@@ -227,7 +265,7 @@
             flops=20_000_000_000, bytes_accessed=20_000_000, transcendentals=8_000_000
         ),
         name="layer",
-    )(coords, lengths, normed, grad_out, embedded, *pieces)
+    )(coords, lengths, bucket, labels, normed, grad_out, embedded, *pieces)
 
 
 def weight_kernel(coords, turned, gp, gwout, after, mine, other):
@@ -273,47 +311,6 @@
         ),
         name="weight_grads",
     )(coords, turned, grad_proj, gwout, after)
-
-
-def bucket_kernel(bucket, labels, tokens, out):
-    owners = out.shape[1]
-    tile, count = owners * CAP, tokens.shape[0]
-    slot = lax.broadcasted_iota(jnp.int32, (tile, count), 0) + pl.program_id(0) * tile
-    pick = jnp.where(slot == bucket[...], 1.0, 0.0).astype(BF)
-    sums = dot_nn(pick, tokens[...]).astype(BF)
-    upper = lax.shift_right_logical(labels[...], 6)
-    lower = jnp.bitwise_and(labels[...], 63)
-    lane = lax.broadcasted_iota(jnp.int32, labels.shape, 1)
-    marks = jnp.where(lane < CAP, upper, pltpu.roll(lower, CAP, 1)).astype(F32).astype(BF)
-    for part in range(out.shape[0]):
-        for owner in range(owners):
-            cols = slice(part * 128, (part + 1) * 128)
-            out[part, owner, 0:CAP, :] = sums[owner * CAP : (owner + 1) * CAP, cols]
-            out[part, owner, CAP:PACKET, :] = jnp.broadcast_to(
-                marks[owner : owner + 1, :], (PACKET - CAP, 128)
-            )
-
-
-def run_buckets(bucket, labels, tokens, parts):
-    count, width = tokens.shape
-    owners = labels.shape[0]
-    per_step = 8
-    return pl.pallas_call(
-        bucket_kernel,
-        grid=(owners // per_step,),
-        in_specs=[
-            pl.BlockSpec((1, count), lambda i: (0, 0)),
-            pl.BlockSpec((per_step, 128), lambda i: (i, 0)),
-            pl.BlockSpec((count, width), lambda i: (0, 0)),
-        ],
-        out_specs=pl.BlockSpec((parts, per_step, PACKET, 128), lambda i: (0, i, 0, 0)),
-        out_shape=jax.ShapeDtypeStruct((parts, owners, PACKET, 128), BF),
-        compiler_params=pltpu.CompilerParams(vmem_limit_bytes=56 * 1024 * 1024),
-        cost_estimate=pl.CostEstimate(
-            flops=200_000_000, bytes_accessed=1_000_000, transcendentals=0
-        ),
-        name="bucket_rows",
-    )(bucket, labels, tokens)
 
 
 def label_kernel(counts, offsets, rows, out):
@@ -550,10 +547,9 @@
     far_ao, far_bo = swap(far_a, 1, table_count), swap(far_b, 1, table_count)
     pieces = [w_in, w_out, low, high, low_o, high_o, far_a, far_b, far_ao, far_bo]
 
-    grad_proj, tokens, gwout = run_layer(
-        coords, lengths, normed, embedded, grad_out, pieces
-    )
-    bucket_rows = run_buckets(bucket, labels, tokens, fsdp_count)
+    grad_proj, gwout, bucket_rows = run_layer(
+        coords, lengths, bucket, labels, normed, embedded, grad_out, pieces, fsdp_count
+    )
     values = bucket_rows.reshape(fsdp_count * table_count, PACKET, 128)
     got = lax.all_to_all(values, BOTH, split_axis=0, concat_axis=0, tiled=True)
 

time: 157 us -> 156 us (level)
    pallas_call x2 -> x1, Pallas kernels: 43.1 us -> 42.2 us  [run_layer(): pl.pallas_call(layer_kernel, grid=(tokens // SEQ,), in_specs=[smem, smem,...]
where the time goes in v5:
time: 156 us
  Pallas kernels  80.2 us (51%)
  starting transfers between devices  37.9 us (24%)
  waiting for transfers between devices  29.4 us (19%)
  local copies, waits for them, and re-layouts  5.96 us (4%)
    pallas_call x1, Pallas kernels, run_layer(): pl.pallas_call(layer_kernel, grid=(tokens // SEQ,), in_specs=[smem, smem,...  42.2 us
    pallas_call x3, Pallas kernels, run_scatter(): pl.pallas_call(functools.partial(scatter_kernel, first, last), grid=(1,),...  14.8 us
    all_to_all x1, waiting for transfers between devices, per_device(): got = lax.all_to_all(values, BOTH, split_axis=0, concat_axis=0, tiled=True)  13 us
    ppermute x9, starting transfers between devices, table_ring(): return lax.ppermute(array, 'table', pairs)  11.5 us
    ppermute x6, starting transfers between devices, swap(): return lax.ppermute(array, 'table', [(i, i ^ bit) for i in range(count)])  9.86 us
    pallas_call x1, Pallas kernels, run_weights(): pl.pallas_call(weight_kernel, grid=(4,), in_specs=[pl.BlockSpec(memory_sp...  9.7 us
    ppermute x7, starting transfers between devices, ring(): lax.ppermute(array, axis, [(i, (i + shift) % size) for i in range(size)])  8.56 us
    all_to_all x1, starting transfers between devices, per_device(): got = lax.all_to_all(values, BOTH, split_axis=0, concat_axis=0, tiled=True)  7.98 us
  transfers between devices with their start and end apart: 23, of which 12 were waited for; matrix products, arithmetic and copies ran while one was open for 2% of the time, Pallas kernels for 21%

profile of v5, /device:TPU:1, one launch (start us, length us, event | category | flops | bytes accessed | tf_op | source)
XLA Modules:
  0.0 155.7 jit_solution(10666357367858153968)
XLA Ops:
  2.5 3.4 %collective-permute-start.1 = (bf16[64,2560]{1,0:T(8,128)(2,1)S(1)}, bf16[64,2560]{1,0:T(8,128)(2,1)S(1)}, u32[]{:S(2)}, u32[]{:S(2)}) collective-permute-start(bf16[64,2560]{1,0:T(8,128)(2,1)S(1)} %pad_maximum_fusion), channel_id=1, source_target_pairs={{0,96},{32,0},{64,32},{96,64},{1,97},{33,1},{65,33},{97,65},{2,98}... | collective-permute-start | bytes 983048 | tf_op jit(solution)/shard_map/ppermute | solution.py:421
  7.2 1.6 %labels.1.refs_0_ = s32[32,128]{1,0:T(8,128)} custom-call(s32[32]{0:T(128)} %bitcast.16, s32[32]{0:T(128)} %bitcast.17, s32[21,128]{1,0:T(8,128)} %pad_bitcast_fusion.rows), custom_call_target="tpu_custom_call" | custom-call | flops 10000 | bytes 10000 | tf_op jit(solution)/shard_map/labels/pallas_call | solution.py:331
  8.8 2.8 %norm.2 = (bf16[2048,512]{1,0:T(8,128)(2,1)}, bf16[512,2048]{1,0:T(8,128)(2,1)}) custom-call(bf16[2048,512]{1,0:T(8,128)(2,1)} %emb.5, s32[32,128]{1,0:T(8,128)} %labels.1.refs_0_), custom_call_target="tpu_custom_call" | custom-call | flops 10000000 | bytes 3000000 | tf_op jit(solution)/shard_map/norm/pallas_call | solution.py:63
  12.3 3.1 %collective-permute-done.low = bf16[64,2560]{1,0:T(8,128)(2,1)S(1)} collective-permute-done((bf16[64,2560]{1,0:T(8,128)(2,1)S(1)}, bf16[64,2560]{1,0:T(8,128)(2,1)S(1)}, u32[]{:S(2)}, u32[]{:S(2)}) %collective-permute-start) | collective-permute-done | bytes 327712 | tf_op jit(solution)/shard_map/ppermute | solution.py:421
  15.4 1.9 %collective-permute-start.4 = (bf16[64,2560]{1,0:T(8,128)(2,1)S(1)}, bf16[64,2560]{1,0:T(8,128)(2,1)S(1)}, u32[]{:S(2)}, u32[]{:S(2)}) collective-permute-start(bf16[64,2560]{1,0:T(8,128)(2,1)S(1)} %collective-permute-done.low), channel_id=1, source_target_pairs={{0,1},{1,0},{2,3},{3,2},{4,5},{5,4},{6,7},{7,6},{8,9},{9,8},{10,11... | collective-permute-start | bytes 983048 | tf_op jit(solution)/shard_map/ppermute | solution.py:433
  17.5 1.5 collective-permute-start.2
  20.3 2.9 %norm.3 = (bf16[2048,512]{1,0:T(8,128)(2,1)}, bf16[512,2048]{1,0:T(8,128)(2,1)}) custom-call(bf16[2048,512]{1,0:T(8,128)(2,1)} %emb.5, s32[32,128]{1,0:T(8,128)} %labels.1.refs_0_, bf16[2048,512]{1,0:T(8,128)(2,1)} %get-tuple-element.44.refs_1_, bf16[512,2048]{1,0:T(8,128)(2,1)} %get-tuple-element.45.refs_2_), custom_call_target="tpu_custom_call", output_to_operand_aliasing={{0}: (2, {}), {1}: (3, {})} | custom-call | flops 10000000 | bytes 3000000 | tf_op jit(solution)/shard_map/norm/pallas_call | solution.py:63
  23.9 1.5 collective-permute-start.6
  28.3 42.2 %layer.1 = (bf16[2048,2048]{1,0:T(8,128)(2,1)}, f32[512,512]{1,0:T(8,128)}, bf16[4,32,72,128]{3,2,1,0:T(8,128)(2,1)}) custom-call(s32[4]{0:T(128)} %pad_add_fusion.coords.place, s32[4]{0:T(128)} %lens.1, s32[1,2048]{1,0:T(1,128)} %bitcast.15, s32[32,128]{1,0:T(8,128)} %labels.1.refs_0_, bf16[2048,512]{1,0:T(8,128)(2,1)} %get-tuple-element.51.normed, ...), custom_call_target="tpu_custom_call" | custom-call | flops 20000000000 | bytes 20000000 | tf_op jit(solution)/shard_map/layer/pallas_call | solution.py:235
  70.5 8.0 %all-to-all-start = ((bf16[128,72,128]{2,1,0:T(8,128)(2,1)}), bf16[128,72,128]{2,1,0:T(8,128)(2,1)S(1)}, u32[]{:S(2)}, u32[]{:S(2)}) async-start(bf16[128,72,128]{2,1,0:T(8,128)(2,1)} %bitcast.14), calls=%async_computation | async-start | bytes 4718592 | tf_op jit(solution)/shard_map/all_to_all | solution.py:554
  78.5 9.7 %weight_grads.1 = (bf16[512,1280]{1,0:T(8,128)(2,1)}, bf16[512,1280]{1,0:T(8,128)(2,1)}) custom-call(s32[4]{0:T(128)} %pad_add_fusion.coords.place, bf16[512,2048]{1,0:T(8,128)(2,1)} %get-tuple-element.49.turned, bf16[2048,2048]{1,0:T(8,128)(2,1)} %get-tuple-element.54.gp, f32[512,512]{1,0:T(8,128)} %get-tuple-element.55.gwout, ...), custom_call_target="tpu_custom_call" | custom-call | flops 4300000256 | bytes 13000000 | tf_op jit(solution)/shard_map/weight_grads/pallas_call | solution.py:296
  89.3 2.9 %collective-permute-done.8.refs_1_ = bf16[512,1280]{1,0:T(8,128)(2,1)S(1)} collective-permute-done((bf16[512,1280]{1,0:T(8,128)(2,1)}, bf16[512,1280]{1,0:T(8,128)(2,1)S(1)}, u32[]{:S(2)}, u32[]{:S(2)}) %collective-permute-start.8) | collective-permute-done | bytes 1310752 | tf_op jit(solution)/shard_map/ppermute | solution.py:433
  93.5 1.6 %add_cores.1 = (bf16[128,1280]{1,0:T(8,128)(2,1)}, bf16[128,1280]{1,0:T(8,128)(2,1)}, bf16[128,1280]{1,0:T(8,128)(2,1)}, bf16[128,1280]{1,0:T(8,128)(2,1)S(1)}) custom-call(s32[4]{0:T(128)S(1)} %copy-done.1, bf16[512,1280]{1,0:T(8,128)(2,1)S(1)} %copy-done, bf16[512,1280]{1,0:T(8,128)(2,1)S(1)} %collective-permute-done.8.refs_1_), custom_call_target="tpu_custom_call" | custom-call | flops 1000000 | bytes 2000000 | tf_op jit(solution)/shard_map/add_cores/pallas_call | solution.py:442
  95.8 2.0 %collective-permute-start.10 = (bf16[128,1280]{1,0:T(8,128)(2,1)}, bf16[128,1280]{1,0:T(8,128)(2,1)S(1)}, u32[]{:S(2)}, u32[]{:S(2)}) collective-permute-start(bf16[128,1280]{1,0:T(8,128)(2,1)} %get-tuple-element.61), channel_id=1, source_target_pairs={{0,96},{32,0},{64,32},{96,64},{1,97},{33,1},{65,33},{97,65},{2,98}... | collective-permute-start | bytes 983048 | tf_op jit(solution)/shard_map/ppermute | solution.py:421
  98.8 13.0 %all-to-all-done.rows = bf16[128,72,128]{2,1,0:T(8,128)(2,1)S(1)} async-done(((bf16[128,72,128]{2,1,0:T(8,128)(2,1)}), bf16[128,72,128]{2,1,0:T(8,128)(2,1)S(1)}, u32[]{:S(2)}, u32[]{:S(2)}) %all-to-all-start) | async-done | bytes 2359328 | tf_op jit(solution)/shard_map/all_to_all | solution.py:554
  111.8 9.1 %scatter.3 = (f32[4104,128]{1,0:T(8,128)S(1)}, f32[4104,128]{1,0:T(8,128)S(1)}, f32[8,128]{1,0:T(8,128)S(1)}) custom-call(bf16[128,72,128]{2,1,0:T(8,128)(2,1)S(1)} %all-to-all-done.rows), custom_call_target="tpu_custom_call" | custom-call | flops 2000000 | bytes 6000000 | tf_op jit(solution)/shard_map/scatter/pallas_call | solution.py:404
  123.3 1.5 collective-permute-start.13
  126.7 3.1 %collective-permute-done.14.refs_3_ = bf16[32,1280]{1,0:T(8,128)(2,1)S(1)} collective-permute-done((bf16[32,1280]{1,0:T(8,128)(2,1)S(1)}, bf16[32,1280]{1,0:T(8,128)(2,1)S(1)}, u32[]{:S(2)}, u32[]{:S(2)}) %collective-permute-start.14) | collective-permute-done | bytes 81952 | tf_op jit(solution)/shard_map/ppermute | solution.py:429
  130.4 3.3 %collective-permute-start.17 = (bf16[32,1280]{1,0:T(8,128)(2,1)S(1)}, bf16[32,1280]{1,0:T(8,128)(2,1)S(1)}, u32[]{:S(2)}, u32[]{:S(2)}) collective-permute-start(bf16[32,1280]{1,0:T(8,128)(2,1)S(1)} %add_y.1.refs_2_.refs_0_), channel_id=1, source_target_pairs={{0,4},{1,5},{2,6},{3,7},{4,0},{5,1},{6,2},{7,3},{8,12},{9,13},{10,... | collective-permute-start | bytes 245768 | tf_op jit(solution)/shard_map/ppermute | solution.py:429
  135.2 2.0 %scatter.4 = (f32[4104,128]{1,0:T(8,128)S(1)}, f32[4104,128]{1,0:T(8,128)S(1)}, f32[8,128]{1,0:T(8,128)S(1)}) custom-call(bf16[128,72,128]{2,1,0:T(8,128)(2,1)S(1)} %all-to-all-done.rows, f32[4104,128]{1,0:T(8,128)S(1)} %get-tuple-element.68.refs_0_, f32[4104,128]{1,0:T(8,128)S(1)} %get-tuple-element.69.refs_1_, bf16[32,1280]{1,0:T(8,128)(2,1)S(1)} %add_y.1.refs_2_.refs_0_), custom_call_target="tpu_custom_call" | custom-call | flops 2000000 | bytes 6000000 | tf_op jit(solution)/shard_map/scatter/pallas_call | solution.py:404
  137.3 2.5 %collective-permute-done.15.refs_1_ = bf16[32,1280]{1,0:T(8,128)(2,1)S(1)} collective-permute-done((bf16[32,1280]{1,0:T(8,128)(2,1)S(1)}, bf16[32,1280]{1,0:T(8,128)(2,1)S(1)}, u32[]{:S(2)}, u32[]{:S(2)}) %collective-permute-start.15) | collective-permute-done | bytes 81952 | tf_op jit(solution)/shard_map/ppermute | solution.py:429
  142.9 3.7 %scatter.5 = (f32[4096,128]{1,0:T(8,128)}, f32[8,128]{1,0:T(8,128)S(1)}) custom-call(bf16[128,72,128]{2,1,0:T(8,128)(2,1)S(1)} %all-to-all-done.rows, f32[4104,128]{1,0:T(8,128)S(1)} %get-tuple-element.71.refs_0_, f32[4104,128]{1,0:T(8,128)S(1)} %get-tuple-element.72.refs_1_, bf16[32,1280]{1,0:T(8,128)(2,1)S(1)} %add_z.1.refs_2_.refs_0_), custom_call_target="tpu_custom_call" | custom-call | flops 2000000 | bytes 6000000 | tf_op jit(solution)/shard_map/scatter/pallas_call | solution.py:404
  147.6 5.2 %collective-permute-start.21 = (bf16[128,1280]{1,0:T(8,128)(2,1)S(1)}, bf16[128,1280]{1,0:T(8,128)(2,1)S(1)}, u32[]{:S(2)}, u32[]{:S(2)}) collective-permute-start(bf16[128,1280]{1,0:T(8,128)(2,1)S(1)} %join_y.1.refs_0_), channel_id=1, source_target_pairs={{0,1},{1,0},{2,3},{3,2},{4,5},{5,4},{6,7},{7,6},{8,9},{9,8},{10,11... | collective-permute-start | bytes 983048 | tf_op jit(solution)/shard_map/ppermute | solution.py:433
  154.1 1.7 %join_cores.1 = (f32[128,2048]{1,0:T(8,128)}, f32[128,512]{1,0:T(8,128)}) custom-call(s32[4]{0:T(128)S(1)} %copy-done.1, bf16[128,1280]{1,0:T(8,128)(2,1)S(1)} %join_y.1.refs_0_, bf16[128,1280]{1,0:T(8,128)(2,1)S(1)} %collective-permute-done.21.refs_1_), custom_call_target="tpu_custom_call" | custom-call | flops 1000000 | bytes 2000000 | tf_op jit(solution)/shard_map/join_cores/pallas_call | solution.py:442
  (72 shorter events, 24.6 us)
Async XLA Ops:
  0.7 18.3 %copy-start.4 = (s32[2048]{0:T(1024)S(1)}, s32[2048]{0:T(1024)}, u32[]{:S(2)}) copy-start(s32[2048]{0:T(1024)} %param.14) | copy-start | bytes 24580
  2.5 9.8 %collective-permute-start.1 = (bf16[64,2560]{1,0:T(8,128)(2,1)S(1)}, bf16[64,2560]{1,0:T(8,128)(2,1)S(1)}, u32[]{:S(2)}, u32[]{:S(2)}) collective-permute-start(bf16[64,2560]{1,0:T(8,128)(2,1)S(1)} %pad_maximum_fusion), channel_id=1, source_target_pairs={{0,96},{32,0},{64,32},{96,64},{1,97},{33,1},{65,33},{97,65},{2,98}... | collective-permute-start | bytes 983048 | tf_op jit(solution)/shard_map/ppermute | solution.py:421
  5.9 9.5 %collective-permute-start = (bf16[64,2560]{1,0:T(8,128)(2,1)S(1)}, bf16[64,2560]{1,0:T(8,128)(2,1)S(1)}, u32[]{:S(2)}, u32[]{:S(2)}) collective-permute-start(bf16[64,2560]{1,0:T(8,128)(2,1)S(1)} %pad_maximum_fusion), channel_id=1, source_target_pairs={{0,32},{32,64},{64,96},{96,0},{1,33},{33,65},{65,97},{97,1},{2,34}... | collective-permute-start | bytes 983048 | tf_op jit(solution)/shard_map/ppermute | solution.py:421
  15.4 11.4 %collective-permute-start.4 = (bf16[64,2560]{1,0:T(8,128)(2,1)S(1)}, bf16[64,2560]{1,0:T(8,128)(2,1)S(1)}, u32[]{:S(2)}, u32[]{:S(2)}) collective-permute-start(bf16[64,2560]{1,0:T(8,128)(2,1)S(1)} %collective-permute-done.low), channel_id=1, source_target_pairs={{0,1},{1,0},{2,3},{3,2},{4,5},{5,4},{6,7},{7,6},{8,9},{9,8},{10,11... | collective-permute-start | bytes 983048 | tf_op jit(solution)/shard_map/ppermute | solution.py:433
  17.4 9.5 %collective-permute-start.5 = (bf16[64,2560]{1,0:T(8,128)(2,1)S(1)}, bf16[64,2560]{1,0:T(8,128)(2,1)S(1)}, u32[]{:S(2)}, u32[]{:S(2)}) collective-permute-start(bf16[64,2560]{1,0:T(8,128)(2,1)S(1)} %collective-permute-done.1.high), channel_id=1, source_target_pairs={{0,1},{1,0},{2,3},{3,2},{4,5},{5,4},{6,7},{7,6},{8,9},{9,8},{10,11... | collective-permute-start | bytes 983048 | tf_op jit(solution)/shard_map/ppermute | solution.py:433
  17.5 5.7 %collective-permute-start.3 = (bf16[32,2560]{1,0:T(8,128)(2,1)S(1)}, bf16[32,2560]{1,0:T(8,128)(2,1)S(1)}, u32[]{:S(2)}, u32[]{:S(2)}) collective-permute-start(bf16[32,2560]{1,0:T(8,128)(2,1)S(1)} %slice.15), channel_id=1, source_target_pairs={{0,96},{32,0},{64,32},{96,64},{1,97},{33,1},{65,33},{97,65},{2,98}... | collective-permute-start | bytes 491528 | tf_op jit(solution)/shard_map/ppermute | solution.py:421
  17.5 6.4 %collective-permute-start.2 = (bf16[32,2560]{1,0:T(8,128)(2,1)S(1)}, bf16[32,2560]{1,0:T(8,128)(2,1)S(1)}, u32[]{:S(2)}, u32[]{:S(2)}) collective-permute-start(bf16[32,2560]{1,0:T(8,128)(2,1)S(1)} %slice.14), channel_id=1, source_target_pairs={{0,32},{32,64},{64,96},{96,0},{1,33},{33,65},{65,97},{97,1},{2,34}... | collective-permute-start | bytes 491528 | tf_op jit(solution)/shard_map/ppermute | solution.py:421
  23.9 2.5 %collective-permute-start.6 = (bf16[32,2560]{1,0:T(8,128)(2,1)S(1)}, bf16[32,2560]{1,0:T(8,128)(2,1)S(1)}, u32[]{:S(2)}, u32[]{:S(2)}) collective-permute-start(bf16[32,2560]{1,0:T(8,128)(2,1)S(1)} %collective-permute-done.2.far_a), channel_id=1, source_target_pairs={{0,1},{1,0},{2,3},{3,2},{4,5},{5,4},{6,7},{7,6},{8,9},{9,8},{10,11... | collective-permute-start | bytes 491528 | tf_op jit(solution)/shard_map/ppermute | solution.py:433
  25.4 1.4 collective-permute-start.7
  70.5 41.3 %all-to-all-start = ((bf16[128,72,128]{2,1,0:T(8,128)(2,1)}), bf16[128,72,128]{2,1,0:T(8,128)(2,1)S(1)}, u32[]{:S(2)}, u32[]{:S(2)}) async-start(bf16[128,72,128]{2,1,0:T(8,128)(2,1)} %bitcast.14), calls=%async_computation | async-start | bytes 4718592 | tf_op jit(solution)/shard_map/all_to_all | solution.py:554
  88.2 3.9 %collective-permute-start.8 = (bf16[512,1280]{1,0:T(8,128)(2,1)}, bf16[512,1280]{1,0:T(8,128)(2,1)S(1)}, u32[]{:S(2)}, u32[]{:S(2)}) collective-permute-start(bf16[512,1280]{1,0:T(8,128)(2,1)} %get-tuple-element.58), channel_id=1, source_target_pairs={{0,1},{1,0},{2,3},{3,2},{4,5},{5,4},{6,7},{7,6},{8,9},{9,8},{10,11... | collective-permute-start | bytes 3932168 | tf_op jit(solution)/shard_map/ppermute | solution.py:433
  95.1 25.8 %collective-permute-start.9 = (bf16[128,1280]{1,0:T(8,128)(2,1)}, bf16[128,1280]{1,0:T(8,128)(2,1)S(1)}, u32[]{:S(2)}, u32[]{:S(2)}) collective-permute-start(bf16[128,1280]{1,0:T(8,128)(2,1)} %get-tuple-element.60), channel_id=1, source_target_pairs={{0,32},{32,64},{64,96},{96,0},{1,33},{33,65},{65,97},{97,1},{2,34}... | collective-permute-start | bytes 983048 | tf_op jit(solution)/shard_map/ppermute | solution.py:421
  95.8 25.1 %collective-permute-start.10 = (bf16[128,1280]{1,0:T(8,128)(2,1)}, bf16[128,1280]{1,0:T(8,128)(2,1)S(1)}, u32[]{:S(2)}, u32[]{:S(2)}) collective-permute-start(bf16[128,1280]{1,0:T(8,128)(2,1)} %get-tuple-element.61), channel_id=1, source_target_pairs={{0,96},{32,0},{64,32},{96,64},{1,97},{33,1},{65,33},{97,65},{2,98}... | collective-permute-start | bytes 983048 | tf_op jit(solution)/shard_map/ppermute | solution.py:421
  97.8 23.2 %collective-permute-start.11 = (bf16[128,1280]{1,0:T(8,128)(2,1)}, bf16[128,1280]{1,0:T(8,128)(2,1)}, u32[]{:S(2)}, u32[]{:S(2)}) collective-permute-start(bf16[128,1280]{1,0:T(8,128)(2,1)} %get-tuple-element.62), channel_id=1, source_target_pairs={{0,64},{32,96},{64,0},{96,32},{1,65},{33,97},{65,1},{97,33},{2,66}... | collective-permute-start | bytes 983048 | tf_op jit(solution)/shard_map/ppermute | solution.py:421
  122.1 4.6 %collective-permute-start.12 = (bf16[32,1280]{1,0:T(8,128)(2,1)S(1)}, bf16[32,1280]{1,0:T(8,128)(2,1)S(1)}, u32[]{:S(2)}, u32[]{:S(2)}) collective-permute-start(bf16[32,1280]{1,0:T(8,128)(2,1)S(1)} %get-tuple-element.65), channel_id=1, source_target_pairs={{0,8},{1,9},{2,10},{3,11},{4,12},{5,13},{6,14},{7,15},{8,16},{9,17... | collective-permute-start | bytes 245768 | tf_op jit(solution)/shard_map/ppermute | solution.py:429
  123.3 3.4 %collective-permute-start.13 = (bf16[32,1280]{1,0:T(8,128)(2,1)S(1)}, bf16[32,1280]{1,0:T(8,128)(2,1)S(1)}, u32[]{:S(2)}, u32[]{:S(2)}) collective-permute-start(bf16[32,1280]{1,0:T(8,128)(2,1)S(1)} %get-tuple-element.66), channel_id=1, source_target_pairs={{0,24},{1,25},{2,26},{3,27},{4,28},{5,29},{6,30},{7,31},{8,0},{9,1... | collective-permute-start | bytes 245768 | tf_op jit(solution)/shard_map/ppermute | solution.py:429
  124.9 5.0 %collective-permute-start.14 = (bf16[32,1280]{1,0:T(8,128)(2,1)S(1)}, bf16[32,1280]{1,0:T(8,128)(2,1)S(1)}, u32[]{:S(2)}, u32[]{:S(2)}) collective-permute-start(bf16[32,1280]{1,0:T(8,128)(2,1)S(1)} %get-tuple-element.67), channel_id=1, source_target_pairs={{0,16},{1,17},{2,18},{3,19},{4,20},{5,21},{6,22},{7,23},{8,24},{9,... | collective-permute-start | bytes 245768 | tf_op jit(solution)/shard_map/ppermute | solution.py:429
  130.4 6.8 %collective-permute-start.17 = (bf16[32,1280]{1,0:T(8,128)(2,1)S(1)}, bf16[32,1280]{1,0:T(8,128)(2,1)S(1)}, u32[]{:S(2)}, u32[]{:S(2)}) collective-permute-start(bf16[32,1280]{1,0:T(8,128)(2,1)S(1)} %add_y.1.refs_2_.refs_0_), channel_id=1, source_target_pairs={{0,4},{1,5},{2,6},{3,7},{4,0},{5,1},{6,2},{7,3},{8,12},{9,13},{10,... | collective-permute-start | bytes 245768 | tf_op jit(solution)/shard_map/ppermute | solution.py:429
  133.7 3.5 %collective-permute-start.16 = (bf16[32,1280]{1,0:T(8,128)(2,1)S(1)}, bf16[32,1280]{1,0:T(8,128)(2,1)S(1)}, u32[]{:S(2)}, u32[]{:S(2)}) collective-permute-start(bf16[32,1280]{1,0:T(8,128)(2,1)S(1)} %add_y.1.refs_2_.refs_0_), channel_id=1, source_target_pairs={{0,6},{1,7},{2,0},{3,1},{4,2},{5,3},{6,4},{7,5},{8,14},{9,15},{10,... | collective-permute-start | bytes 245768 | tf_op jit(solution)/shard_map/ppermute | solution.py:429
  134.4 5.4 %collective-permute-start.15 = (bf16[32,1280]{1,0:T(8,128)(2,1)S(1)}, bf16[32,1280]{1,0:T(8,128)(2,1)S(1)}, u32[]{:S(2)}, u32[]{:S(2)}) collective-permute-start(bf16[32,1280]{1,0:T(8,128)(2,1)S(1)} %add_y.1.refs_2_.refs_0_), channel_id=1, source_target_pairs={{0,2},{1,3},{2,4},{3,5},{4,6},{5,7},{6,0},{7,1},{8,10},{9,11},{10,... | collective-permute-start | bytes 245768 | tf_op jit(solution)/shard_map/ppermute | solution.py:429
  140.3 6.2 %collective-permute-start.20 = (bf16[32,1280]{1,0:T(8,128)(2,1)S(1)}, bf16[32,1280]{1,0:T(8,128)(2,1)S(1)}, u32[]{:S(2)}, u32[]{:S(2)}) collective-permute-start(bf16[32,1280]{1,0:T(8,128)(2,1)S(1)} %add_z.1.refs_2_.refs_0_), channel_id=1, source_target_pairs={{0,16},{1,17},{2,18},{3,19},{4,20},{5,21},{6,22},{7,23},{8,24},{9,... | collective-permute-start | bytes 245768 | tf_op jit(solution)/shard_map/ppermute | solution.py:429
  141.4 5.2 %collective-permute-start.19 = (bf16[32,1280]{1,0:T(8,128)(2,1)S(1)}, bf16[32,1280]{1,0:T(8,128)(2,1)S(1)}, u32[]{:S(2)}, u32[]{:S(2)}) collective-permute-start(bf16[32,1280]{1,0:T(8,128)(2,1)S(1)} %add_z.1.refs_2_.refs_0_), channel_id=1, source_target_pairs={{0,24},{1,25},{2,26},{3,27},{4,28},{5,29},{6,30},{7,31},{8,0},{9,1... | collective-permute-start | bytes 245768 | tf_op jit(solution)/shard_map/ppermute | solution.py:429
  142.5 4.5 %collective-permute-start.18 = (bf16[32,1280]{1,0:T(8,128)(2,1)S(1)}, bf16[32,1280]{1,0:T(8,128)(2,1)S(1)}, u32[]{:S(2)}, u32[]{:S(2)}) collective-permute-start(bf16[32,1280]{1,0:T(8,128)(2,1)S(1)} %add_z.1.refs_2_.refs_0_), channel_id=1, source_target_pairs={{0,8},{1,9},{2,10},{3,11},{4,12},{5,13},{6,14},{7,15},{8,16},{9,17... | collective-permute-start | bytes 245768 | tf_op jit(solution)/shard_map/ppermute | solution.py:429
  147.6 6.5 %collective-permute-start.21 = (bf16[128,1280]{1,0:T(8,128)(2,1)S(1)}, bf16[128,1280]{1,0:T(8,128)(2,1)S(1)}, u32[]{:S(2)}, u32[]{:S(2)}) collective-permute-start(bf16[128,1280]{1,0:T(8,128)(2,1)S(1)} %join_y.1.refs_0_), channel_id=1, source_target_pairs={{0,1},{1,0},{2,3},{3,2},{4,5},{5,4},{6,7},{7,6},{8,9},{9,8},{10,11... | collective-permute-start | bytes 983048 | tf_op jit(solution)/shard_map/ppermute | solution.py:433
  (12 other events, 65.1 us)
